TPU v7x, 32 devices: a whole 2x2x4 slice. The times are simulated.
32 devices in a mesh: seq: 8 (over z, y), ch: 4 (over x, core).
Axes of the slice: x: 2, y: 2, z: 4, core: 2. Of those that a mesh axis runs over, the one named last changes fastest.
Arguments:
- query_proj: bfloat16 [1024, 2048], P('seq', 'ch'), may hold values from -6 to 6
- key_proj: bfloat16 [1024, 2048], P('seq', 'ch'), may hold values from -6 to 6
- value_proj: bfloat16 [1024, 2048], P('seq', 'ch'), may hold values from -6 to 6
- short_filter: float32 [3, 3, 2048], P(None, None, 'ch'), may hold values from -3.5 to 3.5
- long_filter: float32 [1024, 2048], P('seq', 'ch'), may hold values from -0.1875 to 0.1875
- skip_gain: float32 [2048], P('ch'), may hold values from 0.5 to 1.5
- out_weight: bfloat16 [2048, 4096], P('ch'), may hold values from -0.125 to 0.125
- cotangent: bfloat16 [1024, 4096], P('seq', 'ch'), may hold values from -6 to 6
Outputs:
- layer_out: bfloat16 [1024, 4096], P('seq', 'ch')
- grad_query: float32 [1024, 2048], P('seq', 'ch')
- grad_key: float32 [1024, 2048], P('seq', 'ch')
- grad_value: float32 [1024, 2048], P('seq', 'ch')
- grad_short: float32 [3, 3, 2048], P(None, None, 'ch')
- grad_filter: float32 [1024, 2048], P('seq', 'ch')
- grad_skip: float32 [2048], P('ch')
- grad_w_out_t: float32 [4096, 2048], P('seq', 'ch')
All inputs are finite; a program needn't handle non-finite values.
Results may differ from a plain program's by a relative error of at most 0.011.
Values may be sent and summed in bfloat16 or wider, within the bound.
No kernel may reach another device: no remote copies, remote signals or barrier semaphores. Data moves between devices by JAX's collectives and lax.ppermute only.
A program may use at most 128 MiB of HBM per device.

v0:
```python
import functools
import math

import jax
import jax.numpy as jnp
import ml_dtypes
import numpy as np
from jax import lax
from jax.experimental import pallas as pl
from jax.experimental.pallas import tpu as pltpu
from jax.sharding import PartitionSpec as P

exact_mode = lax.Precision.HIGHEST


def from_behind(shard, axis, by):
    size = lax.axis_size(axis)
    pairs = [(i, i + by) for i in range(size) if 0 <= i + by < size]
    return lax.ppermute(shard, axis, pairs)


def as_sent(shard):

    def short(part):
        return part.astype(jnp.bfloat16) if part.dtype == jnp.float32 else part

    return jax.tree.map(short, shard)


def tables(rows_out, cols_in, period):
    row_index = lax.broadcasted_iota(jnp.int32, (rows_out, cols_in), 0)
    col_index = lax.broadcasted_iota(jnp.int32, (rows_out, cols_in), 1)
    phase_angle = (row_index * col_index % period).astype(jnp.float32) * (2.0 * math.pi / period)
    return (jnp.cos(phase_angle), jnp.sin(phase_angle))


def along_rows(factor, values):
    return jnp.tensordot(factor, values, axes=1, precision=exact_mode)


def rows_spectrum(signal, basis_pair):
    return (along_rows(basis_pair[0], signal), -along_rows(basis_pair[1], signal))


def rows_inverse(complex_pair, basis_pair):
    total = along_rows(basis_pair[0], complex_pair[0]) - along_rows(basis_pair[1], complex_pair[1])
    return total / basis_pair[0].shape[1]


def block_forward(complex_pair, basis_pair):
    cosine_part, sine_part = basis_pair
    real_part = along_rows(cosine_part, complex_pair[0]) + along_rows(sine_part, complex_pair[1])
    imag_part = along_rows(cosine_part, complex_pair[1]) - along_rows(sine_part, complex_pair[0])
    return (real_part, imag_part)


def block_inverse(complex_pair, basis_pair):
    cosine_part, sine_part = basis_pair
    norming = 1.0 / cosine_part.shape[1]
    real_part = along_rows(cosine_part, complex_pair[0]) - along_rows(sine_part, complex_pair[1])
    imag_part = along_rows(cosine_part, complex_pair[1]) + along_rows(sine_part, complex_pair[0])
    return (real_part * norming, imag_part * norming)


def complex_product(first_pair, second_pair):
    return (
        first_pair[0] * second_pair[0] - first_pair[1] * second_pair[1],
        first_pair[0] * second_pair[1] + first_pair[1] * second_pair[0],
    )


def conj_product(first_pair, second_pair):
    return (
        first_pair[0] * second_pair[0] + first_pair[1] * second_pair[1],
        first_pair[0] * second_pair[1] - first_pair[1] * second_pair[0],
    )


def on_device(
    query_proj, key_proj, value_proj, short_filter, long_filter, skip_gain, out_weight, cotangent
):
    block_rows = query_proj.shape[0]
    tap_count = short_filter.shape[1]
    block_count = lax.axis_size("seq")
    streams = jnp.stack([query_proj, key_proj, value_proj])
    earlier = from_behind(streams[:, block_rows - (tap_count - 1) :], "seq", 1)
    extended = jnp.concatenate([earlier, streams], axis=1).astype(jnp.float32)
    shifted = [
        extended[:, tap_count - 1 - offset : tap_count - 1 - offset + block_rows]
        for offset in range(tap_count)
    ]
    filtered = sum(
        (short_filter[:, offset][:, None, :] * shifted[offset] for offset in range(tap_count))
    )
    query_short, key_short, value_short = (filtered[0], filtered[1], filtered[2])
    product = key_short * value_short
    forward_basis = tables(2 * block_rows, block_rows, 2 * block_rows)
    full_basis = tables(2 * block_rows, 2 * block_rows, 2 * block_rows)
    half_basis = tables(block_rows, 2 * block_rows, 2 * block_rows)
    block_basis = tables(2 * block_count, block_count, 2 * block_count)
    return_basis = tables(block_count, 2 * block_count, 2 * block_count)
    input_pair = rows_spectrum(product, forward_basis)
    filter_pair = rows_spectrum(long_filter, forward_basis)
    moved_data = (
        lax.all_to_all(input_pair[0][None], "seq", split_axis=1, concat_axis=0, tiled=True),
        lax.all_to_all(input_pair[1][None], "seq", split_axis=1, concat_axis=0, tiled=True),
        lax.all_to_all(filter_pair[0][None], "seq", split_axis=1, concat_axis=0, tiled=True),
        lax.all_to_all(filter_pair[1][None], "seq", split_axis=1, concat_axis=0, tiled=True),
    )
    input_spectrum = block_forward((moved_data[0], moved_data[1]), block_basis)
    filter_spectrum = block_forward((moved_data[2], moved_data[3]), block_basis)
    inverse_pair = block_inverse(complex_product(filter_spectrum, input_spectrum), return_basis)
    returned = (
        lax.all_to_all(inverse_pair[0], "seq", split_axis=0, concat_axis=1, tiled=True),
        lax.all_to_all(inverse_pair[1], "seq", split_axis=0, concat_axis=1, tiled=True),
    )
    folded = rows_inverse((returned[0][0], returned[1][0]), full_basis)
    carried = from_behind(folded[block_rows:], "seq", 1)
    convolved = folded[:block_rows] + carried
    mixed_seq = convolved + skip_gain * product
    gated_values = (query_short * mixed_seq).astype(jnp.bfloat16)
    partial_value = jnp.dot(gated_values, out_weight, preferred_element_type=jnp.float32)
    layer_out = lax.psum_scatter(partial_value, "ch", scatter_dimension=1, tiled=True).astype(
        jnp.bfloat16
    )
    full_cotangent = lax.all_gather(cotangent, "ch", axis=1, tiled=True)
    grad_gated = lax.dot_general(
        full_cotangent, out_weight, (((1,), (1,)), ((), ())), preferred_element_type=jnp.float32
    )
    grad_w_out_t = lax.psum_scatter(
        lax.dot_general(
            full_cotangent,
            gated_values,
            (((0,), (0,)), ((), ())),
            preferred_element_type=jnp.float32,
        ),
        "seq",
        scatter_dimension=0,
        tiled=True,
    )
    grad_mixed = grad_gated * query_short
    grad_query_short = grad_gated * mixed_seq
    following = from_behind(grad_mixed.astype(jnp.bfloat16), "seq", -1).astype(grad_mixed.dtype)
    spread = jnp.concatenate([grad_mixed, following], axis=0)
    grad_pair = rows_spectrum(spread, full_basis)
    moved_grad = (
        lax.all_to_all(
            grad_pair[0][None].astype(jnp.bfloat16), "seq", split_axis=1, concat_axis=0, tiled=True
        ).astype(jnp.float32),
        lax.all_to_all(
            grad_pair[1][None].astype(jnp.bfloat16), "seq", split_axis=1, concat_axis=0, tiled=True
        ).astype(jnp.float32),
    )
    grad_spectrum = block_forward(moved_grad, block_basis)
    input_back = block_inverse(conj_product(filter_spectrum, grad_spectrum), return_basis)
    filter_back = block_inverse(conj_product(input_spectrum, grad_spectrum), return_basis)
    returned_grad = (
        lax.all_to_all(as_sent(input_back[0]), "seq", split_axis=0, concat_axis=1, tiled=True),
        lax.all_to_all(as_sent(input_back[1]), "seq", split_axis=0, concat_axis=1, tiled=True),
        lax.all_to_all(as_sent(filter_back[0]), "seq", split_axis=0, concat_axis=1, tiled=True),
        lax.all_to_all(as_sent(filter_back[1]), "seq", split_axis=0, concat_axis=1, tiled=True),
    )
    conv_grad = rows_inverse((returned_grad[0][0], returned_grad[1][0]), half_basis)
    grad_filter = rows_inverse((returned_grad[2][0], returned_grad[3][0]), half_basis)
    grad_product = conv_grad + skip_gain * grad_mixed
    grad_streams = jnp.stack(
        [grad_query_short, grad_product * value_short, grad_product * key_short]
    )
    later_rows = from_behind(grad_streams[:, : tap_count - 1], "seq", -1)
    padded_grad = jnp.concatenate([grad_streams, later_rows], axis=1)
    grad_inputs = sum(
        (
            short_filter[:, offset][:, None, :] * padded_grad[:, offset : offset + block_rows]
            for offset in range(tap_count)
        )
    )
    short_terms = jnp.stack(
        [jnp.sum(grad_streams * shifted[offset], axis=1) for offset in range(tap_count)], axis=1
    )
    skip_terms = jnp.sum(grad_mixed * product, axis=0)
    grad_short, grad_skip = lax.psum((short_terms, skip_terms), "seq")
    return (
        layer_out,
        grad_inputs[0],
        grad_inputs[1],
        grad_inputs[2],
        grad_short,
        grad_filter,
        grad_skip,
        grad_w_out_t,
    )


LANES = 128
HALF = 64
F32 = jnp.float32
BF16 = jnp.bfloat16


def swap_bits(shard, axis, mask):
    size = lax.axis_size(axis)
    return lax.ppermute(shard, axis, [(i, i ^ mask) for i in range(size)])


@functools.lru_cache
def wave_tables(rows):
    steps = np.outer(2 * np.arange(rows) + 1, np.arange(rows)) % (4 * rows)
    angle = steps * (math.pi / (2 * rows))
    cosine, sine = np.cos(angle), np.sin(angle)
    inverse = np.concatenate([cosine.T, sine.T], axis=1) / rows
    forward = np.concatenate([cosine, sine], axis=0)
    return forward.astype(ml_dtypes.bfloat16), inverse.astype(ml_dtypes.bfloat16)


def left_lanes(rows):
    return lax.broadcasted_iota(jnp.int32, (rows, LANES), 1) < HALF


def other_half(block):
    return pltpu.roll(block, HALF, 1)


def earlier_rows(block, by):
    if by == 0:
        return block
    row = lax.broadcasted_iota(jnp.int32, block.shape, 0)
    return jnp.where(row >= by, pltpu.roll(block, by, 0), 0.0)


def later_rows(block, by):
    if by == 0:
        return block
    size = block.shape[0]
    row = lax.broadcasted_iota(jnp.int32, block.shape, 0)
    return jnp.where(row < size - by, pltpu.roll(block, size - by, 0), 0.0)


def big_dot(matrix_ref, operand, out_ref, step=256):
    for start in range(0, matrix_ref.shape[0], step):
        out_ref[start : start + step] = jnp.dot(
            matrix_ref[start : start + step], operand, preferred_element_type=F32
        )


def pack_streams_kernel(q_ref, k_ref, v_ref, h_ref, out_ref):
    rows = q_ref.shape[0]
    left = left_lanes(rows)
    for peer in range(out_ref.shape[0]):
        lanes = slice(LANES * (peer // 2), LANES * (peer // 2) + LANES)
        pairs = ((k_ref, q_ref), (v_ref, h_ref))
        for at, (first_ref, second_ref) in enumerate(pairs):
            first = first_ref[:, lanes].astype(F32)
            second = second_ref[:, lanes].astype(F32)
            if peer % 2 == 0:
                both = jnp.where(left, first, other_half(second))
            else:
                both = jnp.where(left, other_half(first), second)
            out_ref[peer, at] = both.astype(BF16)


def grad_gated_kernel(ids_ref, c0_ref, c1_ref, c2_ref, c3_ref, w_ref, out_ref):
    mine = ids_ref[1]
    width = c0_ref.shape[1]
    total = None
    for mask, part_ref in enumerate((c0_ref, c1_ref, c2_ref, c3_ref)):
        at = pl.multiple_of((mine ^ mask) * width, width)
        term = lax.dot_general(
            part_ref[...],
            w_ref[:, pl.ds(at, width)],
            (((1,), (1,)), ((), ())),
            preferred_element_type=F32,
        )
        total = term if total is None else total + term
    out_ref[...] = total.astype(BF16)


def forward_kernel(
    ids_ref, moved_ref, prm_ref, fwd_ref, inv_ref, gg_ref, c0_ref, c1_ref, c2_ref, c3_ref,
    send_ref, kqs_ref, vhs_ref, mq_ref, spec_ref, y_ref,
):
    peers, _, rows, _ = moved_ref.shape
    size = peers * rows
    left = left_lanes(size)
    kq = moved_ref[:, 0].reshape(size, LANES).astype(F32)
    vh = moved_ref[:, 1].reshape(size, LANES).astype(F32)
    kqs = sum(prm_ref[j : j + 1] * earlier_rows(kq, j) for j in range(3))
    vhs = sum(prm_ref[3 + j : 4 + j] * earlier_rows(vh, j) for j in range(3))
    kqs_ref[...] = kqs
    vhs_ref[...] = vhs
    product = kqs * vhs
    big_dot(fwd_ref, jnp.where(left, product, vhs).astype(BF16), spec_ref)
    xc, xs = spec_ref[:size], spec_ref[size:]
    hc, hs = other_half(xc), other_half(xs)
    y_parts = jnp.concatenate([xc * hc - xs * hs, xc * hs + xs * hc], axis=0).astype(BF16)
    big_dot(inv_ref, y_parts, y_ref)
    both_product = jnp.where(left, product, other_half(product))
    mixed = y_ref[...] + prm_ref[12:13] * both_product
    mq_ref[...] = jnp.where(left, mixed, kqs)
    gated = kqs * mixed
    left_rows = left_lanes(rows)
    for peer in range(peers):
        lanes = slice(LANES * (peer // 2), LANES * (peer // 2) + LANES)
        gg = gg_ref[:, lanes].astype(F32)
        if peer % 2 == 1:
            gg = other_half(gg)
        mine = gated[rows * peer : rows * peer + rows]
        send_ref[peer, :rows] = jnp.where(left_rows, gg, mine).astype(BF16)
    own = ids_ref[1]
    for mask, part_ref in enumerate((c0_ref, c1_ref, c2_ref, c3_ref)):
        for half in range(2):
            at = pl.multiple_of(half * 4 * LANES + own * LANES, LANES)
            send_ref[2 * (own ^ mask) + half, rows:] = part_ref[:, pl.ds(at, LANES)]


def project_kernel(ids_ref, moved_ref, w_ref, gated_ref, keep_ref, send_ref, cot_ref):
    peers = moved_ref.shape[0]
    rows = moved_ref.shape[1] // 2
    left = left_lanes(rows)
    for tile in range(peers // 2):
        first = moved_ref[2 * tile, :rows].astype(F32)
        second = moved_ref[2 * tile + 1, :rows].astype(F32)
        both = jnp.where(left, other_half(first), second)
        gated_ref[:, LANES * tile : LANES * tile + LANES] = both.astype(BF16)
    cot_ref[...] = moved_ref[:, rows:]
    gated = gated_ref[...]
    mine = ids_ref[1]
    width = keep_ref.shape[2]
    for mask in (1, 3, 0, 2):
        at = pl.multiple_of((mine ^ mask) * width, width)
        part = jnp.dot(gated, w_ref[:, pl.ds(at, width)], preferred_element_type=F32)
        if mask % 2 == 1:
            send_ref[mask // 2] = part.astype(BF16)
        else:
            keep_ref[mask // 2] = part


def backward_kernel(
    streams_ref, moved_ref, prm_ref, fwd_ref, inv_ref, kqs_ref, vhs_ref, mq_ref, spec_ref,
    send_ref, mspec_ref, back_ref,
):
    peers, _, rows, _ = streams_ref.shape
    size = peers * rows
    left = left_lanes(size)
    gg = moved_ref[:, :rows].reshape(size, LANES).astype(F32)
    gg = jnp.where(left, gg, other_half(gg))
    z = gg * mq_ref[...]
    grad_mixed = jnp.where(left, other_half(z), z)
    big_dot(fwd_ref, grad_mixed.astype(BF16), mspec_ref)
    xc, xs = spec_ref[:size], spec_ref[size:]
    mc, ms = mspec_ref[:size], mspec_ref[size:]
    parts = jnp.concatenate([xc * mc + xs * ms, xc * ms - xs * mc], axis=0).astype(BF16)
    big_dot(inv_ref, parts, back_ref)
    back = back_ref[...]
    kqs, vhs = kqs_ref[...], vhs_ref[...]
    grad_product = back + prm_ref[12:13] * grad_mixed
    grad_product = jnp.where(left, other_half(grad_product), grad_product)
    grad_kv = grad_product * jnp.where(left, vhs, other_half(kqs))
    grad_qf = jnp.where(left, z, back)
    grad_qf = jnp.where(left, z, other_half(back))
    kq = streams_ref[:, 0].reshape(size, LANES).astype(F32)
    vh = streams_ref[:, 1].reshape(size, LANES).astype(F32)
    raw_kv = jnp.where(left, kq, other_half(vh))
    raw_q = other_half(kq)
    out_kv = sum(prm_ref[6 + j : 7 + j] * later_rows(grad_kv, j) for j in range(3))
    out_qf = sum(prm_ref[9 + j : 10 + j] * later_rows(grad_qf, j) for j in range(3))
    sums = [jnp.sum(grad_kv * earlier_rows(raw_kv, j), axis=0, keepdims=True) for j in range(3)]
    sums += [jnp.sum(grad_qf * earlier_rows(raw_q, j), axis=0, keepdims=True) for j in range(3)]
    sums += [jnp.sum(grad_mixed * kqs * vhs, axis=0, keepdims=True)]
    sums += [jnp.zeros_like(sums[0])]
    small = jnp.concatenate(sums, axis=0)
    small_high = small.astype(BF16).astype(F32)
    small = jnp.concatenate([small_high, small - small_high], axis=0).astype(BF16)
    for peer in range(peers):
        at = slice(rows * peer, rows * peer + rows)
        send_ref[peer, :rows] = out_kv[at].astype(BF16)
        send_ref[peer, rows : 2 * rows] = out_qf[at].astype(BF16)
        send_ref[peer, 2 * rows :] = small


def unpack_kernel(moved_ref, q_ref, k_ref, v_ref, f_ref, short_ref, skip_ref):
    peers = moved_ref.shape[0]
    rows = q_ref.shape[0]
    left = left_lanes(rows)
    left_few = left_lanes(8)

    def merged(first, second, mask):
        return (
            jnp.where(mask, first, other_half(second)),
            jnp.where(mask, other_half(first), second),
        )

    for tile in range(peers // 2):
        lanes = slice(LANES * tile, LANES * tile + LANES)
        first, second = moved_ref[2 * tile].astype(F32), moved_ref[2 * tile + 1].astype(F32)
        k_ref[:, lanes], v_ref[:, lanes] = merged(first[:rows], second[:rows], left)
        q_ref[:, lanes], f_ref[:, lanes] = merged(
            first[rows : 2 * rows], second[rows : 2 * rows], left
        )
        few = [part[2 * rows : 2 * rows + 8] + part[2 * rows + 8 :] for part in (first, second)]
        low, high = merged(few[0], few[1], left_few)
        short_ref[0, :, lanes] = low[3:6]
        short_ref[1, :, lanes] = low[0:3]
        short_ref[2, :, lanes] = high[0:3]
        skip_ref[:, lanes] = low[6:7]


def grad_weight_kernel(ids_ref, *refs):
    out_ref = refs[-1]
    cots, gates = refs[:4], refs[4:-1]
    own_row, own = ids_ref[0], ids_ref[1]
    for mask, cot_ref in enumerate(cots):
        total = None
        for at, gate_ref in enumerate(gates):
            term = lax.dot_general(
                cot_ref[own_row ^ at],
                gate_ref[...],
                (((0,), (0,)), ((), ())),
                preferred_element_type=F32,
            )
            total = term if total is None else total + term
        out_ref[pl.ds(pl.multiple_of((own ^ mask) * LANES, LANES), LANES)] = total


def call(kernel, outs, scalars, *arrays, scratch=(), limit=32, flops=0):
    vmem = pl.BlockSpec(memory_space=pltpu.VMEM)
    smem = pl.BlockSpec(memory_space=pltpu.SMEM)
    many = isinstance(outs, list)
    moved = sum(math.prod(a.shape) * a.dtype.itemsize for a in arrays)
    return pl.pallas_call(
        kernel,
        out_shape=outs,
        in_specs=[smem] * len(scalars) + [vmem] * len(arrays),
        out_specs=[vmem] * len(outs) if many else vmem,
        scratch_shapes=list(scratch),
        compiler_params=pltpu.CompilerParams(vmem_limit_bytes=limit * 2**20),
        cost_estimate=pl.CostEstimate(flops=flops, bytes_accessed=moved, transcendentals=0),
    )(*scalars, *arrays)


def shaped(shape, dtype):
    return jax.ShapeDtypeStruct(shape, dtype)


def gathered_pairs(block, axis):
    near = swap_bits(block, axis, 1)
    far = swap_bits(block, axis, 2)
    return [block, near, far, swap_bits(far, axis, 1)]


def gathered_all(block, axis):
    blocks = {0: block}
    mask = lax.axis_size(axis) // 2
    while mask:
        blocks |= {at | mask: swap_bits(held, axis, mask) for at, held in blocks.items()}
        mask //= 2
    return [blocks[at] for at in range(len(blocks))]


def on_device_packed(
    query_proj, key_proj, value_proj, short_filter, long_filter, skip_gain, out_weight, cotangent
):
    peers = lax.axis_size("seq")
    rows, channels = query_proj.shape
    features = cotangent.shape[1]
    size = peers * rows
    seq_at, ch_at = lax.axis_index("seq"), lax.axis_index("ch")
    ids = jnp.stack([seq_at, ch_at]).astype(jnp.int32)
    forward_table, inverse_table = (jnp.asarray(table) for table in wave_tables(size))
    cots = gathered_pairs(cotangent, "ch")

    own_short = lax.dynamic_slice_in_dim(short_filter, seq_at * HALF, HALF, 2)
    own_skip = lax.dynamic_slice_in_dim(skip_gain, seq_at * HALF, HALF, 0)[None]
    unit = (lax.broadcasted_iota(jnp.int32, (3, HALF), 0) == 0).astype(F32)
    wq, wk, wv = own_short[0], own_short[1], own_short[2]
    prm = jnp.concatenate(
        [
            jnp.concatenate([wk, wv, wk, wq, own_skip], axis=0),
            jnp.concatenate([wq, unit, wv, unit, own_skip], axis=0),
        ],
        axis=1,
    )

    packed = call(
        pack_streams_kernel,
        shaped((peers, 2, rows, LANES), BF16),
        [],
        query_proj,
        key_proj,
        value_proj,
        long_filter,
    )
    streams = lax.all_to_all(packed, "seq", 0, 0, tiled=True)
    grad_gated = call(
        grad_gated_kernel,
        shaped((rows, channels), BF16),
        [ids],
        *cots,
        out_weight,
        flops=2 * rows * channels * 4 * features,
    )
    wide = shaped((size, LANES), F32)
    send, kqs, vhs, mq, spec = call(
        forward_kernel,
        [shaped((peers, 2 * rows, LANES), BF16), wide, wide, wide, shaped((2 * size, LANES), F32)],
        [ids],
        streams,
        prm,
        forward_table,
        inverse_table,
        grad_gated,
        *cots,
        scratch=[pltpu.VMEM((size, LANES), F32)],
        flops=8 * size * size * LANES,
    )
    moved = lax.all_to_all(send, "seq", 0, 0, tiled=True)
    gated, keep, away, cot_rows = call(
        project_kernel,
        [
            shaped((rows, channels), BF16),
            shaped((2, rows, features), F32),
            shaped((2, rows, features), BF16),
            shaped((peers, rows, LANES), BF16),
        ],
        [ids],
        moved,
        out_weight,
        flops=2 * rows * channels * 4 * features,
    )
    near = swap_bits(away, "ch", 1)
    passed = (keep[1] + near[1].astype(F32)).astype(BF16)
    layer_out = (keep[0] + near[0].astype(F32) + swap_bits(passed, "ch", 2).astype(F32)).astype(
        BF16
    )
    cot_parts = gathered_pairs(cot_rows, "ch")
    gates = gathered_all(gated, "seq")
    back = call(
        backward_kernel,
        shaped((peers, 2 * rows + 16, LANES), BF16),
        [],
        streams,
        moved,
        prm,
        forward_table,
        inverse_table,
        kqs,
        vhs,
        mq,
        spec,
        scratch=[pltpu.VMEM((2 * size, LANES), F32), pltpu.VMEM((size, LANES), F32)],
        flops=8 * size * size * LANES,
    )
    returned = lax.all_to_all(back, "seq", 0, 0, tiled=True)
    plain = shaped((rows, channels), F32)
    grad_query, grad_key, grad_value, grad_filter, grad_short, grad_skip = call(
        unpack_kernel,
        [plain, plain, plain, plain, shaped((3, 3, channels), F32), shaped((1, channels), F32)],
        [],
        returned,
    )
    grad_w_out_t = call(
        grad_weight_kernel,
        shaped((4 * LANES, channels), F32),
        [ids],
        *cot_parts,
        *gates,
        flops=2 * size * channels * 4 * LANES,
    )
    return (
        layer_out,
        grad_query,
        grad_key,
        grad_value,
        grad_short,
        grad_filter,
        grad_skip[0],
        grad_w_out_t,
    )


def solution(mesh):
    in_specs = (
        P("seq", "ch"),
        P("seq", "ch"),
        P("seq", "ch"),
        P(None, None, "ch"),
        P("seq", "ch"),
        P("ch"),
        P("ch", None),
        P("seq", "ch"),
    )
    out_specs = (
        P("seq", "ch"),
        P("seq", "ch"),
        P("seq", "ch"),
        P("seq", "ch"),
        P(None, None, "ch"),
        P("seq", "ch"),
        P("ch"),
        P("seq", "ch"),
    )
    split = dict(mesh.shape)

    def whole(*arrays):
        rows = arrays[0].shape[0] // split["seq"]
        channels = arrays[0].shape[1] // split["ch"]
        features = arrays[7].shape[1]
        packs = (
            split["ch"] == 4
            and channels == HALF * split["seq"]
            and features == 4 * LANES * split["seq"]
            and arrays[0].shape[0] <= 1024
            and rows % 16 == 0
            and arrays[3].shape[1] == 3
        )
        body = on_device_packed if packs else on_device
        return jax.shard_map(
            body,
            mesh=mesh,
            in_specs=in_specs,
            out_specs=out_specs,
            check_vma=False,
        )(*arrays)

    return whole
```

profile of v0, /device:TPU:0, one launch (start us, length us, event | category | flops | bytes accessed | tf_op | source)
XLA Modules:
  0.0 105.1 jit_solution(10809724123863523376)
XLA Ops:
  0.6 0.0 copy-start
  0.7 1.0 copy-done.9
  1.7 0.9 copy-done.10
  2.6 0.9 copy-done.11
  3.5 0.9 copy-done.12
  4.4 1.0 shard_map.161
  5.4 7.3 %all-to-all-start = ((bf16[8,2,128,128]{3,2,1,0:T(8,128)(2,1)}), bf16[8,2,128,128]{3,2,1,0:T(8,128)(2,1)S(1)}, u32[]{:S(2)}, u32[]{:S(2)}) async-start(bf16[8,2,128,128]{3,2,1,0:T(8,128)(2,1)} %shard_map.161), calls=%async_computation | async-start | bytes 1048576 | tf_op jit(solution)/shard_map/all_to_all | solution.py:492
  12.7 1.5 %collective-permute-start.1 = (bf16[128,1024]{1,0:T(8,128)(2,1)}, bf16[128,1024]{1,0:T(8,128)(2,1)S(1)}, u32[]{:S(2)}, u32[]{:S(2)}) collective-permute-start(bf16[128,1024]{1,0:T(8,128)(2,1)} %c0_ref.3), channel_id=1, source_target_pairs={{0,2},{1,3},{2,0},{3,1},{4,6},{5,7},{6,4},{7,5},{8,10},{9,11},{10,... | collective-permute-start | bytes 786440 | tf_op jit(solution)/shard_map/ppermute | solution.py:202
  14.2 0.8 dynamic-slice_bitcast_fusion.2
  14.9 5.7 %collective-permute-done.1.c2_ref = bf16[128,1024]{1,0:T(8,128)(2,1)S(1)} collective-permute-done((bf16[128,1024]{1,0:T(8,128)(2,1)}, bf16[128,1024]{1,0:T(8,128)(2,1)S(1)}, u32[]{:S(2)}, u32[]{:S(2)}) %collective-permute-start.1) | collective-permute-done | bytes 262176 | tf_op jit(solution)/shard_map/ppermute | solution.py:202
  20.6 0.1 dynamic-slice_bitcast_fusion.3
  20.7 0.1 concatenate.9
  20.8 0.1 iota.11
  20.9 0.1 concatenate.10
  21.0 0.1 pad_add_fusion.ids_ref
  21.1 0.1 pad_maximum_fusion.prm_ref
  21.1 1.0 collective-permute-done.2.c3_ref
  22.2 2.2 %copy-done.1 = bf16[512,4096]{1,0:T(8,128)(2,1)S(1)} copy-done((bf16[512,4096]{1,0:T(8,128)(2,1)S(1)}, bf16[512,4096]{1,0:T(8,128)(2,1)}, u32[]{:S(2)}) %copy-start.1) | copy-done | bytes 4194328
  24.4 0.9 copy-done.7
  25.3 2.1 %shard_map.162.gg_ref = bf16[128,512]{1,0:T(8,128)(2,1)S(1)} custom-call(s32[2]{0:T(128)S(1)} %pad_add_fusion.ids_ref, bf16[128,1024]{1,0:T(8,128)(2,1)S(1)} %copy-done.7, bf16[128,1024]{1,0:T(8,128)(2,1)S(1)} %collective-permute-done.c1_ref, bf16[128,1024]{1,0:T(8,128)(2,1)S(1)} %collective-permute-done.1.c2_ref, ...), custom_call_target="tpu_custom_call" | custom-call | flops 536870912 | bytes 5242880 | tf_op jit(solution)/shard_map/pallas_call | solution.py:429
  27.4 0.0 copy-start.3
  27.4 2.2 %copy-done.3 = bf16[1024,2048]{1,0:T(8,128)(2,1)S(1)} copy-done((bf16[1024,2048]{1,0:T(8,128)(2,1)S(1)}, bf16[1024,2048]{1,0:T(8,128)(2,1)}, u32[]{:S(2)}) %copy-start.3) | copy-done | bytes 4194328
  29.6 2.2 %copy-done.5 = bf16[2048,1024]{1,0:T(8,128)(2,1)S(1)} copy-done((bf16[2048,1024]{1,0:T(8,128)(2,1)S(1)}, bf16[2048,1024]{1,0:T(8,128)(2,1)}, u32[]{:S(2)}) %copy-start.5) | copy-done | bytes 4194328
  31.8 3.7 %shard_map.163 = (bf16[8,256,128]{2,1,0:T(8,128)(2,1)S(1)}, f32[1024,128]{1,0:T(8,128)S(1)}, f32[1024,128]{1,0:T(8,128)S(1)}, f32[1024,128]{1,0:T(8,128)S(1)}, f32[2048,128]{1,0:T(8,128)S(1)}) custom-call(s32[2]{0:T(128)S(1)} %pad_add_fusion.ids_ref, bf16[8,2,128,128]{3,2,1,0:T(8,128)(2,1)S(1)} %all-to-all-done.moved_ref.streams_ref, ...), custom_call_target="tpu_custom_call" | custom-call | flops 1073741824 | bytes 10099200 | tf_op jit(solution)/shard_map/pallas_call | solution.py:429
  35.5 0.0 copy-start.4
  35.5 20.6 %all_to_all.15.moved_ref = bf16[8,256,128]{2,1,0:T(8,128)(2,1)S(1)} all-to-all(bf16[8,256,128]{2,1,0:T(8,128)(2,1)S(1)} %get-tuple-element.23), channel_id=1, replica_groups=mesh['seq'=8,'ch'=4] {'seq'}, dimensions={0} | all-to-all | bytes 1048576 | tf_op jit(solution)/shard_map/all_to_all | solution.py:515
  56.1 1.3 %shard_map.164 = (bf16[128,512]{1,0:T(8,128)(2,1)S(1)}, f32[2,128,1024]{2,1,0:T(8,128)S(1)}, bf16[2,128,1024]{2,1,0:T(8,128)(2,1)S(1)}, bf16[8,128,128]{2,1,0:T(8,128)(2,1)S(1)}) custom-call(s32[2]{0:T(128)S(1)} %pad_add_fusion.ids_ref, bf16[8,256,128]{2,1,0:T(8,128)(2,1)S(1)} %all_to_all.15.moved_ref, bf16[512,4096]{1,0:T(8,128)(2,1)S(1)} %copy-done.2), custom_call_target="tpu_custom_call" | custom-call | flops 536870912 | bytes 4718592 | tf_op jit(solution)/shard_map/pallas_call | solution.py:429
  57.4 0.1 collective-permute-start.3
  57.5 1.5 %collective-permute-start.6 = (bf16[8,128,128]{2,1,0:T(8,128)(2,1)S(1)}, bf16[8,128,128]{2,1,0:T(8,128)(2,1)S(1)}, u32[]{:S(2)}, u32[]{:S(2)}) collective-permute-start(bf16[8,128,128]{2,1,0:T(8,128)(2,1)S(1)} %get-tuple-element.36.refs_0_), channel_id=1, source_target_pairs={{0,2},{1,3},{2,0},{3,1},{4,6},{5,7},{6,4},{7,5},{8,10},{9,11},{10,... | collective-permute-start | bytes 786440 | tf_op jit(solution)/shard_map/ppermute | solution.py:202
  59.0 4.4 %shard_map.165 = bf16[8,272,128]{2,1,0:T(8,128)(2,1)} custom-call(bf16[8,2,128,128]{3,2,1,0:T(8,128)(2,1)S(1)} %all-to-all-done.moved_ref.streams_ref, bf16[8,256,128]{2,1,0:T(8,128)(2,1)S(1)} %all_to_all.15.moved_ref, f32[13,128]{1,0:T(8,128)S(1)} %pad_maximum_fusion.prm_ref, bf16[2048,1024]{1,0:T(8,128)(2,1)S(1)} %copy-done.6, ...), custom_call_target="tpu_custom_call" | custom-call | flops 1073741824 | bytes 12065280 | tf_op jit(solution)/shard_map/pallas_call | solution.py:429
  63.4 3.6 %all-to-all-start.2 = ((bf16[8,272,128]{2,1,0:T(8,128)(2,1)}), bf16[8,272,128]{2,1,0:T(8,128)(2,1)S(1)}, u32[]{:S(2)}, u32[]{:S(2)}) async-start(bf16[8,272,128]{2,1,0:T(8,128)(2,1)} %shard_map.165), calls=%async_computation.2 | async-start | bytes 1114112 | tf_op jit(solution)/shard_map/all_to_all | solution.py:552
  67.0 2.9 %collective-permute-start.11 = (bf16[128,512]{1,0:T(8,128)(2,1)S(1)}, bf16[128,512]{1,0:T(8,128)(2,1)S(1)}, u32[]{:S(2)}, u32[]{:S(2)}) collective-permute-start(bf16[128,512]{1,0:T(8,128)(2,1)S(1)} %get-tuple-element.37.refs_4_), channel_id=1, source_target_pairs={{0,16},{4,20},{8,24},{12,28},{16,0},{20,4},{24,8},{28,12},{1,17},{... | collective-permute-start | bytes 393224 | tf_op jit(solution)/shard_map/ppermute | solution.py:202
  69.9 1.5 %collective-permute-start.9 = (bf16[128,512]{1,0:T(8,128)(2,1)S(1)}, bf16[128,512]{1,0:T(8,128)(2,1)S(1)}, u32[]{:S(2)}, u32[]{:S(2)}) collective-permute-start(bf16[128,512]{1,0:T(8,128)(2,1)S(1)} %get-tuple-element.37.refs_4_), channel_id=1, source_target_pairs={{0,8},{4,12},{8,0},{12,4},{16,24},{20,28},{24,16},{28,20},{1,9},{5... | collective-permute-start | bytes 393224 | tf_op jit(solution)/shard_map/ppermute | solution.py:202
  71.4 1.5 %collective-permute-start.8 = (bf16[128,512]{1,0:T(8,128)(2,1)S(1)}, bf16[128,512]{1,0:T(8,128)(2,1)S(1)}, u32[]{:S(2)}, u32[]{:S(2)}) collective-permute-start(bf16[128,512]{1,0:T(8,128)(2,1)S(1)} %get-tuple-element.37.refs_4_), channel_id=1, source_target_pairs={{0,4},{4,0},{8,12},{12,8},{16,20},{20,16},{24,28},{28,24},{1,5},{5... | collective-permute-start | bytes 393224 | tf_op jit(solution)/shard_map/ppermute | solution.py:202
  72.9 15.4 %collective-permute-done.11.refs_8_ = bf16[128,512]{1,0:T(8,128)(2,1)S(1)} collective-permute-done((bf16[128,512]{1,0:T(8,128)(2,1)S(1)}, bf16[128,512]{1,0:T(8,128)(2,1)S(1)}, u32[]{:S(2)}, u32[]{:S(2)}) %collective-permute-start.11) | collective-permute-done | bytes 131104 | tf_op jit(solution)/shard_map/ppermute | solution.py:202
  88.3 0.6 collective-permute-start.7
  88.9 0.1 fusion.1
  88.9 0.6 collective-permute-start.4
  89.5 1.5 %collective-permute-start.12 = (bf16[128,512]{1,0:T(8,128)(2,1)S(1)}, bf16[128,512]{1,0:T(8,128)(2,1)S(1)}, u32[]{:S(2)}, u32[]{:S(2)}) collective-permute-start(bf16[128,512]{1,0:T(8,128)(2,1)S(1)} %collective-permute-done.11.refs_8_), channel_id=1, source_target_pairs={{0,4},{4,0},{8,12},{12,8},{16,20},{20,16},{24,28},{28,24},{1,5},{5... | collective-permute-start | bytes 393224 | tf_op jit(solution)/shard_map/ppermute | solution.py:202
  91.1 0.5 collective-permute-start.10
  91.6 2.6 %collective-permute-done.13.refs_10_ = bf16[128,512]{1,0:T(8,128)(2,1)S(1)} collective-permute-done((bf16[128,512]{1,0:T(8,128)(2,1)S(1)}, bf16[128,512]{1,0:T(8,128)(2,1)S(1)}, u32[]{:S(2)}, u32[]{:S(2)}) %collective-permute-start.13) | collective-permute-done | bytes 131104 | tf_op jit(solution)/shard_map/ppermute | solution.py:202
  94.2 1.5 %collective-permute-start.14 = (bf16[128,512]{1,0:T(8,128)(2,1)S(1)}, bf16[128,512]{1,0:T(8,128)(2,1)S(1)}, u32[]{:S(2)}, u32[]{:S(2)}) collective-permute-start(bf16[128,512]{1,0:T(8,128)(2,1)S(1)} %collective-permute-done.13.refs_10_), channel_id=1, source_target_pairs={{0,4},{4,0},{8,12},{12,8},{16,20},{20,16},{24,28},{28,24},{1,5},{5... | collective-permute-start | bytes 393224 | tf_op jit(solution)/shard_map/ppermute | solution.py:202
  95.7 0.3 collective-permute-done.12.refs_9_
  96.0 2.5 %collective-permute-done.10.refs_7_ = bf16[128,512]{1,0:T(8,128)(2,1)S(1)} collective-permute-done((bf16[128,512]{1,0:T(8,128)(2,1)S(1)}, bf16[128,512]{1,0:T(8,128)(2,1)S(1)}, u32[]{:S(2)}, u32[]{:S(2)}) %collective-permute-start.10) | collective-permute-done | bytes 131104 | tf_op jit(solution)/shard_map/ppermute | solution.py:202
  98.4 1.9 %collective-permute-done.14.refs_11_ = bf16[128,512]{1,0:T(8,128)(2,1)S(1)} collective-permute-done((bf16[128,512]{1,0:T(8,128)(2,1)S(1)}, bf16[128,512]{1,0:T(8,128)(2,1)S(1)}, u32[]{:S(2)}, u32[]{:S(2)}) %collective-permute-start.14) | collective-permute-done | bytes 131104 | tf_op jit(solution)/shard_map/ppermute | solution.py:202
  100.3 2.8 %shard_map.167 = f32[512,512]{1,0:T(8,128)} custom-call(s32[2]{0:T(128)S(1)} %pad_add_fusion.ids_ref, bf16[8,128,128]{2,1,0:T(8,128)(2,1)S(1)} %get-tuple-element.36.refs_0_, bf16[8,128,128]{2,1,0:T(8,128)(2,1)S(1)} %collective-permute-done.5.refs_1_, bf16[8,128,128]{2,1,0:T(8,128)(2,1)S(1)} %collective-permute-done.6.refs_2_, ...), custom_call_target="tpu_custom_call" | custom-call | flops 536870912 | bytes 2097152 | tf_op jit(solution)/shard_map/pallas_call | solution.py:429
  103.1 0.8 fusion
  103.9 1.2 %shard_map.166 = (f32[128,512]{1,0:T(8,128)}, f32[128,512]{1,0:T(8,128)}, f32[128,512]{1,0:T(8,128)}, f32[128,512]{1,0:T(8,128)}, f32[3,3,512]{2,1,0:T(4,128)}, /*index=5*/f32[1,512]{1,0:T(1,128)}) custom-call(bf16[8,272,128]{2,1,0:T(8,128)(2,1)S(1)} %all-to-all-done.2.moved_ref), custom_call_target="tpu_custom_call" | custom-call | bytes 557056 | tf_op jit(solution)/shard_map/pallas_call | solution.py:429
  (30 shorter events, 0.1 us)
Async XLA Ops:
  0.6 20.0 %copy-start = (f32[512]{0:T(512)S(1)}, f32[512]{0:T(512)}, u32[]{:S(2)}) copy-start(f32[512]{0:T(512)} %param.15) | copy-start | bytes 6148
  0.6 26.7 %copy-start.8 = (bf16[128,1024]{1,0:T(8,128)(2,1)S(1)}, bf16[128,1024]{1,0:T(8,128)(2,1)}, u32[]{:S(2)}) copy-start(bf16[128,1024]{1,0:T(8,128)(2,1)} %c0_ref.3) | copy-start | bytes 786436
  0.7 1.0 copy-start.9
  1.7 0.9 copy-start.10
  2.6 0.9 copy-start.11
  3.5 0.9 copy-start.12
  5.4 22.0 %all-to-all-start = ((bf16[8,2,128,128]{3,2,1,0:T(8,128)(2,1)}), bf16[8,2,128,128]{3,2,1,0:T(8,128)(2,1)S(1)}, u32[]{:S(2)}, u32[]{:S(2)}) async-start(bf16[8,2,128,128]{3,2,1,0:T(8,128)(2,1)} %shard_map.161), calls=%async_computation | async-start | bytes 1048576 | tf_op jit(solution)/shard_map/all_to_all | solution.py:492
  12.7 8.0 %collective-permute-start.1 = (bf16[128,1024]{1,0:T(8,128)(2,1)}, bf16[128,1024]{1,0:T(8,128)(2,1)S(1)}, u32[]{:S(2)}, u32[]{:S(2)}) collective-permute-start(bf16[128,1024]{1,0:T(8,128)(2,1)} %c0_ref.3), channel_id=1, source_target_pairs={{0,2},{1,3},{2,0},{3,1},{4,6},{5,7},{6,4},{7,5},{8,10},{9,11},{10,... | collective-permute-start | bytes 786440 | tf_op jit(solution)/shard_map/ppermute | solution.py:202
  14.2 7.0 %collective-permute-start = (bf16[128,1024]{1,0:T(8,128)(2,1)}, bf16[128,1024]{1,0:T(8,128)(2,1)S(1)}, u32[]{:S(2)}, u32[]{:S(2)}) collective-permute-start(bf16[128,1024]{1,0:T(8,128)(2,1)} %c0_ref.3), channel_id=1, source_target_pairs={{0,1},{1,0},{2,3},{3,2},{4,5},{5,4},{6,7},{7,6},{8,9},{9,8},{10,11... | collective-permute-start | bytes 786440 | tf_op jit(solution)/shard_map/ppermute | solution.py:202
  20.6 1.5 %collective-permute-start.2 = (bf16[128,1024]{1,0:T(8,128)(2,1)S(1)}, bf16[128,1024]{1,0:T(8,128)(2,1)S(1)}, u32[]{:S(2)}, u32[]{:S(2)}) collective-permute-start(bf16[128,1024]{1,0:T(8,128)(2,1)S(1)} %collective-permute-done.1.c2_ref), channel_id=1, source_target_pairs={{0,1},{1,0},{2,3},{3,2},{4,5},{5,4},{6,7},{7,6},{8,9},{9,8},{10,11... | collective-permute-start | bytes 786440 | tf_op jit(solution)/shard_map/ppermute | solution.py:202
  22.2 2.2 %copy-start.1 = (bf16[512,4096]{1,0:T(8,128)(2,1)S(1)}, bf16[512,4096]{1,0:T(8,128)(2,1)}, u32[]{:S(2)}) copy-start(bf16[512,4096]{1,0:T(8,128)(2,1)} %w_ref.3) | copy-start | bytes 12582916
  24.4 0.9 copy-start.7
  27.4 2.2 %copy-start.3 = (bf16[1024,2048]{1,0:T(8,128)(2,1)S(1)}, bf16[1024,2048]{1,0:T(8,128)(2,1)}, u32[]{:S(2)}) copy-start(bf16[1024,2048]{1,0:T(8,128)(2,1)} %constant.21.clone.inv_ref) | copy-start | bytes 12582916
  29.6 2.2 %copy-start.5 = (bf16[2048,1024]{1,0:T(8,128)(2,1)S(1)}, bf16[2048,1024]{1,0:T(8,128)(2,1)}, u32[]{:S(2)}) copy-start(bf16[2048,1024]{1,0:T(8,128)(2,1)} %constant.20.clone.fwd_ref) | copy-start | bytes 12582916
  31.8 24.3 %copy-start.2 = (bf16[512,4096]{1,0:T(8,128)(2,1)S(1)}, bf16[512,4096]{1,0:T(8,128)(2,1)}, u32[]{:S(2)}) copy-start(bf16[512,4096]{1,0:T(8,128)(2,1)} %w_ref.3) | copy-start | bytes 12582916
  31.8 27.2 %copy-start.6 = (bf16[2048,1024]{1,0:T(8,128)(2,1)S(1)}, bf16[2048,1024]{1,0:T(8,128)(2,1)}, u32[]{:S(2)}) copy-start(bf16[2048,1024]{1,0:T(8,128)(2,1)} %constant.20.clone.fwd_ref) | copy-start | bytes 12582916
  35.5 23.5 %copy-start.4 = (bf16[1024,2048]{1,0:T(8,128)(2,1)S(1)}, bf16[1024,2048]{1,0:T(8,128)(2,1)}, u32[]{:S(2)}) copy-start(bf16[1024,2048]{1,0:T(8,128)(2,1)} %constant.21.clone.inv_ref) | copy-start | bytes 12582916
  57.4 30.9 %collective-permute-start.3 = (bf16[2,128,1024]{2,1,0:T(8,128)(2,1)S(1)}, bf16[2,128,1024]{2,1,0:T(8,128)(2,1)S(1)}, u32[]{:S(2)}, u32[]{:S(2)}) collective-permute-start(bf16[2,128,1024]{2,1,0:T(8,128)(2,1)S(1)} %get-tuple-element.25), channel_id=1, source_target_pairs={{0,1},{1,0},{2,3},{3,2},{4,5},{5,4},{6,7},{7,6},{8,9},{9,8},{10,11... | collective-permute-start | bytes 1572872 | tf_op jit(solution)/shard_map/ppermute | solution.py:202
  57.5 30.8 %collective-permute-start.6 = (bf16[8,128,128]{2,1,0:T(8,128)(2,1)S(1)}, bf16[8,128,128]{2,1,0:T(8,128)(2,1)S(1)}, u32[]{:S(2)}, u32[]{:S(2)}) collective-permute-start(bf16[8,128,128]{2,1,0:T(8,128)(2,1)S(1)} %get-tuple-element.36.refs_0_), channel_id=1, source_target_pairs={{0,2},{1,3},{2,0},{3,1},{4,6},{5,7},{6,4},{7,5},{8,10},{9,11},{10,... | collective-permute-start | bytes 786440 | tf_op jit(solution)/shard_map/ppermute | solution.py:202
  63.4 40.5 %all-to-all-start.2 = ((bf16[8,272,128]{2,1,0:T(8,128)(2,1)}), bf16[8,272,128]{2,1,0:T(8,128)(2,1)S(1)}, u32[]{:S(2)}, u32[]{:S(2)}) async-start(bf16[8,272,128]{2,1,0:T(8,128)(2,1)} %shard_map.165), calls=%async_computation.2 | async-start | bytes 1114112 | tf_op jit(solution)/shard_map/all_to_all | solution.py:552
  67.0 21.2 %collective-permute-start.11 = (bf16[128,512]{1,0:T(8,128)(2,1)S(1)}, bf16[128,512]{1,0:T(8,128)(2,1)S(1)}, u32[]{:S(2)}, u32[]{:S(2)}) collective-permute-start(bf16[128,512]{1,0:T(8,128)(2,1)S(1)} %get-tuple-element.37.refs_4_), channel_id=1, source_target_pairs={{0,16},{4,20},{8,24},{12,28},{16,0},{20,4},{24,8},{28,12},{1,17},{... | collective-permute-start | bytes 393224 | tf_op jit(solution)/shard_map/ppermute | solution.py:202
  69.9 19.0 %collective-permute-start.9 = (bf16[128,512]{1,0:T(8,128)(2,1)S(1)}, bf16[128,512]{1,0:T(8,128)(2,1)S(1)}, u32[]{:S(2)}, u32[]{:S(2)}) collective-permute-start(bf16[128,512]{1,0:T(8,128)(2,1)S(1)} %get-tuple-element.37.refs_4_), channel_id=1, source_target_pairs={{0,8},{4,12},{8,0},{12,4},{16,24},{20,28},{24,16},{28,20},{1,9},{5... | collective-permute-start | bytes 393224 | tf_op jit(solution)/shard_map/ppermute | solution.py:202
  71.4 18.1 %collective-permute-start.8 = (bf16[128,512]{1,0:T(8,128)(2,1)S(1)}, bf16[128,512]{1,0:T(8,128)(2,1)S(1)}, u32[]{:S(2)}, u32[]{:S(2)}) collective-permute-start(bf16[128,512]{1,0:T(8,128)(2,1)S(1)} %get-tuple-element.37.refs_4_), channel_id=1, source_target_pairs={{0,4},{4,0},{8,12},{12,8},{16,20},{20,16},{24,28},{28,24},{1,5},{5... | collective-permute-start | bytes 393224 | tf_op jit(solution)/shard_map/ppermute | solution.py:202
  88.3 2.8 %collective-permute-start.5 = (bf16[8,128,128]{2,1,0:T(8,128)(2,1)S(1)}, bf16[8,128,128]{2,1,0:T(8,128)(2,1)S(1)}, u32[]{:S(2)}, u32[]{:S(2)}) collective-permute-start(bf16[8,128,128]{2,1,0:T(8,128)(2,1)S(1)} %get-tuple-element.36.refs_0_), channel_id=1, source_target_pairs={{0,1},{1,0},{2,3},{3,2},{4,5},{5,4},{6,7},{7,6},{8,9},{9,8},{10,11... | collective-permute-start | bytes 786440 | tf_op jit(solution)/shard_map/ppermute | solution.py:202
  88.3 5.9 %collective-permute-start.13 = (bf16[128,512]{1,0:T(8,128)(2,1)S(1)}, bf16[128,512]{1,0:T(8,128)(2,1)S(1)}, u32[]{:S(2)}, u32[]{:S(2)}) collective-permute-start(bf16[128,512]{1,0:T(8,128)(2,1)S(1)} %collective-permute-done.11.refs_8_), channel_id=1, source_target_pairs={{0,8},{4,12},{8,0},{12,4},{16,24},{20,28},{24,16},{28,20},{1,9},{5... | collective-permute-start | bytes 393224 | tf_op jit(solution)/shard_map/ppermute | solution.py:202
  88.3 12.0 %collective-permute-start.7 = (bf16[8,128,128]{2,1,0:T(8,128)(2,1)S(1)}, bf16[8,128,128]{2,1,0:T(8,128)(2,1)S(1)}, u32[]{:S(2)}, u32[]{:S(2)}) collective-permute-start(bf16[8,128,128]{2,1,0:T(8,128)(2,1)S(1)} %collective-permute-done.6.refs_2_), channel_id=1, source_target_pairs={{0,1},{1,0},{2,3},{3,2},{4,5},{5,4},{6,7},{7,6},{8,9},{9,8},{10,11... | collective-permute-start | bytes 786440 | tf_op jit(solution)/shard_map/ppermute | solution.py:202
  88.9 14.2 %collective-permute-start.4 = (bf16[128,1024]{1,0:T(8,128)(2,1)S(1)}, bf16[128,1024]{1,0:T(8,128)(2,1)S(1)}, u32[]{:S(2)}, u32[]{:S(2)}) collective-permute-start(bf16[128,1024]{1,0:T(8,128)(2,1)S(1)} %fusion.1), channel_id=1, source_target_pairs={{0,2},{1,3},{2,0},{3,1},{4,6},{5,7},{6,4},{7,5},{8,10},{9,11},{10,... | collective-permute-start | bytes 786440 | tf_op jit(solution)/shard_map/ppermute | solution.py:202
  89.5 6.4 %collective-permute-start.12 = (bf16[128,512]{1,0:T(8,128)(2,1)S(1)}, bf16[128,512]{1,0:T(8,128)(2,1)S(1)}, u32[]{:S(2)}, u32[]{:S(2)}) collective-permute-start(bf16[128,512]{1,0:T(8,128)(2,1)S(1)} %collective-permute-done.11.refs_8_), channel_id=1, source_target_pairs={{0,4},{4,0},{8,12},{12,8},{16,20},{20,16},{24,28},{28,24},{1,5},{5... | collective-permute-start | bytes 393224 | tf_op jit(solution)/shard_map/ppermute | solution.py:202
  91.1 7.4 %collective-permute-start.10 = (bf16[128,512]{1,0:T(8,128)(2,1)S(1)}, bf16[128,512]{1,0:T(8,128)(2,1)S(1)}, u32[]{:S(2)}, u32[]{:S(2)}) collective-permute-start(bf16[128,512]{1,0:T(8,128)(2,1)S(1)} %collective-permute-done.9.refs_6_), channel_id=1, source_target_pairs={{0,4},{4,0},{8,12},{12,8},{16,20},{20,16},{24,28},{28,24},{1,5},{5... | collective-permute-start | bytes 393224 | tf_op jit(solution)/shard_map/ppermute | solution.py:202
  94.2 6.1 %collective-permute-start.14 = (bf16[128,512]{1,0:T(8,128)(2,1)S(1)}, bf16[128,512]{1,0:T(8,128)(2,1)S(1)}, u32[]{:S(2)}, u32[]{:S(2)}) collective-permute-start(bf16[128,512]{1,0:T(8,128)(2,1)S(1)} %collective-permute-done.13.refs_10_), channel_id=1, source_target_pairs={{0,4},{4,0},{8,12},{12,8},{16,20},{20,16},{24,28},{28,24},{1,5},{5... | collective-permute-start | bytes 393224 | tf_op jit(solution)/shard_map/ppermute | solution.py:202
where the time goes:
time: 106 us; the launch traced here: 105 us
  waiting for transfers between devices  29.4 us (28%)
  starting transfers between devices  24.6 us (23%)
  blocking collectives  20.6 us (19%)
  Pallas kernels  16.4 us (15%)
  local copies, waits for them, and re-layouts  12.4 us (12%)
    ppermute x15, waiting for transfers between devices, swap_bits(): return lax.ppermute(shard, axis, [(i, i ^ mask) for i in range(size)])  29.4 us
    all_to_all x1, blocking collectives, on_device_packed(): moved = lax.all_to_all(send, 'seq', 0, 0, tiled=True)  20.6 us
    pallas_call x7, Pallas kernels, call(): pl.pallas_call(kernel, out_shape=outs, in_specs=[smem] * len(scalars) + [...  16.4 us
    ppermute x15, starting transfers between devices, swap_bits(): return lax.ppermute(shard, axis, [(i, i ^ mask) for i in range(size)])  13.6 us
    unnamed x26, local copies, waits for them, and re-layouts  11.2 us
    all_to_all x1, starting transfers between devices, on_device_packed(): streams = lax.all_to_all(packed, 'seq', 0, 0, tiled=True)  7.28 us
    all_to_all x1, starting transfers between devices, on_device_packed(): returned = lax.all_to_all(back, 'seq', 0, 0, tiled=True)  3.64 us
  transfers between devices with their start and end apart: 17, of which 7 were waited for; matrix products, arithmetic and copies ran while one was open for 2% of the time, Pallas kernels for 9%

commit v1 on v0

--- a/solution.py
+++ b/solution.py
@@ -193,6 +193,7 @@
 
 LANES = 128
 HALF = 64
+LIMIT = 64 * 2**20 - 2**17
 F32 = jnp.float32
 BF16 = jnp.bfloat16
 
@@ -204,12 +205,13 @@
 
 @functools.lru_cache
 def wave_tables(rows):
-    steps = np.outer(2 * np.arange(rows) + 1, np.arange(rows)) % (4 * rows)
+    half = rows // 2
+    steps = np.outer(2 * np.arange(half) + 1, np.arange(rows)) % (4 * rows)
     angle = steps * (math.pi / (2 * rows))
-    cosine, sine = np.cos(angle), np.sin(angle)
-    inverse = np.concatenate([cosine.T, sine.T], axis=1) / rows
-    forward = np.concatenate([cosine, sine], axis=0)
-    return forward.astype(ml_dtypes.bfloat16), inverse.astype(ml_dtypes.bfloat16)
+    waves = np.concatenate([np.cos(angle), np.sin(angle)], axis=0)
+    split = np.stack([waves[:, 0::2], waves[:, 1::2]])
+    inverse = np.swapaxes(split, 1, 2) / rows
+    return split.astype(ml_dtypes.bfloat16), inverse.astype(ml_dtypes.bfloat16)
 
 
 def left_lanes(rows):
@@ -235,20 +237,58 @@
     return jnp.where(row < size - by, pltpu.roll(block, size - by, 0), 0.0)
 
 
-def big_dot(matrix_ref, operand, out_ref, step=256):
-    for start in range(0, matrix_ref.shape[0], step):
-        out_ref[start : start + step] = jnp.dot(
-            matrix_ref[start : start + step], operand, preferred_element_type=F32
-        )
-
-
-def pack_streams_kernel(q_ref, k_ref, v_ref, h_ref, out_ref):
+def spectrum(table_ref, signal_ref, out_ref):
+    half = table_ref.shape[2]
+    quarter = 256
+    even = signal_ref[pl.ds(0, half, stride=2)].astype(BF16)
+    odd = signal_ref[pl.ds(1, half, stride=2)].astype(BF16)
+    for start in range(0, 2 * half, quarter):
+        at = slice(start, start + quarter)
+        first = jnp.dot(table_ref[0, at], even, preferred_element_type=F32)
+        second = jnp.dot(table_ref[1, at], odd, preferred_element_type=F32)
+        kind, row = (0, start) if start < half else (2, start - half)
+        out_ref[kind, row : row + quarter] = first + second
+        mirrored = first - second if kind == 0 else second - first
+        out_ref[kind + 1, row : row + quarter] = mirrored
+
+
+def from_spectrum(table_ref, parts, out_ref):
+    half = table_ref.shape[1]
+    quarter = 256
+    cosine, cosine_mirror, sine, sine_mirror = parts
+    even = jnp.concatenate([cosine + cosine_mirror, sine - sine_mirror], axis=0).astype(BF16)
+    odd = jnp.concatenate([cosine - cosine_mirror, sine + sine_mirror], axis=0).astype(BF16)
+    for side, operand in enumerate((even, odd)):
+        for start in range(0, half, quarter):
+            out_ref[pl.ds(2 * start + side, quarter, stride=2)] = jnp.dot(
+                table_ref[side, start : start + quarter], operand, preferred_element_type=F32
+            )
+
+
+def fetch(pairs, sems):
+    copies = [
+        pltpu.make_async_copy(source, target, sems.at[at])
+        for at, (source, target) in enumerate(pairs)
+    ]
+    for copy in copies:
+        copy.start()
+    return copies
+
+
+def finish(copies):
+    for copy in copies:
+        copy.wait()
+
+
+def pack_streams_kernel(q_hbm, k_hbm, v_hbm, h_hbm, out_hbm, q_ref, k_ref, v_ref, h_ref, out_ref, sems):
+    copies = fetch(((k_hbm, k_ref), (q_hbm, q_ref), (v_hbm, v_ref), (h_hbm, h_ref)), sems)
     rows = q_ref.shape[0]
     left = left_lanes(rows)
-    for peer in range(out_ref.shape[0]):
-        lanes = slice(LANES * (peer // 2), LANES * (peer // 2) + LANES)
-        pairs = ((k_ref, q_ref), (v_ref, h_ref))
-        for at, (first_ref, second_ref) in enumerate(pairs):
+    for at, (first_ref, second_ref) in enumerate(((k_ref, q_ref), (v_ref, h_ref))):
+        copies[2 * at].wait()
+        copies[2 * at + 1].wait()
+        for peer in range(out_ref.shape[0]):
+            lanes = slice(LANES * (peer // 2), LANES * (peer // 2) + LANES)
             first = first_ref[:, lanes].astype(F32)
             second = second_ref[:, lanes].astype(F32)
             if peer % 2 == 0:
@@ -256,106 +296,183 @@
             else:
                 both = jnp.where(left, other_half(first), second)
             out_ref[peer, at] = both.astype(BF16)
-
-
-def grad_gated_kernel(ids_ref, c0_ref, c1_ref, c2_ref, c3_ref, w_ref, out_ref):
+    finish(fetch(((out_ref, out_hbm),), sems))
+
+
+def fold_rows(block):
+    half = block.shape[0] // 2
+    return jnp.where(left_lanes(half), block[:half], other_half(block[half:]))
+
+
+def unfold_rows(folds):
+    blocks, half, _ = folds.shape
+    turned = pltpu.roll(folds, HALF, 2)
+    left = lax.broadcasted_iota(jnp.int32, folds.shape, 2) < HALF
+    both = [jnp.where(left, folds, turned), jnp.where(left, turned, folds)]
+    return jnp.concatenate(both, axis=1).reshape(blocks * 2 * half, LANES)
+
+
+def column_parts(w_hbm, w_ref, order, mine, sems):
+    width = w_ref.shape[2]
+    places = [pl.multiple_of((mine ^ mask) * width, width) for mask in order]
+    return fetch(
+        [(w_hbm.at[:, pl.ds(at, width)], w_ref.at[n]) for n, at in enumerate(places)], sems
+    )
+
+
+def grad_gated_kernel(
+    ids_ref, c0_hbm, c1_hbm, c2_hbm, c3_hbm, w_hbm, after_ref, send_hbm,
+    c0_ref, c1_ref, c2_ref, c3_ref, w_ref, send_ref, cot_sems, sems,
+):
     mine = ids_ref[1]
-    width = c0_ref.shape[1]
+    cots = (c0_ref, c1_ref, c2_ref, c3_ref)
+    loads = fetch(zip((c0_hbm, c1_hbm, c2_hbm, c3_hbm), cots), cot_sems)
+    copies = column_parts(w_hbm, w_ref, range(4), mine, sems)
+    rows = c0_ref.shape[0]
+    for mask, part_ref in enumerate(cots):
+        loads[mask].wait()
+        for half in range(2):
+            at = pl.multiple_of(half * 4 * LANES + mine * LANES, LANES)
+            turned = part_ref[:, pl.ds(at, LANES)].astype(F32).T
+            send_ref[2 * (mine ^ mask) + half, rows // 2 :] = turned.astype(BF16)
     total = None
-    for mask, part_ref in enumerate((c0_ref, c1_ref, c2_ref, c3_ref)):
-        at = pl.multiple_of((mine ^ mask) * width, width)
+    for mask, part_ref in enumerate(cots):
+        copies[mask].wait()
         term = lax.dot_general(
-            part_ref[...],
-            w_ref[:, pl.ds(at, width)],
-            (((1,), (1,)), ((), ())),
-            preferred_element_type=F32,
+            part_ref[...], w_ref[mask], (((1,), (1,)), ((), ())), preferred_element_type=F32
         )
         total = term if total is None else total + term
-    out_ref[...] = total.astype(BF16)
+    for peer in range(send_ref.shape[0]):
+        tile = total[:, LANES * (peer // 2) : LANES * (peer // 2) + LANES]
+        if peer % 2 == 1:
+            tile = other_half(tile)
+        send_ref[peer, : rows // 2] = fold_rows(tile).astype(BF16)
+    finish(fetch(((send_ref, send_hbm),), sems))
 
 
 def forward_kernel(
-    ids_ref, moved_ref, prm_ref, fwd_ref, inv_ref, gg_ref, c0_ref, c1_ref, c2_ref, c3_ref,
-    send_ref, kqs_ref, vhs_ref, mq_ref, spec_ref, y_ref,
+    moved_hbm, fwd_hbm, inv_hbm, after_hbm, prm_ref,
+    send_hbm, kqs_hbm, vhs_hbm, mq_hbm, spec_hbm,
+    moved_ref, fwd_ref, inv_ref, send_ref, kqs_ref, vhs_ref, mq_ref, spec_ref,
+    signal_ref, y_ref, sems, out_sems,
 ):
+    copies = fetch(((moved_hbm, moved_ref), (fwd_hbm, fwd_ref), (inv_hbm, inv_ref)), sems)
     peers, _, rows, _ = moved_ref.shape
     size = peers * rows
     left = left_lanes(size)
+    copies[0].wait()
     kq = moved_ref[:, 0].reshape(size, LANES).astype(F32)
     vh = moved_ref[:, 1].reshape(size, LANES).astype(F32)
     kqs = sum(prm_ref[j : j + 1] * earlier_rows(kq, j) for j in range(3))
     vhs = sum(prm_ref[3 + j : 4 + j] * earlier_rows(vh, j) for j in range(3))
     kqs_ref[...] = kqs
     vhs_ref[...] = vhs
+    done = fetch(((kqs_ref, kqs_hbm), (vhs_ref, vhs_hbm)), out_sems)
     product = kqs * vhs
-    big_dot(fwd_ref, jnp.where(left, product, vhs).astype(BF16), spec_ref)
-    xc, xs = spec_ref[:size], spec_ref[size:]
-    hc, hs = other_half(xc), other_half(xs)
-    y_parts = jnp.concatenate([xc * hc - xs * hs, xc * hs + xs * hc], axis=0).astype(BF16)
-    big_dot(inv_ref, y_parts, y_ref)
+    signal_ref[...] = jnp.where(left, product, vhs)
+    copies[1].wait()
+    spectrum(fwd_ref, signal_ref, spec_ref)
+    done += fetch(((spec_ref, spec_hbm),), out_sems.at[pl.ds(2, 1)])
+    parts = [None] * 4
+    for mirror in range(2):
+        xc, xs = spec_ref[mirror], spec_ref[2 + mirror]
+        hc, hs = other_half(xc), other_half(xs)
+        parts[mirror] = xc * hc - xs * hs
+        parts[2 + mirror] = xc * hs + xs * hc
+    copies[2].wait()
+    from_spectrum(inv_ref, parts, y_ref)
     both_product = jnp.where(left, product, other_half(product))
     mixed = y_ref[...] + prm_ref[12:13] * both_product
     mq_ref[...] = jnp.where(left, mixed, kqs)
     gated = kqs * mixed
     left_rows = left_lanes(rows)
-    for peer in range(peers):
-        lanes = slice(LANES * (peer // 2), LANES * (peer // 2) + LANES)
-        gg = gg_ref[:, lanes].astype(F32)
-        if peer % 2 == 1:
-            gg = other_half(gg)
-        mine = gated[rows * peer : rows * peer + rows]
-        send_ref[peer, :rows] = jnp.where(left_rows, gg, mine).astype(BF16)
-    own = ids_ref[1]
-    for mask, part_ref in enumerate((c0_ref, c1_ref, c2_ref, c3_ref)):
-        for half in range(2):
-            at = pl.multiple_of(half * 4 * LANES + own * LANES, LANES)
-            send_ref[2 * (own ^ mask) + half, rows:] = part_ref[:, pl.ds(at, LANES)]
-
-
-def project_kernel(ids_ref, moved_ref, w_ref, gated_ref, keep_ref, send_ref, cot_ref):
-    peers = moved_ref.shape[0]
-    rows = moved_ref.shape[1] // 2
-    left = left_lanes(rows)
-    for tile in range(peers // 2):
-        first = moved_ref[2 * tile, :rows].astype(F32)
-        second = moved_ref[2 * tile + 1, :rows].astype(F32)
-        both = jnp.where(left, other_half(first), second)
-        gated_ref[:, LANES * tile : LANES * tile + LANES] = both.astype(BF16)
-    cot_ref[...] = moved_ref[:, rows:]
+    for pair in range(peers // 2):
+        first = gated[2 * rows * pair : 2 * rows * pair + rows]
+        second = gated[2 * rows * pair + rows : 2 * rows * (pair + 1)]
+        send_ref[pair] = jnp.where(left_rows, other_half(first), second).astype(BF16)
+    done += fetch(((mq_ref, mq_hbm), (send_ref, send_hbm)), out_sems.at[pl.ds(3, 2)])
+    finish(done)
+
+
+def project_kernel(ids_ref, *refs):
+    gates = refs[:8]
+    w_hbm, keep_hbm, *send_hbm = refs[8:13]
+    gate_ref, w_ref, keep_ref, *send_ref = refs[13:19]
+    gated_ref, gate_sems, sems = refs[19:]
+    own_row, mine = ids_ref[0], ids_ref[1]
+    loads = fetch(
+        [(gate.at[own_row // 2], gate_ref.at[at]) for at, gate in enumerate(gates)], gate_sems
+    )
+    order = (2, 3, 1, 0)
+    copies = column_parts(w_hbm, w_ref, order, mine, sems)
+    left = left_lanes(gate_ref.shape[1])
+    odd = own_row % 2 == 1
+    finish(loads)
+    for pair in range(len(gates) // 2):
+        one = gate_ref[2 * pair].astype(F32)
+        two = gate_ref[2 * pair + 1].astype(F32)
+        even_rows = jnp.where(left, one, other_half(two))
+        odd_rows = jnp.where(left, other_half(two), one)
+        lanes = pl.ds(pl.multiple_of(((own_row // 2) ^ pair) * LANES, LANES), LANES)
+        gated_ref[:, lanes] = jnp.where(odd, odd_rows, even_rows).astype(BF16)
     gated = gated_ref[...]
-    mine = ids_ref[1]
-    width = keep_ref.shape[2]
-    for mask in (1, 3, 0, 2):
-        at = pl.multiple_of((mine ^ mask) * width, width)
-        part = jnp.dot(gated, w_ref[:, pl.ds(at, width)], preferred_element_type=F32)
-        if mask % 2 == 1:
-            send_ref[mask // 2] = part.astype(BF16)
+    done = []
+    for n, mask in enumerate(order):
+        copies[n].wait()
+        part = jnp.dot(gated, w_ref[n], preferred_element_type=F32)
+        if mask:
+            send_ref[mask - 1][...] = part.astype(BF16)
+            target = (send_ref[mask - 1], send_hbm[mask - 1])
         else:
-            keep_ref[mask // 2] = part
+            keep_ref[...] = part
+            target = (keep_ref, keep_hbm)
+        done += fetch((target,), gate_sems.at[pl.ds(n, 1)])
+    finish(done)
 
 
 def backward_kernel(
-    streams_ref, moved_ref, prm_ref, fwd_ref, inv_ref, kqs_ref, vhs_ref, mq_ref, spec_ref,
-    send_ref, mspec_ref, back_ref,
+    moved_hbm, mq_hbm, spec_hbm, kqs_hbm, vhs_hbm, streams_hbm, fwd_hbm, inv_hbm, prm_ref,
+    send_hbm,
+    moved_ref, mq_ref, spec_ref, kqs_ref, vhs_ref, streams_ref, fwd_ref, inv_ref, send_ref,
+    signal_ref, mspec_ref, back_ref, sems,
 ):
+    copies = fetch(
+        (
+            (moved_hbm.at[:, pl.ds(0, moved_ref.shape[1])], moved_ref),
+            (mq_hbm, mq_ref),
+            (fwd_hbm, fwd_ref),
+            (spec_hbm, spec_ref),
+            (inv_hbm, inv_ref),
+            (kqs_hbm, kqs_ref),
+            (vhs_hbm, vhs_ref),
+            (streams_hbm, streams_ref),
+        ),
+        sems,
+    )
     peers, _, rows, _ = streams_ref.shape
     size = peers * rows
     left = left_lanes(size)
-    gg = moved_ref[:, :rows].reshape(size, LANES).astype(F32)
-    gg = jnp.where(left, gg, other_half(gg))
-    z = gg * mq_ref[...]
+    finish(copies[:2])
+    z = unfold_rows(moved_ref[...].astype(F32)) * mq_ref[...]
     grad_mixed = jnp.where(left, other_half(z), z)
-    big_dot(fwd_ref, grad_mixed.astype(BF16), mspec_ref)
-    xc, xs = spec_ref[:size], spec_ref[size:]
-    mc, ms = mspec_ref[:size], mspec_ref[size:]
-    parts = jnp.concatenate([xc * mc + xs * ms, xc * ms - xs * mc], axis=0).astype(BF16)
-    big_dot(inv_ref, parts, back_ref)
+    signal_ref[...] = grad_mixed
+    copies[2].wait()
+    spectrum(fwd_ref, signal_ref, mspec_ref)
+    copies[3].wait()
+    parts = [None] * 4
+    for mirror in range(2):
+        xc, xs = spec_ref[mirror], spec_ref[2 + mirror]
+        mc, ms = mspec_ref[mirror], mspec_ref[2 + mirror]
+        parts[mirror] = xc * mc + xs * ms
+        parts[2 + mirror] = xc * ms - xs * mc
+    copies[4].wait()
+    from_spectrum(inv_ref, parts, back_ref)
+    finish(copies[5:])
     back = back_ref[...]
     kqs, vhs = kqs_ref[...], vhs_ref[...]
     grad_product = back + prm_ref[12:13] * grad_mixed
     grad_product = jnp.where(left, other_half(grad_product), grad_product)
     grad_kv = grad_product * jnp.where(left, vhs, other_half(kqs))
-    grad_qf = jnp.where(left, z, back)
     grad_qf = jnp.where(left, z, other_half(back))
     kq = streams_ref[:, 0].reshape(size, LANES).astype(F32)
     vh = streams_ref[:, 1].reshape(size, LANES).astype(F32)
@@ -375,9 +492,14 @@
         send_ref[peer, :rows] = out_kv[at].astype(BF16)
         send_ref[peer, rows : 2 * rows] = out_qf[at].astype(BF16)
         send_ref[peer, 2 * rows :] = small
-
-
-def unpack_kernel(moved_ref, q_ref, k_ref, v_ref, f_ref, short_ref, skip_ref):
+    finish(fetch(((send_ref, send_hbm),), sems))
+
+
+def unpack_kernel(
+    moved_hbm, q_hbm, k_hbm, v_hbm, f_hbm, short_ref, skip_ref,
+    moved_ref, q_ref, k_ref, v_ref, f_ref, sems,
+):
+    finish(fetch(((moved_hbm, moved_ref),), sems))
     peers = moved_ref.shape[0]
     rows = q_ref.shape[0]
     left = left_lanes(rows)
@@ -389,52 +511,87 @@
             jnp.where(mask, other_half(first), second),
         )
 
-    for tile in range(peers // 2):
+    tiles = range(peers // 2)
+    for tile in tiles:
         lanes = slice(LANES * tile, LANES * tile + LANES)
-        first, second = moved_ref[2 * tile].astype(F32), moved_ref[2 * tile + 1].astype(F32)
-        k_ref[:, lanes], v_ref[:, lanes] = merged(first[:rows], second[:rows], left)
-        q_ref[:, lanes], f_ref[:, lanes] = merged(
-            first[rows : 2 * rows], second[rows : 2 * rows], left
-        )
-        few = [part[2 * rows : 2 * rows + 8] + part[2 * rows + 8 :] for part in (first, second)]
-        low, high = merged(few[0], few[1], left_few)
+        first, second = (moved_ref[2 * tile + n, :rows].astype(F32) for n in range(2))
+        k_ref[:, lanes], v_ref[:, lanes] = merged(first, second, left)
+    done = fetch(((k_ref, k_hbm), (v_ref, v_hbm)), sems)
+    for tile in tiles:
+        lanes = slice(LANES * tile, LANES * tile + LANES)
+        first, second = (moved_ref[2 * tile + n, rows : 2 * rows].astype(F32) for n in range(2))
+        q_ref[:, lanes], f_ref[:, lanes] = merged(first, second, left)
+        few = [moved_ref[2 * tile + n, 2 * rows :].astype(F32) for n in range(2)]
+        low, high = merged(few[0][:8] + few[0][8:], few[1][:8] + few[1][8:], left_few)
         short_ref[0, :, lanes] = low[3:6]
         short_ref[1, :, lanes] = low[0:3]
         short_ref[2, :, lanes] = high[0:3]
         skip_ref[:, lanes] = low[6:7]
+    done += fetch(((q_ref, q_hbm), (f_ref, f_hbm)), sems.at[pl.ds(2, 2)])
+    finish(done)
 
 
 def grad_weight_kernel(ids_ref, *refs):
-    out_ref = refs[-1]
-    cots, gates = refs[:4], refs[4:-1]
+    cots, gates = refs[:4], refs[4:12]
+    out_hbm, cot_ref, gate_ref, side_ref, total_ref, sems, out_sems = refs[12:]
     own_row, own = ids_ref[0], ids_ref[1]
-    for mask, cot_ref in enumerate(cots):
-        total = None
-        for at, gate_ref in enumerate(gates):
-            term = lax.dot_general(
-                cot_ref[own_row ^ at],
-                gate_ref[...],
-                (((0,), (0,)), ((), ())),
-                preferred_element_type=F32,
+    copies = fetch(
+        [(cot, cot_ref.at[at]) for at, cot in enumerate(cots)]
+        + [(gate, gate_ref.at[at]) for at, gate in enumerate(gates)],
+        sems,
+    )
+    _, peers, high, wide = cot_ref.shape
+    left = left_lanes(4 * high)
+    odd = own_row % 2 == 1
+    for mask in range(4):
+        copies[mask].wait()
+        for peer in range(peers):
+            lanes = slice(wide * (peer // 2), wide * (peer // 2) + wide)
+            side_ref[peer % 2, high * mask : high * mask + high, lanes] = cot_ref[mask, peer]
+    done = []
+    for pair in range(peers // 2):
+        finish(copies[4 + 2 * pair : 6 + 2 * pair])
+        found = []
+        for at in (2 * pair, 2 * pair + 1):
+            gate = gate_ref[at].reshape(peers // 2 * wide, LANES)
+            found.append(
+                [jnp.dot(side_ref[n], gate, preferred_element_type=F32) for n in range(2)]
             )
-            total = term if total is None else total + term
-        out_ref[pl.ds(pl.multiple_of((own ^ mask) * LANES, LANES), LANES)] = total
-
-
-def call(kernel, outs, scalars, *arrays, scratch=(), limit=32, flops=0):
+        (even_low, even_high), (odd_low, odd_high) = found
+        even_sum = even_low + other_half(even_high)
+        odd_sum = odd_low + other_half(odd_high)
+        ahead = jnp.where(left, even_sum, other_half(odd_sum))
+        behind = jnp.where(left, odd_sum, other_half(even_sum))
+        tile = jnp.where(odd, behind, ahead)
+        for mask in range(4):
+            at = pl.ds(pl.multiple_of((own ^ mask) * high, high), high)
+            total_ref[pair, at] = tile[high * mask : high * mask + high]
+        lanes = pl.ds(pl.multiple_of(((own_row // 2) ^ pair) * LANES, LANES), LANES)
+        done += fetch(
+            ((total_ref.at[pair], out_hbm.at[:, lanes]),), out_sems.at[pl.ds(pair, 1)]
+        )
+    finish(done)
+
+
+def call(
+    kernel, outs, scalars, *arrays, small=(), small_outs=(), scratch=(), dmas=(8,)
+):
     vmem = pl.BlockSpec(memory_space=pltpu.VMEM)
     smem = pl.BlockSpec(memory_space=pltpu.SMEM)
-    many = isinstance(outs, list)
-    moved = sum(math.prod(a.shape) * a.dtype.itemsize for a in arrays)
+    hbm = pl.BlockSpec(memory_space=pltpu.HBM)
     return pl.pallas_call(
         kernel,
-        out_shape=outs,
-        in_specs=[smem] * len(scalars) + [vmem] * len(arrays),
-        out_specs=[vmem] * len(outs) if many else vmem,
-        scratch_shapes=list(scratch),
-        compiler_params=pltpu.CompilerParams(vmem_limit_bytes=limit * 2**20),
-        cost_estimate=pl.CostEstimate(flops=flops, bytes_accessed=moved, transcendentals=0),
-    )(*scalars, *arrays)
+        out_shape=list(outs) + list(small_outs),
+        in_specs=[smem] * len(scalars) + [hbm] * len(arrays) + [vmem] * len(small),
+        out_specs=[hbm] * len(outs) + [vmem] * len(small_outs),
+        scratch_shapes=[pltpu.VMEM(a.shape, a.dtype) for a in scratch]
+        + [pltpu.SemaphoreType.DMA((count,)) for count in dmas],
+        compiler_params=pltpu.CompilerParams(vmem_limit_bytes=LIMIT),
+        cost_estimate=pl.CostEstimate(
+            flops=1, bytes_accessed=1, transcendentals=0
+        ),
+        name=kernel.__name__.removesuffix("_kernel"),
+    )(*scalars, *arrays, *small)
 
 
 def shaped(shape, dtype):
@@ -447,11 +604,18 @@
     return [block, near, far, swap_bits(far, axis, 1)]
 
 
-def gathered_all(block, axis):
-    blocks = {0: block}
+def gathered_first(block, axis):
     mask = lax.axis_size(axis) // 2
+    return {0: block, mask: swap_bits(block, axis, mask), mask // 2: swap_bits(block, axis, mask // 2), 1: swap_bits(block, axis, 1)}
+
+
+def gathered_rest(blocks, axis):
+    top = lax.axis_size(axis) // 2
+    mask = top // 2
     while mask:
-        blocks |= {at | mask: swap_bits(held, axis, mask) for at, held in blocks.items()}
+        for at in list(blocks):
+            if at % (2 * mask) == 0 and at | mask not in blocks:
+                blocks[at | mask] = swap_bits(blocks[at], axis, mask)
         mask //= 2
     return [blocks[at] for at in range(len(blocks))]
 
@@ -480,91 +644,103 @@
         axis=1,
     )
 
-    packed = call(
-        pack_streams_kernel,
-        shaped((peers, 2, rows, LANES), BF16),
-        [],
-        query_proj,
-        key_proj,
-        value_proj,
-        long_filter,
-    )
+    inputs = (query_proj, key_proj, value_proj, long_filter)
+    packs = shaped((peers, 2, rows, LANES), BF16)
+    (packed,) = call(pack_streams_kernel, [packs], [], *inputs, scratch=(*inputs, packs))
     streams = lax.all_to_all(packed, "seq", 0, 0, tiled=True)
-    grad_gated = call(
+    weight_room = shaped((4, channels, features), BF16)
+    sent = shaped((peers, rows // 2 + rows, LANES), BF16)
+    (sent_grad,) = call(
         grad_gated_kernel,
-        shaped((rows, channels), BF16),
+        [sent],
         [ids],
         *cots,
         out_weight,
-        flops=2 * rows * channels * 4 * features,
-    )
+        small=(prm,),
+        scratch=(*cots, weight_room, sent),
+        dmas=(4, 4),
+    )
+    moved_grad = lax.all_to_all(sent_grad, "seq", 0, 0, tiled=True)
     wide = shaped((size, LANES), F32)
-    send, kqs, vhs, mq, spec = call(
+    spectra = shaped((4, size // 2, LANES), F32)
+    folds = shaped((peers // 2, rows, LANES), BF16)
+    tables = (forward_table, inverse_table)
+    results = [folds, wide, wide, wide, spectra]
+    gated, kqs, vhs, mq, spec = call(
         forward_kernel,
-        [shaped((peers, 2 * rows, LANES), BF16), wide, wide, wide, shaped((2 * size, LANES), F32)],
-        [ids],
-        streams,
-        prm,
-        forward_table,
-        inverse_table,
-        grad_gated,
-        *cots,
-        scratch=[pltpu.VMEM((size, LANES), F32)],
-        flops=8 * size * size * LANES,
-    )
-    moved = lax.all_to_all(send, "seq", 0, 0, tiled=True)
-    gated, keep, away, cot_rows = call(
-        project_kernel,
-        [
-            shaped((rows, channels), BF16),
-            shaped((2, rows, features), F32),
-            shaped((2, rows, features), BF16),
-            shaped((peers, rows, LANES), BF16),
-        ],
-        [ids],
-        moved,
-        out_weight,
-        flops=2 * rows * channels * 4 * features,
-    )
-    near = swap_bits(away, "ch", 1)
-    passed = (keep[1] + near[1].astype(F32)).astype(BF16)
-    layer_out = (keep[0] + near[0].astype(F32) + swap_bits(passed, "ch", 2).astype(F32)).astype(
-        BF16
-    )
-    cot_parts = gathered_pairs(cot_rows, "ch")
-    gates = gathered_all(gated, "seq")
-    back = call(
-        backward_kernel,
-        shaped((peers, 2 * rows + 16, LANES), BF16),
+        results,
         [],
         streams,
-        moved,
-        prm,
-        forward_table,
-        inverse_table,
-        kqs,
-        vhs,
-        mq,
-        spec,
-        scratch=[pltpu.VMEM((2 * size, LANES), F32), pltpu.VMEM((size, LANES), F32)],
-        flops=8 * size * size * LANES,
-    )
+        *tables,
+        sent_grad,
+        small=(prm,),
+        scratch=(packs, *tables, *results, wide, wide),
+        dmas=(3, 5),
+    )
+    first_gates = gathered_first(gated, "seq")
+    backs = shaped((peers, 2 * rows + 16, LANES), BF16)
+    saved = (mq, spec, kqs, vhs, streams, *tables)
+    (back,) = call(
+        backward_kernel,
+        [backs],
+        [],
+        moved_grad,
+        *saved,
+        small=(prm,),
+        scratch=(
+            shaped((peers, rows // 2, LANES), BF16), *saved, backs, wide, spectra, wide
+        ),
+    )
+    cot_parts = gathered_pairs(moved_grad[:, rows // 2 :], "ch")
+    back, first_gates = lax.optimization_barrier((back, first_gates))
+    gates = gathered_rest(first_gates, "seq")
+    back, gates = lax.optimization_barrier((back, gates))
     returned = lax.all_to_all(back, "seq", 0, 0, tiled=True)
+    sums = [shaped((rows, features), F32)] + [shaped((rows, features), BF16)] * 3
+    keep, *away = call(
+        project_kernel,
+        sums,
+        [ids],
+        *gates,
+        out_weight,
+        scratch=(
+            shaped((peers, rows, LANES), BF16),
+            weight_room,
+            *sums,
+            shaped((rows, channels), BF16),
+        ),
+        dmas=(8, 4),
+    )
+    shares = [swap_bits(part, "ch", mask) for mask, part in enumerate(away, 1)]
     plain = shaped((rows, channels), F32)
     grad_query, grad_key, grad_value, grad_filter, grad_short, grad_skip = call(
         unpack_kernel,
-        [plain, plain, plain, plain, shaped((3, 3, channels), F32), shaped((1, channels), F32)],
+        [plain] * 4,
         [],
         returned,
-    )
-    grad_w_out_t = call(
+        small_outs=[shaped((3, 3, channels), F32), shaped((1, channels), F32)],
+        scratch=(backs, plain, plain, plain, plain),
+    )
+    (grad_w_out_t,) = call(
         grad_weight_kernel,
-        shaped((4 * LANES, channels), F32),
+        [shaped((4 * LANES, channels), F32)],
         [ids],
         *cot_parts,
         *gates,
-        flops=2 * size * channels * 4 * LANES,
-    )
+        scratch=(
+            shaped((4, peers, LANES, rows), BF16),
+            shaped((peers, peers // 2, rows, LANES), BF16),
+            shaped((2, 4 * LANES, peers // 2 * rows), BF16),
+            shaped((peers // 2, 4 * LANES, LANES), F32),
+        ),
+        dmas=(12, 4),
+    )
+    shares, grad_w_out_t, grad_filter = lax.optimization_barrier(
+        (shares, grad_w_out_t, grad_filter)
+    )
+    for part in shares:
+        keep = keep + part.astype(F32)
+    layer_out = keep.astype(BF16)
     return (
         layer_out,
         grad_query,

time: 106 us -> 91.8 us (0.87)
  blocking collectives: 20.6 us -> 0 us
  Pallas kernels: 16.4 us -> 32.6 us
  waiting for transfers between devices: 29.4 us -> 17.3 us
  local copies, waits for them, and re-layouts: 12.4 us -> 4.18 us
  starting transfers between devices: 24.6 us -> 32.7 us
  other arithmetic: 1.02 us -> 3.38 us
    all_to_all x1 -> x0, blocking collectives: 20.6 us -> none  [on_device_packed(): moved = lax.all_to_all(send, 'seq', 0, 0, tiled=True)]
    pallas_call x7, Pallas kernels: 16.4 us -> 32.6 us  [call(): pl.pallas_call(kernel, out_shape=list(outs) + list(small_outs), in_specs=...]
    ppermute x15 -> x16, waiting for transfers between devices: 29.4 us -> 15.4 us  [swap_bits(): return lax.ppermute(shard, axis, [(i, i ^ mask) for i in range(size)])]
    unnamed x26 -> x6, local copies, waits for them, and re-layouts: 11.2 us -> 1.37 us
    all_to_all x0 -> x1, starting transfers between devices: none -> 5.73 us  [on_device_packed(): moved_grad = lax.all_to_all(sent_grad, 'seq', 0, 0, tiled=True)]
    all_to_all x0 -> x1, waiting for transfers between devices: none -> 1.93 us  [on_device_packed(): moved_grad = lax.all_to_all(sent_grad, 'seq', 0, 0, tiled=True)]
    slice x0 -> x1, local copies, waits for them, and re-layouts: none -> 1.68 us  [on_device_packed(): cot_parts = gathered_pairs(moved_grad[:, rows // 2:], 'ch')]
    ppermute x15 -> x16, starting transfers between devices: 13.6 us -> 15.3 us  [swap_bits(): return lax.ppermute(shard, axis, [(i, i ^ mask) for i in range(size)])]
  transfers between devices with their start and end apart: 17 -> 19, of which waited for: 7 -> 7; matrix products, arithmetic and copies ran while one was open for 2% -> 4% of each run, Pallas kernels for 9% -> 34%
where the time goes in v1:
time: 91.8 us; the launch traced here: 90.9 us
  starting transfers between devices  32.7 us (36%)
  Pallas kernels  32.6 us (36%)
  waiting for transfers between devices  17.3 us (19%)
  local copies, waits for them, and re-layouts  4.18 us (5%)
  other arithmetic  3.38 us (4%)
    pallas_call x7, Pallas kernels, call(): pl.pallas_call(kernel, out_shape=list(outs) + list(small_outs), in_specs=...  32.6 us
    ppermute x16, waiting for transfers between devices, swap_bits(): return lax.ppermute(shard, axis, [(i, i ^ mask) for i in range(size)])  15.4 us
    ppermute x16, starting transfers between devices, swap_bits(): return lax.ppermute(shard, axis, [(i, i ^ mask) for i in range(size)])  15.3 us
    all_to_all x1, starting transfers between devices, on_device_packed(): streams = lax.all_to_all(packed, 'seq', 0, 0, tiled=True)  7.29 us
    all_to_all x1, starting transfers between devices, on_device_packed(): moved_grad = lax.all_to_all(sent_grad, 'seq', 0, 0, tiled=True)  5.73 us
    all_to_all x1, starting transfers between devices, on_device_packed(): returned = lax.all_to_all(back, 'seq', 0, 0, tiled=True)  4.37 us
    convert_element_type x1, other arithmetic, on_device_packed(): layer_out = keep.astype(BF16)  2.12 us
    all_to_all x1, waiting for transfers between devices, on_device_packed(): moved_grad = lax.all_to_all(sent_grad, 'seq', 0, 0, tiled=True)  1.93 us
  transfers between devices with their start and end apart: 19, of which 7 were waited for; matrix products, arithmetic and copies ran while one was open for 4% of the time, Pallas kernels for 34%

profile of v1, /device:TPU:0, one launch (start us, length us, event | category | flops | bytes accessed | tf_op | source)
XLA Modules:
  0.0 90.9 jit_solution(12693846315560591853)
XLA Ops:
  0.6 0.0 copy-start
  0.6 2.2 %pack_streams.1 = bf16[8,2,128,128]{3,2,1,0:T(8,128)(2,1)} custom-call(bf16[128,512]{1,0:T(8,128)(2,1)} %q_hbm.1, bf16[128,512]{1,0:T(8,128)(2,1)} %k_hbm.1, bf16[128,512]{1,0:T(8,128)(2,1)} %v_hbm.1, f32[128,512]{1,0:T(8,128)} %h_hbm.1), custom_call_target="tpu_custom_call" | custom-call | flops 1 | bytes 1 | tf_op jit(solution)/shard_map/pack_streams/pallas_call | solution.py:582
  2.8 7.3 %all-to-all-start.1 = ((bf16[8,2,128,128]{3,2,1,0:T(8,128)(2,1)}), bf16[8,2,128,128]{3,2,1,0:T(8,128)(2,1)}, u32[]{:S(2)}, u32[]{:S(2)}) async-start(bf16[8,2,128,128]{3,2,1,0:T(8,128)(2,1)} %pack_streams.1), calls=%async_computation.1 | async-start | bytes 1048576 | tf_op jit(solution)/shard_map/all_to_all | solution.py:650
  10.1 1.5 %collective-permute-start.1 = (bf16[128,1024]{1,0:T(8,128)(2,1)}, bf16[128,1024]{1,0:T(8,128)(2,1)S(1)}, u32[]{:S(2)}, u32[]{:S(2)}) collective-permute-start(bf16[128,1024]{1,0:T(8,128)(2,1)} %c0_hbm.1), channel_id=1, source_target_pairs={{0,2},{1,3},{2,0},{3,1},{4,6},{5,7},{6,4},{7,5},{8,10},{9,11},{10,... | collective-permute-start | bytes 786440 | tf_op jit(solution)/shard_map/ppermute | solution.py:203
  11.6 0.0 collective-permute-start
  11.6 0.8 dynamic-slice_bitcast_fusion.2
  12.4 5.7 %collective-permute-done.1.c2_hbm = bf16[128,1024]{1,0:T(8,128)(2,1)S(1)} collective-permute-done((bf16[128,1024]{1,0:T(8,128)(2,1)}, bf16[128,1024]{1,0:T(8,128)(2,1)S(1)}, u32[]{:S(2)}, u32[]{:S(2)}) %collective-permute-start.1) | collective-permute-done | bytes 262176 | tf_op jit(solution)/shard_map/ppermute | solution.py:203
  18.1 0.7 copy-done.2
  18.8 0.0 collective-permute-start.2
  18.8 0.1 dynamic-slice_bitcast_fusion.3
  18.9 0.1 concatenate.9
  19.0 0.1 iota.11
  19.0 0.1 concatenate.10
  19.1 0.6 pad_add_fusion.ids_ref
  19.7 0.7 pad_maximum_fusion.after_ref.prm_ref
  20.4 0.0 collective-permute-done.2.c3_hbm
  20.5 5.6 %grad_gated.1.after_hbm = bf16[8,192,128]{2,1,0:T(8,128)(2,1)} custom-call(s32[2]{0:T(128)} %pad_add_fusion.ids_ref, bf16[128,1024]{1,0:T(8,128)(2,1)} %c0_hbm.1, bf16[128,1024]{1,0:T(8,128)(2,1)} %collective-permute-done.c1_hbm, bf16[128,1024]{1,0:T(8,128)(2,1)} %copy-done.2, bf16[128,1024]{1,0:T(8,128)(2,1)} %collective-permute-done.2.c3_hbm, ...), custom_call_target="tpu_custom_call" | custom-call | flops 1 | bytes 1 | tf_op jit(solution)/shard_map/grad_gated/pallas_call | solution.py:582
  26.0 5.7 %all-to-all-start = ((bf16[8,192,128]{2,1,0:T(8,128)(2,1)}), bf16[8,192,128]{2,1,0:T(8,128)(2,1)}, u32[]{:S(2)}, u32[]{:S(2)}) async-start(bf16[8,192,128]{2,1,0:T(8,128)(2,1)} %grad_gated.1.after_hbm), calls=%async_computation | async-start | bytes 786432 | tf_op jit(solution)/shard_map/all_to_all | solution.py:663
  31.8 5.1 %forward.1 = (bf16[4,128,128]{2,1,0:T(8,128)(2,1)}, f32[1024,128]{1,0:T(8,128)}, f32[1024,128]{1,0:T(8,128)}, f32[1024,128]{1,0:T(8,128)}, f32[4,512,128]{2,1,0:T(8,128)}) custom-call(bf16[8,2,128,128]{3,2,1,0:T(8,128)(2,1)} %all-to-all-done.1.moved_hbm.streams_hbm, bf16[2,1024,512]{2,1,0:T(8,128)(2,1)} %constant.20.clone.fwd_hbm, ...), custom_call_target="tpu_custom_call" | custom-call | flops 1 | bytes 1 | tf_op jit(solution)/shard_map/forward/pallas_call | solution.py:582
  36.9 2.1 %collective-permute-start.3 = (bf16[4,128,128]{2,1,0:T(8,128)(2,1)}, bf16[4,128,128]{2,1,0:T(8,128)(2,1)}, u32[]{:S(2)}, u32[]{:S(2)}) collective-permute-start(bf16[4,128,128]{2,1,0:T(8,128)(2,1)} %get-tuple-element.52.refs_0_.refs_4_), channel_id=1, source_target_pairs={{0,4},{4,0},{8,12},{12,8},{16,20},{20,16},{24,28},{28,24},{1,5},{5... | collective-permute-start | bytes 393224 | tf_op jit(solution)/shard_map/ppermute | solution.py:203
  39.0 1.5 %collective-permute-start.4 = (bf16[4,128,128]{2,1,0:T(8,128)(2,1)}, bf16[4,128,128]{2,1,0:T(8,128)(2,1)}, u32[]{:S(2)}, u32[]{:S(2)}) collective-permute-start(bf16[4,128,128]{2,1,0:T(8,128)(2,1)} %get-tuple-element.52.refs_0_.refs_4_), channel_id=1, source_target_pairs={{0,8},{4,12},{8,0},{12,4},{16,24},{20,28},{24,16},{28,20},{1,9},{5... | collective-permute-start | bytes 393224 | tf_op jit(solution)/shard_map/ppermute | solution.py:203
  40.5 2.4 %collective-permute-start.5 = (bf16[4,128,128]{2,1,0:T(8,128)(2,1)}, bf16[4,128,128]{2,1,0:T(8,128)(2,1)}, u32[]{:S(2)}, u32[]{:S(2)}) collective-permute-start(bf16[4,128,128]{2,1,0:T(8,128)(2,1)} %get-tuple-element.52.refs_0_.refs_4_), channel_id=1, source_target_pairs={{0,16},{4,20},{8,24},{12,28},{16,0},{20,4},{24,8},{28,12},{1,17},{... | collective-permute-start | bytes 393224 | tf_op jit(solution)/shard_map/ppermute | solution.py:203
  42.8 1.9 %all-to-all-done.moved_hbm = bf16[8,192,128]{2,1,0:T(8,128)(2,1)} async-done(((bf16[8,192,128]{2,1,0:T(8,128)(2,1)}), bf16[8,192,128]{2,1,0:T(8,128)(2,1)}, u32[]{:S(2)}, u32[]{:S(2)}) %all-to-all-start) | async-done | bytes 393248 | tf_op jit(solution)/shard_map/all_to_all | solution.py:663
  44.8 6.2 %backward.1 = bf16[8,272,128]{2,1,0:T(8,128)(2,1)} custom-call(bf16[8,192,128]{2,1,0:T(8,128)(2,1)} %all-to-all-done.moved_hbm, f32[1024,128]{1,0:T(8,128)} %get-tuple-element.42.mq_hbm, f32[4,512,128]{2,1,0:T(8,128)} %get-tuple-element.43.spec_hbm, f32[1024,128]{1,0:T(8,128)} %get-tuple-element.44.kqs_hbm, f32[1024,128]{1,0:T(8,128)} %get-tuple-element.45.vhs_hbm, ...), custom_call_target="tpu_custom_call" | custom-call | flops 1 | bytes 1 | tf_op jit(solution)/shard_map/backward/pallas_call | solution.py:582
  51.0 0.0 collective-permute-done.3.refs_1_.refs_5_
  51.0 0.6 collective-permute-start.8
  51.7 1.2 %collective-permute-start.7 = (bf16[4,128,128]{2,1,0:T(8,128)(2,1)}, bf16[4,128,128]{2,1,0:T(8,128)(2,1)}, u32[]{:S(2)}, u32[]{:S(2)}) collective-permute-start(bf16[4,128,128]{2,1,0:T(8,128)(2,1)} %collective-permute-done.5.refs_4_.refs_8_), channel_id=1, source_target_pairs={{0,4},{4,0},{8,12},{12,8},{16,20},{20,16},{24,28},{28,24},{1,5},{5... | collective-permute-start | bytes 393224 | tf_op jit(solution)/shard_map/ppermute | solution.py:203
  52.9 0.8 collective-permute-start.6
  53.7 2.6 %collective-permute-done.8.refs_6_.refs_10_ = bf16[4,128,128]{2,1,0:T(8,128)(2,1)S(1)} collective-permute-done((bf16[4,128,128]{2,1,0:T(8,128)(2,1)}, bf16[4,128,128]{2,1,0:T(8,128)(2,1)S(1)}, u32[]{:S(2)}, u32[]{:S(2)}) %collective-permute-start.8) | collective-permute-done | bytes 131104 | tf_op jit(solution)/shard_map/ppermute | solution.py:203
  56.3 0.7 copy-done.1
  56.9 1.7 %collective-permute-start.9 = (bf16[4,128,128]{2,1,0:T(8,128)(2,1)S(1)}, bf16[4,128,128]{2,1,0:T(8,128)(2,1)}, u32[]{:S(2)}, u32[]{:S(2)}) collective-permute-start(bf16[4,128,128]{2,1,0:T(8,128)(2,1)S(1)} %collective-permute-done.8.refs_6_.refs_10_), channel_id=1, source_target_pairs={{0,4},{4,0},{8,12},{12,8},{16,20},{20,16},{24,28},{28,24},{1,5},{5... | collective-permute-start | bytes 393224 | tf_op jit(solution)/shard_map/ppermute | solution.py:203
  58.6 0.9 %collective-permute-done.6.refs_3_.refs_7_ = bf16[4,128,128]{2,1,0:T(8,128)(2,1)} collective-permute-done((bf16[4,128,128]{2,1,0:T(8,128)(2,1)}, bf16[4,128,128]{2,1,0:T(8,128)(2,1)}, u32[]{:S(2)}, u32[]{:S(2)}) %collective-permute-start.6) | collective-permute-done | bytes 131104 | tf_op jit(solution)/shard_map/ppermute | solution.py:203
  59.6 2.4 %collective-permute-done.9.refs_7_.refs_11_ = bf16[4,128,128]{2,1,0:T(8,128)(2,1)} collective-permute-done((bf16[4,128,128]{2,1,0:T(8,128)(2,1)S(1)}, bf16[4,128,128]{2,1,0:T(8,128)(2,1)}, u32[]{:S(2)}, u32[]{:S(2)}) %collective-permute-start.9) | collective-permute-done | bytes 131104 | tf_op jit(solution)/shard_map/ppermute | solution.py:203
  62.0 4.4 %all-to-all-start.2 = ((bf16[8,272,128]{2,1,0:T(8,128)(2,1)}), bf16[8,272,128]{2,1,0:T(8,128)(2,1)}, u32[]{:S(2)}, u32[]{:S(2)}) async-start(bf16[8,272,128]{2,1,0:T(8,128)(2,1)} %backward.1), calls=%async_computation.2 | async-start | bytes 1114112 | tf_op jit(solution)/shard_map/all_to_all | solution.py:698
  66.4 1.7 %slice.16.refs_0_ = bf16[8,128,128]{2,1,0:T(8,128)(2,1)} slice(bf16[8,192,128]{2,1,0:T(8,128)(2,1)} %all-to-all-done.moved_hbm), slice={[0:8], [64:192], [0:128]} | slice | bytes 524288 | tf_op jit(solution)/shard_map/slice | solution.py:694
  68.1 1.5 %collective-permute-start.14 = (bf16[8,128,128]{2,1,0:T(8,128)(2,1)}, bf16[8,128,128]{2,1,0:T(8,128)(2,1)}, u32[]{:S(2)}, u32[]{:S(2)}) collective-permute-start(bf16[8,128,128]{2,1,0:T(8,128)(2,1)} %slice.16.refs_0_), channel_id=1, source_target_pairs={{0,2},{1,3},{2,0},{3,1},{4,6},{5,7},{6,4},{7,5},{8,10},{9,11},{10,... | collective-permute-start | bytes 786440 | tf_op jit(solution)/shard_map/ppermute | solution.py:203
  69.6 4.8 %project.1 = (f32[128,1024]{1,0:T(8,128)}, bf16[128,1024]{1,0:T(8,128)(2,1)}, bf16[128,1024]{1,0:T(8,128)(2,1)}, bf16[128,1024]{1,0:T(8,128)(2,1)}) custom-call(s32[2]{0:T(128)} %pad_add_fusion.ids_ref, bf16[4,128,128]{2,1,0:T(8,128)(2,1)} %get-tuple-element.52.refs_0_.refs_4_, bf16[4,128,128]{2,1,0:T(8,128)(2,1)} %collective-permute-done.3.refs_1_.refs_5_, ...), custom_call_target="tpu_custom_call" | custom-call | flops 1 | bytes 1 | tf_op jit(solution)/shard_map/project/pallas_call | solution.py:582
  74.3 0.4 collective-permute-done.14.refs_2_
  74.7 0.2 collective-permute-start.15
  74.9 0.3 collective-permute-start.10
  75.3 1.5 %collective-permute-start.11 = (bf16[128,1024]{1,0:T(8,128)(2,1)}, bf16[128,1024]{1,0:T(8,128)(2,1)}, u32[]{:S(2)}, u32[]{:S(2)}) collective-permute-start(bf16[128,1024]{1,0:T(8,128)(2,1)} %get-tuple-element.62), channel_id=1, source_target_pairs={{0,2},{1,3},{2,0},{3,1},{4,6},{5,7},{6,4},{7,5},{8,10},{9,11},{10,... | collective-permute-start | bytes 786440 | tf_op jit(solution)/shard_map/ppermute | solution.py:203
  76.7 0.0 collective-permute-start.12
  76.8 0.0 collective-permute-done.13.refs_1_
  76.8 0.0 collective-permute-done.15.refs_3_
  76.8 5.9 %grad_weight.1 = f32[512,512]{1,0:T(8,128)} custom-call(s32[2]{0:T(128)} %pad_add_fusion.ids_ref, bf16[8,128,128]{2,1,0:T(8,128)(2,1)} %slice.16.refs_0_, bf16[8,128,128]{2,1,0:T(8,128)(2,1)} %collective-permute-done.13.refs_1_, bf16[8,128,128]{2,1,0:T(8,128)(2,1)} %collective-permute-done.14.refs_2_, bf16[8,128,128]{2,1,0:T(8,128)(2,1)} %collective-permute-done.15.refs_3_, ...), custom_call_target="tpu_custom_call" | custom-call | flops 1 | bytes 1 | tf_op jit(solution)/shard_map/grad_weight/pallas_call | solution.py:582
  82.7 2.8 %unpack.1 = (f32[128,512]{1,0:T(8,128)}, f32[128,512]{1,0:T(8,128)}, f32[128,512]{1,0:T(8,128)}, f32[128,512]{1,0:T(8,128)}, f32[3,3,512]{2,1,0:T(4,128)}, /*index=5*/f32[1,512]{1,0:T(1,128)}) custom-call(bf16[8,272,128]{2,1,0:T(8,128)(2,1)} %all-to-all-done.2.moved_hbm), custom_call_target="tpu_custom_call" | custom-call | flops 1 | bytes 1 | tf_op jit(solution)/shard_map/unpack/pallas_call | solution.py:582
  85.6 3.2 %collective-permute-done.12 = bf16[128,1024]{1,0:T(8,128)(2,1)} collective-permute-done((bf16[128,1024]{1,0:T(8,128)(2,1)}, bf16[128,1024]{1,0:T(8,128)(2,1)}, u32[]{:S(2)}, u32[]{:S(2)}) %collective-permute-start.12) | collective-permute-done | bytes 262176 | tf_op jit(solution)/shard_map/ppermute | solution.py:203
  88.8 2.1 %add_convert_fusion = bf16[128,1024]{1,0:T(8,128)(2,1)} fusion(bf16[128,1024]{1,0:T(8,128)(2,1)} %collective-permute-done.12, bf16[128,1024]{1,0:T(8,128)(2,1)} %collective-permute-done.11, f32[128,1024]{1,0:T(8,128)} %get-tuple-element.60, bf16[128,1024]{1,0:T(8,128)(2,1)} %collective-permute-done.10), kind=kLoop, calls=%fused_computation | loop fusion | flops 917504 | bytes 1572864 | tf_op jit(solution)/shard_map/convert_element_type | solution.py:743
  (13 shorter events, 0.0 us)
Async XLA Ops:
  0.6 18.2 %copy-start = (f32[512]{0:T(512)S(1)}, f32[512]{0:T(512)}, u32[]{:S(2)}) copy-start(f32[512]{0:T(512)} %param.15) | copy-start | bytes 6148
  2.8 23.2 %all-to-all-start.1 = ((bf16[8,2,128,128]{3,2,1,0:T(8,128)(2,1)}), bf16[8,2,128,128]{3,2,1,0:T(8,128)(2,1)}, u32[]{:S(2)}, u32[]{:S(2)}) async-start(bf16[8,2,128,128]{3,2,1,0:T(8,128)(2,1)} %pack_streams.1), calls=%async_computation.1 | async-start | bytes 1048576 | tf_op jit(solution)/shard_map/all_to_all | solution.py:650
  10.1 8.0 %collective-permute-start.1 = (bf16[128,1024]{1,0:T(8,128)(2,1)}, bf16[128,1024]{1,0:T(8,128)(2,1)S(1)}, u32[]{:S(2)}, u32[]{:S(2)}) collective-permute-start(bf16[128,1024]{1,0:T(8,128)(2,1)} %c0_hbm.1), channel_id=1, source_target_pairs={{0,2},{1,3},{2,0},{3,1},{4,6},{5,7},{6,4},{7,5},{8,10},{9,11},{10,... | collective-permute-start | bytes 786440 | tf_op jit(solution)/shard_map/ppermute | solution.py:203
  11.6 8.8 %collective-permute-start = (bf16[128,1024]{1,0:T(8,128)(2,1)}, bf16[128,1024]{1,0:T(8,128)(2,1)}, u32[]{:S(2)}, u32[]{:S(2)}) collective-permute-start(bf16[128,1024]{1,0:T(8,128)(2,1)} %c0_hbm.1), channel_id=1, source_target_pairs={{0,1},{1,0},{2,3},{3,2},{4,5},{5,4},{6,7},{7,6},{8,9},{9,8},{10,11... | collective-permute-start | bytes 786440 | tf_op jit(solution)/shard_map/ppermute | solution.py:203
  18.1 0.7 copy-start.2
  18.8 1.7 %collective-permute-start.2 = (bf16[128,1024]{1,0:T(8,128)(2,1)S(1)}, bf16[128,1024]{1,0:T(8,128)(2,1)}, u32[]{:S(2)}, u32[]{:S(2)}) collective-permute-start(bf16[128,1024]{1,0:T(8,128)(2,1)S(1)} %collective-permute-done.1.c2_hbm), channel_id=1, source_target_pairs={{0,1},{1,0},{2,3},{3,2},{4,5},{5,4},{6,7},{7,6},{8,9},{9,8},{10,11... | collective-permute-start | bytes 786440 | tf_op jit(solution)/shard_map/ppermute | solution.py:203
  26.0 18.7 %all-to-all-start = ((bf16[8,192,128]{2,1,0:T(8,128)(2,1)}), bf16[8,192,128]{2,1,0:T(8,128)(2,1)}, u32[]{:S(2)}, u32[]{:S(2)}) async-start(bf16[8,192,128]{2,1,0:T(8,128)(2,1)} %grad_gated.1.after_hbm), calls=%async_computation | async-start | bytes 786432 | tf_op jit(solution)/shard_map/all_to_all | solution.py:663
  36.9 14.1 %collective-permute-start.3 = (bf16[4,128,128]{2,1,0:T(8,128)(2,1)}, bf16[4,128,128]{2,1,0:T(8,128)(2,1)}, u32[]{:S(2)}, u32[]{:S(2)}) collective-permute-start(bf16[4,128,128]{2,1,0:T(8,128)(2,1)} %get-tuple-element.52.refs_0_.refs_4_), channel_id=1, source_target_pairs={{0,4},{4,0},{8,12},{12,8},{16,20},{20,16},{24,28},{28,24},{1,5},{5... | collective-permute-start | bytes 393224 | tf_op jit(solution)/shard_map/ppermute | solution.py:203
  39.0 12.0 %collective-permute-start.4 = (bf16[4,128,128]{2,1,0:T(8,128)(2,1)}, bf16[4,128,128]{2,1,0:T(8,128)(2,1)}, u32[]{:S(2)}, u32[]{:S(2)}) collective-permute-start(bf16[4,128,128]{2,1,0:T(8,128)(2,1)} %get-tuple-element.52.refs_0_.refs_4_), channel_id=1, source_target_pairs={{0,8},{4,12},{8,0},{12,4},{16,24},{20,28},{24,16},{28,20},{1,9},{5... | collective-permute-start | bytes 393224 | tf_op jit(solution)/shard_map/ppermute | solution.py:203
  40.5 10.6 %collective-permute-start.5 = (bf16[4,128,128]{2,1,0:T(8,128)(2,1)}, bf16[4,128,128]{2,1,0:T(8,128)(2,1)}, u32[]{:S(2)}, u32[]{:S(2)}) collective-permute-start(bf16[4,128,128]{2,1,0:T(8,128)(2,1)} %get-tuple-element.52.refs_0_.refs_4_), channel_id=1, source_target_pairs={{0,16},{4,20},{8,24},{12,28},{16,0},{20,4},{24,8},{28,12},{1,17},{... | collective-permute-start | bytes 393224 | tf_op jit(solution)/shard_map/ppermute | solution.py:203
  51.0 5.2 %collective-permute-start.8 = (bf16[4,128,128]{2,1,0:T(8,128)(2,1)}, bf16[4,128,128]{2,1,0:T(8,128)(2,1)S(1)}, u32[]{:S(2)}, u32[]{:S(2)}) collective-permute-start(bf16[4,128,128]{2,1,0:T(8,128)(2,1)} %collective-permute-done.5.refs_4_.refs_8_), channel_id=1, source_target_pairs={{0,8},{4,12},{8,0},{12,4},{16,24},{20,28},{24,16},{28,20},{1,9},{5... | collective-permute-start | bytes 393224 | tf_op jit(solution)/shard_map/ppermute | solution.py:203
  51.7 7.9 %collective-permute-start.7 = (bf16[4,128,128]{2,1,0:T(8,128)(2,1)}, bf16[4,128,128]{2,1,0:T(8,128)(2,1)}, u32[]{:S(2)}, u32[]{:S(2)}) collective-permute-start(bf16[4,128,128]{2,1,0:T(8,128)(2,1)} %collective-permute-done.5.refs_4_.refs_8_), channel_id=1, source_target_pairs={{0,4},{4,0},{8,12},{12,8},{16,20},{20,16},{24,28},{28,24},{1,5},{5... | collective-permute-start | bytes 393224 | tf_op jit(solution)/shard_map/ppermute | solution.py:203
  52.9 6.7 %collective-permute-start.6 = (bf16[4,128,128]{2,1,0:T(8,128)(2,1)}, bf16[4,128,128]{2,1,0:T(8,128)(2,1)}, u32[]{:S(2)}, u32[]{:S(2)}) collective-permute-start(bf16[4,128,128]{2,1,0:T(8,128)(2,1)} %collective-permute-done.4.refs_2_.refs_6_), channel_id=1, source_target_pairs={{0,4},{4,0},{8,12},{12,8},{16,20},{20,16},{24,28},{28,24},{1,5},{5... | collective-permute-start | bytes 393224 | tf_op jit(solution)/shard_map/ppermute | solution.py:203
  56.3 0.7 copy-start.1
  56.9 5.1 %collective-permute-start.9 = (bf16[4,128,128]{2,1,0:T(8,128)(2,1)S(1)}, bf16[4,128,128]{2,1,0:T(8,128)(2,1)}, u32[]{:S(2)}, u32[]{:S(2)}) collective-permute-start(bf16[4,128,128]{2,1,0:T(8,128)(2,1)S(1)} %collective-permute-done.8.refs_6_.refs_10_), channel_id=1, source_target_pairs={{0,4},{4,0},{8,12},{12,8},{16,20},{20,16},{24,28},{28,24},{1,5},{5... | collective-permute-start | bytes 393224 | tf_op jit(solution)/shard_map/ppermute | solution.py:203
  62.0 20.7 %all-to-all-start.2 = ((bf16[8,272,128]{2,1,0:T(8,128)(2,1)}), bf16[8,272,128]{2,1,0:T(8,128)(2,1)}, u32[]{:S(2)}, u32[]{:S(2)}) async-start(bf16[8,272,128]{2,1,0:T(8,128)(2,1)} %backward.1), calls=%async_computation.2 | async-start | bytes 1114112 | tf_op jit(solution)/shard_map/all_to_all | solution.py:698
  68.1 6.7 %collective-permute-start.14 = (bf16[8,128,128]{2,1,0:T(8,128)(2,1)}, bf16[8,128,128]{2,1,0:T(8,128)(2,1)}, u32[]{:S(2)}, u32[]{:S(2)}) collective-permute-start(bf16[8,128,128]{2,1,0:T(8,128)(2,1)} %slice.16.refs_0_), channel_id=1, source_target_pairs={{0,2},{1,3},{2,0},{3,1},{4,6},{5,7},{6,4},{7,5},{8,10},{9,11},{10,... | collective-permute-start | bytes 786440 | tf_op jit(solution)/shard_map/ppermute | solution.py:203
  69.5 7.2 %collective-permute-start.13 = (bf16[8,128,128]{2,1,0:T(8,128)(2,1)}, bf16[8,128,128]{2,1,0:T(8,128)(2,1)}, u32[]{:S(2)}, u32[]{:S(2)}) collective-permute-start(bf16[8,128,128]{2,1,0:T(8,128)(2,1)} %slice.16.refs_0_), channel_id=1, source_target_pairs={{0,1},{1,0},{2,3},{3,2},{4,5},{5,4},{6,7},{7,6},{8,9},{9,8},{10,11... | collective-permute-start | bytes 786440 | tf_op jit(solution)/shard_map/ppermute | solution.py:203
  74.7 2.1 %collective-permute-start.15 = (bf16[8,128,128]{2,1,0:T(8,128)(2,1)}, bf16[8,128,128]{2,1,0:T(8,128)(2,1)}, u32[]{:S(2)}, u32[]{:S(2)}) collective-permute-start(bf16[8,128,128]{2,1,0:T(8,128)(2,1)} %collective-permute-done.14.refs_2_), channel_id=1, source_target_pairs={{0,1},{1,0},{2,3},{3,2},{4,5},{5,4},{6,7},{7,6},{8,9},{9,8},{10,11... | collective-permute-start | bytes 786440 | tf_op jit(solution)/shard_map/ppermute | solution.py:203
  74.9 10.7 %collective-permute-start.10 = (bf16[128,1024]{1,0:T(8,128)(2,1)}, bf16[128,1024]{1,0:T(8,128)(2,1)}, u32[]{:S(2)}, u32[]{:S(2)}) collective-permute-start(bf16[128,1024]{1,0:T(8,128)(2,1)} %get-tuple-element.61), channel_id=1, source_target_pairs={{0,1},{1,0},{2,3},{3,2},{4,5},{5,4},{6,7},{7,6},{8,9},{9,8},{10,11... | collective-permute-start | bytes 786440 | tf_op jit(solution)/shard_map/ppermute | solution.py:203
  75.3 10.3 %collective-permute-start.11 = (bf16[128,1024]{1,0:T(8,128)(2,1)}, bf16[128,1024]{1,0:T(8,128)(2,1)}, u32[]{:S(2)}, u32[]{:S(2)}) collective-permute-start(bf16[128,1024]{1,0:T(8,128)(2,1)} %get-tuple-element.62), channel_id=1, source_target_pairs={{0,2},{1,3},{2,0},{3,1},{4,6},{5,7},{6,4},{7,5},{8,10},{9,11},{10,... | collective-permute-start | bytes 786440 | tf_op jit(solution)/shard_map/ppermute | solution.py:203
  76.7 12.1 %collective-permute-start.12 = (bf16[128,1024]{1,0:T(8,128)(2,1)}, bf16[128,1024]{1,0:T(8,128)(2,1)}, u32[]{:S(2)}, u32[]{:S(2)}) collective-permute-start(bf16[128,1024]{1,0:T(8,128)(2,1)} %get-tuple-element.63), channel_id=1, source_target_pairs={{0,3},{1,2},{2,1},{3,0},{4,7},{5,6},{6,5},{7,4},{8,11},{9,10},{10,... | collective-permute-start | bytes 786440 | tf_op jit(solution)/shard_map/ppermute | solution.py:203

commit v2 on v1

--- a/solution.py
+++ b/solution.py
@@ -193,7 +193,7 @@
 
 LANES = 128
 HALF = 64
-LIMIT = 64 * 2**20 - 2**17
+LIMIT = 63 * 2**20 + 2**19
 F32 = jnp.float32
 BF16 = jnp.bfloat16
 
@@ -395,38 +395,38 @@
 
 
 def project_kernel(ids_ref, *refs):
-    gates = refs[:8]
-    w_hbm, keep_hbm, *send_hbm = refs[8:13]
-    gate_ref, w_ref, keep_ref, *send_ref = refs[13:19]
-    gated_ref, gate_sems, sems = refs[19:]
+    gates = refs[:16]
+    w_hbm, other_hbm, keep_hbm, away_hbm = refs[16:20]
+    gate_ref, w_ref, keep_ref, away_ref, gated_ref, gate_sems, sems = refs[20:]
     own_row, mine = ids_ref[0], ids_ref[1]
     loads = fetch(
         [(gate.at[own_row // 2], gate_ref.at[at]) for at, gate in enumerate(gates)], gate_sems
     )
-    order = (2, 3, 1, 0)
-    copies = column_parts(w_hbm, w_ref, order, mine, sems)
+    width = keep_ref.shape[1]
+    copies = []
+    for n, (hbm, mask) in enumerate(((w_hbm, 2), (other_hbm, 2), (w_hbm, 0), (other_hbm, 0))):
+        at = pl.multiple_of((mine ^ mask) * width, width)
+        copies += fetch(((hbm.at[:, pl.ds(at, width)], w_ref.at[n]),), sems.at[pl.ds(n, 1)])
     left = left_lanes(gate_ref.shape[1])
     odd = own_row % 2 == 1
-    finish(loads)
-    for pair in range(len(gates) // 2):
-        one = gate_ref[2 * pair].astype(F32)
-        two = gate_ref[2 * pair + 1].astype(F32)
-        even_rows = jnp.where(left, one, other_half(two))
-        odd_rows = jnp.where(left, other_half(two), one)
-        lanes = pl.ds(pl.multiple_of(((own_row // 2) ^ pair) * LANES, LANES), LANES)
-        gated_ref[:, lanes] = jnp.where(odd, odd_rows, even_rows).astype(BF16)
-    gated = gated_ref[...]
+    for side in range(2):
+        finish(loads[8 * side : 8 * side + 8])
+        for pair in range(4):
+            one = gate_ref[8 * side + 2 * pair].astype(F32)
+            two = gate_ref[8 * side + 2 * pair + 1].astype(F32)
+            even_rows = jnp.where(left, one, other_half(two))
+            odd_rows = jnp.where(left, other_half(two), one)
+            lanes = pl.ds(pl.multiple_of(((own_row // 2) ^ pair) * LANES, LANES), LANES)
+            gated_ref[side, :, lanes] = jnp.where(odd, odd_rows, even_rows).astype(BF16)
     done = []
-    for n, mask in enumerate(order):
-        copies[n].wait()
-        part = jnp.dot(gated, w_ref[n], preferred_element_type=F32)
-        if mask:
-            send_ref[mask - 1][...] = part.astype(BF16)
-            target = (send_ref[mask - 1], send_hbm[mask - 1])
-        else:
-            keep_ref[...] = part
-            target = (keep_ref, keep_hbm)
-        done += fetch((target,), gate_sems.at[pl.ds(n, 1)])
+    for n, (out_ref, out_hbm) in enumerate(((away_ref, away_hbm), (keep_ref, keep_hbm))):
+        total = None
+        for side in range(2):
+            copies[2 * n + side].wait()
+            part = jnp.dot(gated_ref[side], w_ref[2 * n + side], preferred_element_type=F32)
+            total = part if total is None else total + part
+        out_ref[...] = total.astype(out_ref.dtype)
+        done += fetch(((out_ref, out_hbm),), gate_sems.at[pl.ds(n, 1)])
     finish(done)
 
 
@@ -535,9 +535,12 @@
     cots, gates = refs[:4], refs[4:12]
     out_hbm, cot_ref, gate_ref, side_ref, total_ref, sems, out_sems = refs[12:]
     own_row, own = ids_ref[0], ids_ref[1]
+    lanes = [pl.ds(LANES * half, LANES) for half in range(2)]
     copies = fetch(
         [(cot, cot_ref.at[at]) for at, cot in enumerate(cots)]
-        + [(gate, gate_ref.at[at]) for at, gate in enumerate(gates)],
+        + [
+            (gate, gate_ref.at[at // 2, :, :, lanes[at % 2]]) for at, gate in enumerate(gates)
+        ],
         sems,
     )
     _, peers, high, wide = cot_ref.shape
@@ -546,30 +549,24 @@
     for mask in range(4):
         copies[mask].wait()
         for peer in range(peers):
-            lanes = slice(wide * (peer // 2), wide * (peer // 2) + wide)
-            side_ref[peer % 2, high * mask : high * mask + high, lanes] = cot_ref[mask, peer]
+            at = slice(wide * (peer // 2), wide * (peer // 2) + wide)
+            side_ref[peer % 2, high * mask : high * mask + high, at] = cot_ref[mask, peer]
     done = []
     for pair in range(peers // 2):
         finish(copies[4 + 2 * pair : 6 + 2 * pair])
-        found = []
-        for at in (2 * pair, 2 * pair + 1):
-            gate = gate_ref[at].reshape(peers // 2 * wide, LANES)
-            found.append(
-                [jnp.dot(side_ref[n], gate, preferred_element_type=F32) for n in range(2)]
-            )
-        (even_low, even_high), (odd_low, odd_high) = found
-        even_sum = even_low + other_half(even_high)
-        odd_sum = odd_low + other_half(odd_high)
+        gate = gate_ref[pair].reshape(peers // 2 * wide, 2 * LANES)
+        low = jnp.dot(side_ref[0], gate, preferred_element_type=F32)
+        high_part = jnp.dot(side_ref[1], gate, preferred_element_type=F32)
+        even_sum = low[:, :LANES] + other_half(high_part[:, :LANES])
+        odd_sum = low[:, LANES:] + other_half(high_part[:, LANES:])
         ahead = jnp.where(left, even_sum, other_half(odd_sum))
         behind = jnp.where(left, odd_sum, other_half(even_sum))
         tile = jnp.where(odd, behind, ahead)
         for mask in range(4):
             at = pl.ds(pl.multiple_of((own ^ mask) * high, high), high)
             total_ref[pair, at] = tile[high * mask : high * mask + high]
-        lanes = pl.ds(pl.multiple_of(((own_row // 2) ^ pair) * LANES, LANES), LANES)
-        done += fetch(
-            ((total_ref.at[pair], out_hbm.at[:, lanes]),), out_sems.at[pl.ds(pair, 1)]
-        )
+        to = pl.ds(pl.multiple_of(((own_row // 2) ^ pair) * LANES, LANES), LANES)
+        done += fetch(((total_ref.at[pair], out_hbm.at[:, to]),), out_sems.at[pl.ds(pair, 1)])
     finish(done)
 
 
@@ -604,22 +601,6 @@
     return [block, near, far, swap_bits(far, axis, 1)]
 
 
-def gathered_first(block, axis):
-    mask = lax.axis_size(axis) // 2
-    return {0: block, mask: swap_bits(block, axis, mask), mask // 2: swap_bits(block, axis, mask // 2), 1: swap_bits(block, axis, 1)}
-
-
-def gathered_rest(blocks, axis):
-    top = lax.axis_size(axis) // 2
-    mask = top // 2
-    while mask:
-        for at in list(blocks):
-            if at % (2 * mask) == 0 and at | mask not in blocks:
-                blocks[at | mask] = swap_bits(blocks[at], axis, mask)
-        mask //= 2
-    return [blocks[at] for at in range(len(blocks))]
-
-
 def on_device_packed(
     query_proj, key_proj, value_proj, short_filter, long_filter, skip_gain, out_weight, cotangent
 ):
@@ -661,6 +642,8 @@
         dmas=(4, 4),
     )
     moved_grad = lax.all_to_all(sent_grad, "seq", 0, 0, tiled=True)
+    other_weight = swap_bits(out_weight, "ch", 1)
+    moved_grad, other_weight = lax.optimization_barrier((moved_grad, other_weight))
     wide = shaped((size, LANES), F32)
     spectra = shaped((4, size // 2, LANES), F32)
     folds = shaped((peers // 2, rows, LANES), BF16)
@@ -677,7 +660,7 @@
         scratch=(packs, *tables, *results, wide, wide),
         dmas=(3, 5),
     )
-    first_gates = gathered_first(gated, "seq")
+    blocks = {0: gated} | {mask: swap_bits(gated, "seq", mask) for mask in (4, 2, 1)}
     backs = shaped((peers, 2 * rows + 16, LANES), BF16)
     saved = (mq, spec, kqs, vhs, streams, *tables)
     (back,) = call(
@@ -691,27 +674,37 @@
             shaped((peers, rows // 2, LANES), BF16), *saved, backs, wide, spectra, wide
         ),
     )
-    cot_parts = gathered_pairs(moved_grad[:, rows // 2 :], "ch")
-    back, first_gates = lax.optimization_barrier((back, first_gates))
-    gates = gathered_rest(first_gates, "seq")
-    back, gates = lax.optimization_barrier((back, gates))
+    back, blocks = lax.optimization_barrier((back, blocks))
+    blocks[6] = swap_bits(blocks[4], "seq", 2)
+    blocks[3], blocks[5] = swap_bits(blocks[2], "seq", 1), swap_bits(blocks[4], "seq", 1)
+    cot_rows = moved_grad[:, rows // 2 :]
+    blocks[6], cot_rows = lax.optimization_barrier((blocks[6], cot_rows))
+    blocks[7] = swap_bits(blocks[6], "seq", 1)
+    gates = [blocks[at] for at in range(8)]
+    near, far = swap_bits(cot_rows, "ch", 1), swap_bits(cot_rows, "ch", 2)
+    other_gates = [swap_bits(block, "ch", 1) for block in gates]
+    back, gates, other_gates[:7] = lax.optimization_barrier((back, gates, other_gates[:7]))
     returned = lax.all_to_all(back, "seq", 0, 0, tiled=True)
-    sums = [shaped((rows, features), F32)] + [shaped((rows, features), BF16)] * 3
-    keep, *away = call(
+    sums = [shaped((rows, features), F32), shaped((rows, features), BF16)]
+    keep, away = call(
         project_kernel,
         sums,
         [ids],
         *gates,
+        *other_gates,
         out_weight,
+        other_weight,
         scratch=(
-            shaped((peers, rows, LANES), BF16),
+            shaped((2 * peers, rows, LANES), BF16),
             weight_room,
             *sums,
-            shaped((rows, channels), BF16),
+            shaped((2, rows, channels), BF16),
         ),
-        dmas=(8, 4),
-    )
-    shares = [swap_bits(part, "ch", mask) for mask, part in enumerate(away, 1)]
+        dmas=(16, 4),
+    )
+    share = swap_bits(away, "ch", 2)
+    far, near, away = lax.optimization_barrier((far, near, away))
+    cot_parts = [cot_rows, near, far, swap_bits(far, "ch", 1)]
     plain = shaped((rows, channels), F32)
     grad_query, grad_key, grad_value, grad_filter, grad_short, grad_skip = call(
         unpack_kernel,
@@ -729,18 +722,16 @@
         *gates,
         scratch=(
             shaped((4, peers, LANES, rows), BF16),
-            shaped((peers, peers // 2, rows, LANES), BF16),
+            shaped((peers // 2, peers // 2, rows, 2 * LANES), BF16),
             shaped((2, 4 * LANES, peers // 2 * rows), BF16),
             shaped((peers // 2, 4 * LANES, LANES), F32),
         ),
         dmas=(12, 4),
     )
-    shares, grad_w_out_t, grad_filter = lax.optimization_barrier(
-        (shares, grad_w_out_t, grad_filter)
-    )
-    for part in shares:
-        keep = keep + part.astype(F32)
-    layer_out = keep.astype(BF16)
+    share, grad_w_out_t, grad_filter = lax.optimization_barrier(
+        (share, grad_w_out_t, grad_filter)
+    )
+    layer_out = (keep + share.astype(F32)).astype(BF16)
     return (
         layer_out,
         grad_query,

time: 91.8 us -> 89.9 us (0.979)
  waiting for transfers between devices: 17.3 us -> 16.1 us
  local copies, waits for them, and re-layouts: 4.18 us -> 3 us
  starting transfers between devices: 32.7 us -> 33.7 us
    ppermute x16 -> x23, starting transfers between devices: 15.3 us -> 16.5 us  [swap_bits(): return lax.ppermute(shard, axis, [(i, i ^ mask) for i in range(size)])]
    ppermute x16 -> x23, waiting for transfers between devices: 15.4 us -> 14.3 us  [swap_bits(): return lax.ppermute(shard, axis, [(i, i ^ mask) for i in range(size)])]
  transfers between devices with their start and end apart: 19 -> 26, of which waited for: 7 -> 7; matrix products, arithmetic and copies ran while one was open for 4% -> 4% of each run, Pallas kernels for 34% -> 36%
where the time goes in v2:
time: 89.9 us; the launch traced here: 89.2 us
  starting transfers between devices  33.7 us (37%)
  Pallas kernels  32.3 us (36%)
  waiting for transfers between devices  16.1 us (18%)
  other arithmetic  3.13 us (3%)
  local copies, waits for them, and re-layouts  3 us (3%)
  between operations  0.93 us (1%)
    pallas_call x7, Pallas kernels, call(): pl.pallas_call(kernel, out_shape=list(outs) + list(small_outs), in_specs=...  32.3 us
    ppermute x23, starting transfers between devices, swap_bits(): return lax.ppermute(shard, axis, [(i, i ^ mask) for i in range(size)])  16.5 us
    ppermute x23, waiting for transfers between devices, swap_bits(): return lax.ppermute(shard, axis, [(i, i ^ mask) for i in range(size)])  14.3 us
    all_to_all x1, starting transfers between devices, on_device_packed(): streams = lax.all_to_all(packed, 'seq', 0, 0, tiled=True)  6.86 us
    all_to_all x1, starting transfers between devices, on_device_packed(): moved_grad = lax.all_to_all(sent_grad, 'seq', 0, 0, tiled=True)  5.73 us
    all_to_all x1, starting transfers between devices, on_device_packed(): returned = lax.all_to_all(back, 'seq', 0, 0, tiled=True)  4.52 us
    all_to_all x1, waiting for transfers between devices, on_device_packed(): moved_grad = lax.all_to_all(sent_grad, 'seq', 0, 0, tiled=True)  1.85 us
    convert_element_type x1, other arithmetic, on_device_packed(): layer_out = (keep + share.astype(F32)).astype(BF16)  1.81 us
  transfers between devices with their start and end apart: 26, of which 7 were waited for; matrix products, arithmetic and copies ran while one was open for 4% of the time, Pallas kernels for 36%

profile of v2, /device:TPU:0, one launch (start us, length us, event | category | flops | bytes accessed | tf_op | source)
XLA Modules:
  0.0 89.2 jit_solution(2078543382140470046)
XLA Ops:
  0.6 0.0 copy-start
  0.6 0.5 collective-permute-start.3
  1.2 2.1 %pack_streams.1 = bf16[8,2,128,128]{3,2,1,0:T(8,128)(2,1)} custom-call(bf16[128,512]{1,0:T(8,128)(2,1)} %q_hbm.1, bf16[128,512]{1,0:T(8,128)(2,1)} %k_hbm.1, bf16[128,512]{1,0:T(8,128)(2,1)} %v_hbm.1, f32[128,512]{1,0:T(8,128)} %h_hbm.1), custom_call_target="tpu_custom_call" | custom-call | flops 1 | bytes 1 | tf_op jit(solution)/shard_map/pack_streams/pallas_call | solution.py:579
  3.3 6.9 %all-to-all-start.1 = ((bf16[8,2,128,128]{3,2,1,0:T(8,128)(2,1)}), bf16[8,2,128,128]{3,2,1,0:T(8,128)(2,1)}, u32[]{:S(2)}, u32[]{:S(2)}) async-start(bf16[8,2,128,128]{3,2,1,0:T(8,128)(2,1)} %pack_streams.1), calls=%async_computation.1 | async-start | bytes 1048576 | tf_op jit(solution)/shard_map/all_to_all | solution.py:631
  10.2 1.5 %collective-permute-start.1 = (bf16[128,1024]{1,0:T(8,128)(2,1)}, bf16[128,1024]{1,0:T(8,128)(2,1)S(1)}, u32[]{:S(2)}, u32[]{:S(2)}) collective-permute-start(bf16[128,1024]{1,0:T(8,128)(2,1)} %c0_hbm.1), channel_id=1, source_target_pairs={{0,2},{1,3},{2,0},{3,1},{4,6},{5,7},{6,4},{7,5},{8,10},{9,11},{10,... | collective-permute-start | bytes 786440 | tf_op jit(solution)/shard_map/ppermute | solution.py:203
  11.7 0.8 dynamic-slice_bitcast_fusion.2
  12.5 6.3 %collective-permute-done.1.c2_hbm = bf16[128,1024]{1,0:T(8,128)(2,1)S(1)} collective-permute-done((bf16[128,1024]{1,0:T(8,128)(2,1)}, bf16[128,1024]{1,0:T(8,128)(2,1)S(1)}, u32[]{:S(2)}, u32[]{:S(2)}) %collective-permute-start.1) | collective-permute-done | bytes 262176 | tf_op jit(solution)/shard_map/ppermute | solution.py:203
  18.8 0.0 collective-permute-start.2
  18.8 0.1 dynamic-slice_bitcast_fusion.3
  18.9 0.1 concatenate.9
  19.0 0.1 iota.11
  19.1 0.1 concatenate.10
  19.2 0.6 pad_add_fusion.ids_ref
  19.8 0.7 pad_maximum_fusion.after_ref.prm_ref
  20.5 5.6 %grad_gated.1.after_hbm = bf16[8,192,128]{2,1,0:T(8,128)(2,1)} custom-call(s32[2]{0:T(128)} %pad_add_fusion.ids_ref, bf16[128,1024]{1,0:T(8,128)(2,1)} %c0_hbm.1, bf16[128,1024]{1,0:T(8,128)(2,1)} %collective-permute-done.c1_hbm, bf16[128,1024]{1,0:T(8,128)(2,1)} %copy-done.7, bf16[128,1024]{1,0:T(8,128)(2,1)} %collective-permute-done.2.c3_hbm, ...), custom_call_target="tpu_custom_call" | custom-call | flops 1 | bytes 1 | tf_op jit(solution)/shard_map/grad_gated/pallas_call | solution.py:579
  26.1 5.7 %all-to-all-start = ((bf16[8,192,128]{2,1,0:T(8,128)(2,1)}), bf16[8,192,128]{2,1,0:T(8,128)(2,1)S(1)}, u32[]{:S(2)}, u32[]{:S(2)}) async-start(bf16[8,192,128]{2,1,0:T(8,128)(2,1)} %grad_gated.1.after_hbm), calls=%async_computation | async-start | bytes 786432 | tf_op jit(solution)/shard_map/all_to_all | solution.py:644
  31.8 5.1 %forward.1 = (bf16[4,128,128]{2,1,0:T(8,128)(2,1)}, f32[1024,128]{1,0:T(8,128)}, f32[1024,128]{1,0:T(8,128)}, f32[1024,128]{1,0:T(8,128)}, f32[4,512,128]{2,1,0:T(8,128)}) custom-call(bf16[8,2,128,128]{3,2,1,0:T(8,128)(2,1)} %all-to-all-done.1.moved_hbm.streams_hbm, bf16[2,1024,512]{2,1,0:T(8,128)(2,1)} %constant.20.clone.fwd_hbm, ...), custom_call_target="tpu_custom_call" | custom-call | flops 1 | bytes 1 | tf_op jit(solution)/shard_map/forward/pallas_call | solution.py:579
  37.0 2.1 %collective-permute-start.4 = (bf16[4,128,128]{2,1,0:T(8,128)(2,1)}, bf16[4,128,128]{2,1,0:T(8,128)(2,1)}, u32[]{:S(2)}, u32[]{:S(2)}) collective-permute-start(bf16[4,128,128]{2,1,0:T(8,128)(2,1)} %get-tuple-element.63.refs_0_.refs_4_), channel_id=1, source_target_pairs={{0,4},{4,0},{8,12},{12,8},{16,20},{20,16},{24,28},{28,24},{1,5},{5... | collective-permute-start | bytes 393224 | tf_op jit(solution)/shard_map/ppermute | solution.py:203
  39.1 1.5 %collective-permute-start.5 = (bf16[4,128,128]{2,1,0:T(8,128)(2,1)}, bf16[4,128,128]{2,1,0:T(8,128)(2,1)}, u32[]{:S(2)}, u32[]{:S(2)}) collective-permute-start(bf16[4,128,128]{2,1,0:T(8,128)(2,1)} %get-tuple-element.63.refs_0_.refs_4_), channel_id=1, source_target_pairs={{0,8},{4,12},{8,0},{12,4},{16,24},{20,28},{24,16},{28,20},{1,9},{5... | collective-permute-start | bytes 393224 | tf_op jit(solution)/shard_map/ppermute | solution.py:203
  40.5 2.4 %collective-permute-start.6 = (bf16[4,128,128]{2,1,0:T(8,128)(2,1)}, bf16[4,128,128]{2,1,0:T(8,128)(2,1)}, u32[]{:S(2)}, u32[]{:S(2)}) collective-permute-start(bf16[4,128,128]{2,1,0:T(8,128)(2,1)} %get-tuple-element.63.refs_0_.refs_4_), channel_id=1, source_target_pairs={{0,16},{4,20},{8,24},{12,28},{16,0},{20,4},{24,8},{28,12},{1,17},{... | collective-permute-start | bytes 393224 | tf_op jit(solution)/shard_map/ppermute | solution.py:203
  42.9 1.9 %all-to-all-done.moved_hbm = bf16[8,192,128]{2,1,0:T(8,128)(2,1)S(1)} async-done(((bf16[8,192,128]{2,1,0:T(8,128)(2,1)}), bf16[8,192,128]{2,1,0:T(8,128)(2,1)S(1)}, u32[]{:S(2)}, u32[]{:S(2)}) %all-to-all-start) | async-done | bytes 393248 | tf_op jit(solution)/shard_map/all_to_all | solution.py:644
  44.8 0.8 copy-done.1
  45.5 6.2 %backward.1 = bf16[8,272,128]{2,1,0:T(8,128)(2,1)} custom-call(bf16[8,192,128]{2,1,0:T(8,128)(2,1)} %copy-done.1, f32[1024,128]{1,0:T(8,128)} %get-tuple-element.52.mq_hbm, f32[4,512,128]{2,1,0:T(8,128)} %get-tuple-element.53.spec_hbm, f32[1024,128]{1,0:T(8,128)} %get-tuple-element.54.kqs_hbm, f32[1024,128]{1,0:T(8,128)} %get-tuple-element.55.vhs_hbm, ...), custom_call_target="tpu_custom_call" | custom-call | flops 1 | bytes 1 | tf_op jit(solution)/shard_map/backward/pallas_call | solution.py:579
  51.8 0.6 collective-permute-start.9
  52.4 1.2 %collective-permute-start.7 = (bf16[4,128,128]{2,1,0:T(8,128)(2,1)}, bf16[4,128,128]{2,1,0:T(8,128)(2,1)S(1)}, u32[]{:S(2)}, u32[]{:S(2)}) collective-permute-start(bf16[4,128,128]{2,1,0:T(8,128)(2,1)} %collective-permute-done.5.refs_2_.refs_6_), channel_id=1, source_target_pairs={{0,4},{4,0},{8,12},{12,8},{16,20},{20,16},{24,28},{28,24},{1,5},{5... | collective-permute-start | bytes 393224 | tf_op jit(solution)/shard_map/ppermute | solution.py:203
  53.5 0.8 collective-permute-start.8
  54.4 0.5 collective-permute-start.12
  54.9 2.1 %collective-permute-done.9.refs_6_.refs_10_ = bf16[4,128,128]{2,1,0:T(8,128)(2,1)S(1)} collective-permute-done((bf16[4,128,128]{2,1,0:T(8,128)(2,1)}, bf16[4,128,128]{2,1,0:T(8,128)(2,1)S(1)}, u32[]{:S(2)}, u32[]{:S(2)}) %collective-permute-start.9) | collective-permute-done | bytes 131104 | tf_op jit(solution)/shard_map/ppermute | solution.py:203
  57.0 1.0 %slice.15.refs_0_ = bf16[8,128,128]{2,1,0:T(8,128)(2,1)S(1)} slice(bf16[8,192,128]{2,1,0:T(8,128)(2,1)} %copy-done.1), slice={[0:8], [64:192], [0:128]} | slice | bytes 524288 | tf_op jit(solution)/shard_map/slice | solution.py:680
  58.0 0.0 copy-start.2
  58.0 0.0 copy-start.4
  58.1 0.5 collective-permute-start.15
  58.6 0.4 collective-permute-done.8.refs_5_.refs_9_
  59.0 1.6 %collective-permute-start.10 = (bf16[4,128,128]{2,1,0:T(8,128)(2,1)S(1)}, bf16[4,128,128]{2,1,0:T(8,128)(2,1)S(1)}, u32[]{:S(2)}, u32[]{:S(2)}) collective-permute-start(bf16[4,128,128]{2,1,0:T(8,128)(2,1)S(1)} %collective-permute-done.9.refs_6_.refs_10_), channel_id=1, source_target_pairs={{0,4},{4,0},{8,12},{12,8},{16,20},{20,16},{24,28},{28,24},{1,5},{5... | collective-permute-start | bytes 393224 | tf_op jit(solution)/shard_map/ppermute | solution.py:203
  60.6 0.5 collective-permute-start.14
  61.1 0.1 collective-permute-start.16
  61.2 2.9 %collective-permute-done.10.refs_7_.refs_11_ = bf16[4,128,128]{2,1,0:T(8,128)(2,1)S(1)} collective-permute-done((bf16[4,128,128]{2,1,0:T(8,128)(2,1)S(1)}, bf16[4,128,128]{2,1,0:T(8,128)(2,1)S(1)}, u32[]{:S(2)}, u32[]{:S(2)}) %collective-permute-start.10) | collective-permute-done | bytes 131104 | tf_op jit(solution)/shard_map/ppermute | solution.py:203
  64.2 4.5 %all-to-all-start.2 = ((bf16[8,272,128]{2,1,0:T(8,128)(2,1)}), bf16[8,272,128]{2,1,0:T(8,128)(2,1)}, u32[]{:S(2)}, u32[]{:S(2)}) async-start(bf16[8,272,128]{2,1,0:T(8,128)(2,1)} %backward.1), calls=%async_computation.2 | async-start | bytes 1114112 | tf_op jit(solution)/shard_map/all_to_all | solution.py:687
  68.7 1.5 %collective-permute-start.20 = (bf16[8,128,128]{2,1,0:T(8,128)(2,1)S(1)}, bf16[8,128,128]{2,1,0:T(8,128)(2,1)}, u32[]{:S(2)}, u32[]{:S(2)}) collective-permute-start(bf16[8,128,128]{2,1,0:T(8,128)(2,1)S(1)} %slice.15.refs_0_), channel_id=1, source_target_pairs={{0,2},{1,3},{2,0},{3,1},{4,6},{5,7},{6,4},{7,5},{8,10},{9,11},{10,... | collective-permute-start | bytes 786440 | tf_op jit(solution)/shard_map/ppermute | solution.py:203
  70.2 0.5 collective-permute-start.18
  70.8 1.3 %collective-permute-done.18.refs_15_ = bf16[4,128,128]{2,1,0:T(8,128)(2,1)} collective-permute-done((bf16[4,128,128]{2,1,0:T(8,128)(2,1)S(1)}, bf16[4,128,128]{2,1,0:T(8,128)(2,1)}, u32[]{:S(2)}, u32[]{:S(2)}) %collective-permute-start.18) | collective-permute-done | bytes 131104 | tf_op jit(solution)/shard_map/ppermute | solution.py:203
  72.1 5.1 %project.1 = (f32[128,1024]{1,0:T(8,128)}, bf16[128,1024]{1,0:T(8,128)(2,1)}) custom-call(s32[2]{0:T(128)} %pad_add_fusion.ids_ref, bf16[4,128,128]{2,1,0:T(8,128)(2,1)} %get-tuple-element.63.refs_0_.refs_4_, bf16[4,128,128]{2,1,0:T(8,128)(2,1)} %collective-permute-done.4.refs_1_.refs_5_, bf16[4,128,128]{2,1,0:T(8,128)(2,1)} %collective-permute-done.5.refs_2_.refs_6_, ...), custom_call_target="tpu_custom_call" | custom-call | flops 1 | bytes 1 | tf_op jit(solution)/shard_map/project/pallas_call | solution.py:579
  77.2 0.2 collective-permute-start.22
  77.4 0.5 collective-permute-start.19
  78.0 1.2 %collective-permute-done.22.refs_3_ = bf16[8,128,128]{2,1,0:T(8,128)(2,1)} collective-permute-done((bf16[8,128,128]{2,1,0:T(8,128)(2,1)}, bf16[8,128,128]{2,1,0:T(8,128)(2,1)}, u32[]{:S(2)}, u32[]{:S(2)}) %collective-permute-start.22) | collective-permute-done | bytes 262176 | tf_op jit(solution)/shard_map/ppermute | solution.py:203
  79.2 5.4 %grad_weight.1 = f32[512,512]{1,0:T(8,128)} custom-call(s32[2]{0:T(128)} %pad_add_fusion.ids_ref, bf16[8,128,128]{2,1,0:T(8,128)(2,1)} %copy-done.2, bf16[8,128,128]{2,1,0:T(8,128)(2,1)} %collective-permute-done.21.refs_1_, bf16[8,128,128]{2,1,0:T(8,128)(2,1)} %collective-permute-done.20.refs_2_, bf16[8,128,128]{2,1,0:T(8,128)(2,1)} %collective-permute-done.22.refs_3_, ...), custom_call_target="tpu_custom_call" | custom-call | flops 1 | bytes 1 | tf_op jit(solution)/shard_map/grad_weight/pallas_call | solution.py:579
  84.5 2.8 %unpack.1 = (f32[128,512]{1,0:T(8,128)}, f32[128,512]{1,0:T(8,128)}, f32[128,512]{1,0:T(8,128)}, f32[128,512]{1,0:T(8,128)}, f32[3,3,512]{2,1,0:T(4,128)}, /*index=5*/f32[1,512]{1,0:T(1,128)}) custom-call(bf16[8,272,128]{2,1,0:T(8,128)(2,1)} %all-to-all-done.2.moved_hbm), custom_call_target="tpu_custom_call" | custom-call | flops 1 | bytes 1 | tf_op jit(solution)/shard_map/unpack/pallas_call | solution.py:579
  87.4 1.8 %add_convert_fusion = bf16[128,1024]{1,0:T(8,128)(2,1)} fusion(f32[128,1024]{1,0:T(8,128)} %get-tuple-element.79, bf16[128,1024]{1,0:T(8,128)(2,1)S(1)} %collective-permute-done.19), kind=kLoop, calls=%fused_computation | loop fusion | flops 393216 | bytes 1048576 | tf_op jit(solution)/shard_map/convert_element_type | solution.py:734
  (51 shorter events, 0.1 us)
Async XLA Ops:
  0.6 18.2 %copy-start = (f32[512]{0:T(512)S(1)}, f32[512]{0:T(512)}, u32[]{:S(2)}) copy-start(f32[512]{0:T(512)} %param.15) | copy-start | bytes 6148
  0.6 44.1 %collective-permute-start.3 = (bf16[512,4096]{1,0:T(8,128)(2,1)}, bf16[512,4096]{1,0:T(8,128)(2,1)}, u32[]{:S(2)}, u32[]{:S(2)}) collective-permute-start(bf16[512,4096]{1,0:T(8,128)(2,1)} %refs_16_.1), channel_id=1, source_target_pairs={{0,1},{1,0},{2,3},{3,2},{4,5},{5,4},{6,7},{7,6},{8,9},{9,8},{10,11... | collective-permute-start | bytes 12582920 | tf_op jit(solution)/shard_map/ppermute | solution.py:203
  3.3 22.8 %all-to-all-start.1 = ((bf16[8,2,128,128]{3,2,1,0:T(8,128)(2,1)}), bf16[8,2,128,128]{3,2,1,0:T(8,128)(2,1)}, u32[]{:S(2)}, u32[]{:S(2)}) async-start(bf16[8,2,128,128]{3,2,1,0:T(8,128)(2,1)} %pack_streams.1), calls=%async_computation.1 | async-start | bytes 1048576 | tf_op jit(solution)/shard_map/all_to_all | solution.py:631
  10.2 8.6 %collective-permute-start.1 = (bf16[128,1024]{1,0:T(8,128)(2,1)}, bf16[128,1024]{1,0:T(8,128)(2,1)S(1)}, u32[]{:S(2)}, u32[]{:S(2)}) collective-permute-start(bf16[128,1024]{1,0:T(8,128)(2,1)} %c0_hbm.1), channel_id=1, source_target_pairs={{0,2},{1,3},{2,0},{3,1},{4,6},{5,7},{6,4},{7,5},{8,10},{9,11},{10,... | collective-permute-start | bytes 786440 | tf_op jit(solution)/shard_map/ppermute | solution.py:203
  11.7 8.8 %collective-permute-start = (bf16[128,1024]{1,0:T(8,128)(2,1)}, bf16[128,1024]{1,0:T(8,128)(2,1)}, u32[]{:S(2)}, u32[]{:S(2)}) collective-permute-start(bf16[128,1024]{1,0:T(8,128)(2,1)} %c0_hbm.1), channel_id=1, source_target_pairs={{0,1},{1,0},{2,3},{3,2},{4,5},{5,4},{6,7},{7,6},{8,9},{9,8},{10,11... | collective-permute-start | bytes 786440 | tf_op jit(solution)/shard_map/ppermute | solution.py:203
  18.8 1.7 %copy-start.7 = (bf16[128,1024]{1,0:T(8,128)(2,1)}, bf16[128,1024]{1,0:T(8,128)(2,1)S(1)}, u32[]{:S(2)}) copy-start(bf16[128,1024]{1,0:T(8,128)(2,1)S(1)} %collective-permute-done.1.c2_hbm) | copy-start | bytes 786436
  18.8 1.7 %collective-permute-start.2 = (bf16[128,1024]{1,0:T(8,128)(2,1)S(1)}, bf16[128,1024]{1,0:T(8,128)(2,1)}, u32[]{:S(2)}, u32[]{:S(2)}) collective-permute-start(bf16[128,1024]{1,0:T(8,128)(2,1)S(1)} %collective-permute-done.1.c2_hbm), channel_id=1, source_target_pairs={{0,1},{1,0},{2,3},{3,2},{4,5},{5,4},{6,7},{7,6},{8,9},{9,8},{10,11... | collective-permute-start | bytes 786440 | tf_op jit(solution)/shard_map/ppermute | solution.py:203
  26.1 18.7 %all-to-all-start = ((bf16[8,192,128]{2,1,0:T(8,128)(2,1)}), bf16[8,192,128]{2,1,0:T(8,128)(2,1)S(1)}, u32[]{:S(2)}, u32[]{:S(2)}) async-start(bf16[8,192,128]{2,1,0:T(8,128)(2,1)} %grad_gated.1.after_hbm), calls=%async_computation | async-start | bytes 786432 | tf_op jit(solution)/shard_map/all_to_all | solution.py:644
  37.0 14.7 %collective-permute-start.4 = (bf16[4,128,128]{2,1,0:T(8,128)(2,1)}, bf16[4,128,128]{2,1,0:T(8,128)(2,1)}, u32[]{:S(2)}, u32[]{:S(2)}) collective-permute-start(bf16[4,128,128]{2,1,0:T(8,128)(2,1)} %get-tuple-element.63.refs_0_.refs_4_), channel_id=1, source_target_pairs={{0,4},{4,0},{8,12},{12,8},{16,20},{20,16},{24,28},{28,24},{1,5},{5... | collective-permute-start | bytes 393224 | tf_op jit(solution)/shard_map/ppermute | solution.py:203
  39.1 12.7 %collective-permute-start.5 = (bf16[4,128,128]{2,1,0:T(8,128)(2,1)}, bf16[4,128,128]{2,1,0:T(8,128)(2,1)}, u32[]{:S(2)}, u32[]{:S(2)}) collective-permute-start(bf16[4,128,128]{2,1,0:T(8,128)(2,1)} %get-tuple-element.63.refs_0_.refs_4_), channel_id=1, source_target_pairs={{0,8},{4,12},{8,0},{12,4},{16,24},{20,28},{24,16},{28,20},{1,9},{5... | collective-permute-start | bytes 393224 | tf_op jit(solution)/shard_map/ppermute | solution.py:203
  40.5 11.2 %collective-permute-start.6 = (bf16[4,128,128]{2,1,0:T(8,128)(2,1)}, bf16[4,128,128]{2,1,0:T(8,128)(2,1)}, u32[]{:S(2)}, u32[]{:S(2)}) collective-permute-start(bf16[4,128,128]{2,1,0:T(8,128)(2,1)} %get-tuple-element.63.refs_0_.refs_4_), channel_id=1, source_target_pairs={{0,16},{4,20},{8,24},{12,28},{16,0},{20,4},{24,8},{28,12},{1,17},{... | collective-permute-start | bytes 393224 | tf_op jit(solution)/shard_map/ppermute | solution.py:203
  44.8 0.8 copy-start.1
  51.8 5.2 %collective-permute-start.9 = (bf16[4,128,128]{2,1,0:T(8,128)(2,1)}, bf16[4,128,128]{2,1,0:T(8,128)(2,1)S(1)}, u32[]{:S(2)}, u32[]{:S(2)}) collective-permute-start(bf16[4,128,128]{2,1,0:T(8,128)(2,1)} %collective-permute-done.6.refs_4_.refs_8_), channel_id=1, source_target_pairs={{0,8},{4,12},{8,0},{12,4},{16,24},{20,28},{24,16},{28,20},{1,9},{5... | collective-permute-start | bytes 393224 | tf_op jit(solution)/shard_map/ppermute | solution.py:203
  52.4 5.7 %collective-permute-start.7 = (bf16[4,128,128]{2,1,0:T(8,128)(2,1)}, bf16[4,128,128]{2,1,0:T(8,128)(2,1)S(1)}, u32[]{:S(2)}, u32[]{:S(2)}) collective-permute-start(bf16[4,128,128]{2,1,0:T(8,128)(2,1)} %collective-permute-done.5.refs_2_.refs_6_), channel_id=1, source_target_pairs={{0,4},{4,0},{8,12},{12,8},{16,20},{20,16},{24,28},{28,24},{1,5},{5... | collective-permute-start | bytes 393224 | tf_op jit(solution)/shard_map/ppermute | solution.py:203
  53.5 5.5 %collective-permute-start.8 = (bf16[4,128,128]{2,1,0:T(8,128)(2,1)}, bf16[4,128,128]{2,1,0:T(8,128)(2,1)S(1)}, u32[]{:S(2)}, u32[]{:S(2)}) collective-permute-start(bf16[4,128,128]{2,1,0:T(8,128)(2,1)} %collective-permute-done.6.refs_4_.refs_8_), channel_id=1, source_target_pairs={{0,4},{4,0},{8,12},{12,8},{16,20},{20,16},{24,28},{28,24},{1,5},{5... | collective-permute-start | bytes 393224 | tf_op jit(solution)/shard_map/ppermute | solution.py:203
  54.4 6.2 %collective-permute-start.11 = (bf16[4,128,128]{2,1,0:T(8,128)(2,1)}, bf16[4,128,128]{2,1,0:T(8,128)(2,1)S(1)}, u32[]{:S(2)}, u32[]{:S(2)}) collective-permute-start(bf16[4,128,128]{2,1,0:T(8,128)(2,1)} %get-tuple-element.63.refs_0_.refs_4_), channel_id=1, source_target_pairs={{0,1},{1,0},{2,3},{3,2},{4,5},{5,4},{6,7},{7,6},{8,9},{9,8},{10,11... | collective-permute-start | bytes 393224 | tf_op jit(solution)/shard_map/ppermute | solution.py:203
  54.4 6.2 %collective-permute-start.12 = (bf16[4,128,128]{2,1,0:T(8,128)(2,1)}, bf16[4,128,128]{2,1,0:T(8,128)(2,1)S(1)}, u32[]{:S(2)}, u32[]{:S(2)}) collective-permute-start(bf16[4,128,128]{2,1,0:T(8,128)(2,1)} %collective-permute-done.4.refs_1_.refs_5_), channel_id=1, source_target_pairs={{0,1},{1,0},{2,3},{3,2},{4,5},{5,4},{6,7},{7,6},{8,9},{9,8},{10,11... | collective-permute-start | bytes 393224 | tf_op jit(solution)/shard_map/ppermute | solution.py:203
  57.0 15.1 %copy-start.3 = (bf16[4,128,128]{2,1,0:T(8,128)(2,1)}, bf16[4,128,128]{2,1,0:T(8,128)(2,1)S(1)}, u32[]{:S(2)}) copy-start(bf16[4,128,128]{2,1,0:T(8,128)(2,1)S(1)} %collective-permute-done.9.refs_6_.refs_10_) | copy-start | bytes 393220
  57.0 4.1 %collective-permute-start.13 = (bf16[4,128,128]{2,1,0:T(8,128)(2,1)}, bf16[4,128,128]{2,1,0:T(8,128)(2,1)S(1)}, u32[]{:S(2)}, u32[]{:S(2)}) collective-permute-start(bf16[4,128,128]{2,1,0:T(8,128)(2,1)} %collective-permute-done.5.refs_2_.refs_6_), channel_id=1, source_target_pairs={{0,1},{1,0},{2,3},{3,2},{4,5},{5,4},{6,7},{7,6},{8,9},{9,8},{10,11... | collective-permute-start | bytes 393224 | tf_op jit(solution)/shard_map/ppermute | solution.py:203
  58.0 19.2 %copy-start.2 = (bf16[8,128,128]{2,1,0:T(8,128)(2,1)}, bf16[8,128,128]{2,1,0:T(8,128)(2,1)S(1)}, u32[]{:S(2)}) copy-start(bf16[8,128,128]{2,1,0:T(8,128)(2,1)S(1)} %slice.15.refs_0_) | copy-start | bytes 786436
  58.0 6.0 %copy-start.4 = (bf16[4,128,128]{2,1,0:T(8,128)(2,1)}, bf16[4,128,128]{2,1,0:T(8,128)(2,1)S(1)}, u32[]{:S(2)}) copy-start(bf16[4,128,128]{2,1,0:T(8,128)(2,1)S(1)} %collective-permute-done.7.refs_3_.refs_7_) | copy-start | bytes 393220
  58.1 3.2 %collective-permute-start.15 = (bf16[4,128,128]{2,1,0:T(8,128)(2,1)}, bf16[4,128,128]{2,1,0:T(8,128)(2,1)S(1)}, u32[]{:S(2)}, u32[]{:S(2)}) collective-permute-start(bf16[4,128,128]{2,1,0:T(8,128)(2,1)} %collective-permute-done.6.refs_4_.refs_8_), channel_id=1, source_target_pairs={{0,1},{1,0},{2,3},{3,2},{4,5},{5,4},{6,7},{7,6},{8,9},{9,8},{10,11... | collective-permute-start | bytes 393224 | tf_op jit(solution)/shard_map/ppermute | solution.py:203
  59.0 5.1 %copy-start.5 = (bf16[4,128,128]{2,1,0:T(8,128)(2,1)}, bf16[4,128,128]{2,1,0:T(8,128)(2,1)S(1)}, u32[]{:S(2)}) copy-start(bf16[4,128,128]{2,1,0:T(8,128)(2,1)S(1)} %collective-permute-done.8.refs_5_.refs_9_) | copy-start | bytes 393220
  59.0 5.1 %collective-permute-start.10 = (bf16[4,128,128]{2,1,0:T(8,128)(2,1)S(1)}, bf16[4,128,128]{2,1,0:T(8,128)(2,1)S(1)}, u32[]{:S(2)}, u32[]{:S(2)}) collective-permute-start(bf16[4,128,128]{2,1,0:T(8,128)(2,1)S(1)} %collective-permute-done.9.refs_6_.refs_10_), channel_id=1, source_target_pairs={{0,4},{4,0},{8,12},{12,8},{16,20},{20,16},{24,28},{28,24},{1,5},{5... | collective-permute-start | bytes 393224 | tf_op jit(solution)/shard_map/ppermute | solution.py:203
  60.6 10.1 %copy-start.8 = (bf16[4,128,128]{2,1,0:T(8,128)(2,1)}, bf16[4,128,128]{2,1,0:T(8,128)(2,1)S(1)}, u32[]{:S(2)}) copy-start(bf16[4,128,128]{2,1,0:T(8,128)(2,1)S(1)} %collective-permute-done.11.refs_8_) | copy-start | bytes 393220
  60.6 3.5 %collective-permute-start.17 = (bf16[4,128,128]{2,1,0:T(8,128)(2,1)S(1)}, bf16[4,128,128]{2,1,0:T(8,128)(2,1)S(1)}, u32[]{:S(2)}, u32[]{:S(2)}) collective-permute-start(bf16[4,128,128]{2,1,0:T(8,128)(2,1)S(1)} %collective-permute-done.9.refs_6_.refs_10_), channel_id=1, source_target_pairs={{0,1},{1,0},{2,3},{3,2},{4,5},{5,4},{6,7},{7,6},{8,9},{9,8},{10,11... | collective-permute-start | bytes 393224 | tf_op jit(solution)/shard_map/ppermute | solution.py:203
  60.6 10.1 %copy-start.9 = (bf16[4,128,128]{2,1,0:T(8,128)(2,1)}, bf16[4,128,128]{2,1,0:T(8,128)(2,1)S(1)}, u32[]{:S(2)}) copy-start(bf16[4,128,128]{2,1,0:T(8,128)(2,1)S(1)} %collective-permute-done.12.refs_9_) | copy-start | bytes 393220
  60.6 3.5 %collective-permute-start.14 = (bf16[4,128,128]{2,1,0:T(8,128)(2,1)S(1)}, bf16[4,128,128]{2,1,0:T(8,128)(2,1)S(1)}, u32[]{:S(2)}, u32[]{:S(2)}) collective-permute-start(bf16[4,128,128]{2,1,0:T(8,128)(2,1)S(1)} %collective-permute-done.7.refs_3_.refs_7_), channel_id=1, source_target_pairs={{0,1},{1,0},{2,3},{3,2},{4,5},{5,4},{6,7},{7,6},{8,9},{9,8},{10,11... | collective-permute-start | bytes 393224 | tf_op jit(solution)/shard_map/ppermute | solution.py:203
  61.1 9.6 %copy-start.10 = (bf16[4,128,128]{2,1,0:T(8,128)(2,1)}, bf16[4,128,128]{2,1,0:T(8,128)(2,1)S(1)}, u32[]{:S(2)}) copy-start(bf16[4,128,128]{2,1,0:T(8,128)(2,1)S(1)} %collective-permute-done.13.refs_10_) | copy-start | bytes 393220
  61.1 3.0 %collective-permute-start.16 = (bf16[4,128,128]{2,1,0:T(8,128)(2,1)S(1)}, bf16[4,128,128]{2,1,0:T(8,128)(2,1)S(1)}, u32[]{:S(2)}, u32[]{:S(2)}) collective-permute-start(bf16[4,128,128]{2,1,0:T(8,128)(2,1)S(1)} %collective-permute-done.8.refs_5_.refs_9_), channel_id=1, source_target_pairs={{0,1},{1,0},{2,3},{3,2},{4,5},{5,4},{6,7},{7,6},{8,9},{9,8},{10,11... | collective-permute-start | bytes 393224 | tf_op jit(solution)/shard_map/ppermute | solution.py:203
  61.2 9.5 %copy-start.11 = (bf16[4,128,128]{2,1,0:T(8,128)(2,1)}, bf16[4,128,128]{2,1,0:T(8,128)(2,1)S(1)}, u32[]{:S(2)}) copy-start(bf16[4,128,128]{2,1,0:T(8,128)(2,1)S(1)} %collective-permute-done.15.refs_12_) | copy-start | bytes 393220
  64.1 6.1 %copy-start.6 = (bf16[4,128,128]{2,1,0:T(8,128)(2,1)}, bf16[4,128,128]{2,1,0:T(8,128)(2,1)S(1)}, u32[]{:S(2)}) copy-start(bf16[4,128,128]{2,1,0:T(8,128)(2,1)S(1)} %collective-permute-done.10.refs_7_.refs_11_) | copy-start | bytes 393220
  64.1 6.6 %copy-start.12 = (bf16[4,128,128]{2,1,0:T(8,128)(2,1)}, bf16[4,128,128]{2,1,0:T(8,128)(2,1)S(1)}, u32[]{:S(2)}) copy-start(bf16[4,128,128]{2,1,0:T(8,128)(2,1)S(1)} %collective-permute-done.17.refs_14_) | copy-start | bytes 393220
  64.1 6.6 %copy-start.13 = (bf16[4,128,128]{2,1,0:T(8,128)(2,1)}, bf16[4,128,128]{2,1,0:T(8,128)(2,1)S(1)}, u32[]{:S(2)}) copy-start(bf16[4,128,128]{2,1,0:T(8,128)(2,1)S(1)} %collective-permute-done.14.refs_11_) | copy-start | bytes 393220
  64.2 6.6 %copy-start.14 = (bf16[4,128,128]{2,1,0:T(8,128)(2,1)}, bf16[4,128,128]{2,1,0:T(8,128)(2,1)S(1)}, u32[]{:S(2)}) copy-start(bf16[4,128,128]{2,1,0:T(8,128)(2,1)S(1)} %collective-permute-done.16.refs_13_) | copy-start | bytes 393220
  64.2 20.4 %all-to-all-start.2 = ((bf16[8,272,128]{2,1,0:T(8,128)(2,1)}), bf16[8,272,128]{2,1,0:T(8,128)(2,1)}, u32[]{:S(2)}, u32[]{:S(2)}) async-start(bf16[8,272,128]{2,1,0:T(8,128)(2,1)} %backward.1), calls=%async_computation.2 | async-start | bytes 1114112 | tf_op jit(solution)/shard_map/all_to_all | solution.py:687
  68.7 8.5 %collective-permute-start.20 = (bf16[8,128,128]{2,1,0:T(8,128)(2,1)S(1)}, bf16[8,128,128]{2,1,0:T(8,128)(2,1)}, u32[]{:S(2)}, u32[]{:S(2)}) collective-permute-start(bf16[8,128,128]{2,1,0:T(8,128)(2,1)S(1)} %slice.15.refs_0_), channel_id=1, source_target_pairs={{0,2},{1,3},{2,0},{3,1},{4,6},{5,7},{6,4},{7,5},{8,10},{9,11},{10,... | collective-permute-start | bytes 786440 | tf_op jit(solution)/shard_map/ppermute | solution.py:203
  70.2 7.0 %collective-permute-start.21 = (bf16[8,128,128]{2,1,0:T(8,128)(2,1)S(1)}, bf16[8,128,128]{2,1,0:T(8,128)(2,1)}, u32[]{:S(2)}, u32[]{:S(2)}) collective-permute-start(bf16[8,128,128]{2,1,0:T(8,128)(2,1)S(1)} %slice.15.refs_0_), channel_id=1, source_target_pairs={{0,1},{1,0},{2,3},{3,2},{4,5},{5,4},{6,7},{7,6},{8,9},{9,8},{10,11... | collective-permute-start | bytes 786440 | tf_op jit(solution)/shard_map/ppermute | solution.py:203
  70.2 1.8 %collective-permute-start.18 = (bf16[4,128,128]{2,1,0:T(8,128)(2,1)S(1)}, bf16[4,128,128]{2,1,0:T(8,128)(2,1)}, u32[]{:S(2)}, u32[]{:S(2)}) collective-permute-start(bf16[4,128,128]{2,1,0:T(8,128)(2,1)S(1)} %collective-permute-done.10.refs_7_.refs_11_), channel_id=1, source_target_pairs={{0,1},{1,0},{2,3},{3,2},{4,5},{5,4},{6,7},{7,6},{8,9},{9,8},{10,11... | collective-permute-start | bytes 393224 | tf_op jit(solution)/shard_map/ppermute | solution.py:203
  77.2 1.9 %collective-permute-start.22 = (bf16[8,128,128]{2,1,0:T(8,128)(2,1)}, bf16[8,128,128]{2,1,0:T(8,128)(2,1)}, u32[]{:S(2)}, u32[]{:S(2)}) collective-permute-start(bf16[8,128,128]{2,1,0:T(8,128)(2,1)} %collective-permute-done.20.refs_2_), channel_id=1, source_target_pairs={{0,1},{1,0},{2,3},{3,2},{4,5},{5,4},{6,7},{7,6},{8,9},{9,8},{10,11... | collective-permute-start | bytes 786440 | tf_op jit(solution)/shard_map/ppermute | solution.py:203
  77.4 10.0 %collective-permute-start.19 = (bf16[128,1024]{1,0:T(8,128)(2,1)}, bf16[128,1024]{1,0:T(8,128)(2,1)S(1)}, u32[]{:S(2)}, u32[]{:S(2)}) collective-permute-start(bf16[128,1024]{1,0:T(8,128)(2,1)} %get-tuple-element.80), channel_id=1, source_target_pairs={{0,2},{1,3},{2,0},{3,1},{4,6},{5,7},{6,4},{7,5},{8,10},{9,11},{10,... | collective-permute-start | bytes 786440 | tf_op jit(solution)/shard_map/ppermute | solution.py:203

commit v3 on v2

--- a/solution.py
+++ b/solution.py
@@ -321,10 +321,10 @@
 
 
 def grad_gated_kernel(
-    ids_ref, c0_hbm, c1_hbm, c2_hbm, c3_hbm, w_hbm, after_ref, send_hbm,
+    c0_hbm, c1_hbm, c2_hbm, c3_hbm, w_hbm, send_hbm,
     c0_ref, c1_ref, c2_ref, c3_ref, w_ref, send_ref, cot_sems, sems,
 ):
-    mine = ids_ref[1]
+    mine = lax.axis_index("ch")
     cots = (c0_ref, c1_ref, c2_ref, c3_ref)
     loads = fetch(zip((c0_hbm, c1_hbm, c2_hbm, c3_hbm), cots), cot_sems)
     copies = column_parts(w_hbm, w_ref, range(4), mine, sems)
@@ -634,10 +634,9 @@
     (sent_grad,) = call(
         grad_gated_kernel,
         [sent],
-        [ids],
+        [],
         *cots,
         out_weight,
-        small=(prm,),
         scratch=(*cots, weight_room, sent),
         dmas=(4, 4),
     )

time: 89.9 us -> 89.2 us (level)
  waiting for transfers between devices: 16.1 us -> 17.3 us
  starting transfers between devices: 33.7 us -> 32.6 us
    ppermute x23, waiting for transfers between devices: 14.3 us -> 17.2 us  [swap_bits(): return lax.ppermute(shard, axis, [(i, i ^ mask) for i in range(size)])]
    all_to_all x1, waiting for transfers between devices: 1.85 us -> 0.01 us  [on_device_packed(): moved_grad = lax.all_to_all(sent_grad, 'seq', 0, 0, tiled=True)]
  transfers between devices with their start and end apart: 26 -> 26, of which waited for: 7 -> 8; matrix products, arithmetic and copies ran while one was open for 4% -> 4% of each run, Pallas kernels for 36% -> 36%
where the time goes in v3:
time: 89.2 us; the launch traced here: 88.5 us
  starting transfers between devices  32.6 us (37%)
  Pallas kernels  31.6 us (35%)
  waiting for transfers between devices  17.3 us (19%)
  other arithmetic  3.07 us (3%)
  local copies, waits for them, and re-layouts  3 us (3%)
  between operations  0.93 us (1%)
    pallas_call x7, Pallas kernels, call(): pl.pallas_call(kernel, out_shape=list(outs) + list(small_outs), in_specs=...  31.6 us
    ppermute x23, waiting for transfers between devices, swap_bits(): return lax.ppermute(shard, axis, [(i, i ^ mask) for i in range(size)])  17.2 us
    ppermute x23, starting transfers between devices, swap_bits(): return lax.ppermute(shard, axis, [(i, i ^ mask) for i in range(size)])  15.7 us
    all_to_all x1, starting transfers between devices, on_device_packed(): streams = lax.all_to_all(packed, 'seq', 0, 0, tiled=True)  6.86 us
    all_to_all x1, starting transfers between devices, on_device_packed(): moved_grad = lax.all_to_all(sent_grad, 'seq', 0, 0, tiled=True)  5.66 us
    all_to_all x1, starting transfers between devices, on_device_packed(): returned = lax.all_to_all(back, 'seq', 0, 0, tiled=True)  4.4 us
    convert_element_type x1, other arithmetic, on_device_packed(): layer_out = (keep + share.astype(F32)).astype(BF16)  1.81 us
  transfers between devices with their start and end apart: 26, of which 8 were waited for; matrix products, arithmetic and copies ran while one was open for 4% of the time, Pallas kernels for 36%

profile of v3, /device:TPU:0, one launch (start us, length us, event | category | flops | bytes accessed | tf_op | source)
XLA Modules:
  0.0 88.5 jit_solution(3661725162973412348)
XLA Ops:
  0.6 0.0 copy-start
  0.6 0.5 collective-permute-start.3
  1.2 2.1 %pack_streams.1 = bf16[8,2,128,128]{3,2,1,0:T(8,128)(2,1)} custom-call(bf16[128,512]{1,0:T(8,128)(2,1)} %q_hbm.1, bf16[128,512]{1,0:T(8,128)(2,1)} %k_hbm.1, bf16[128,512]{1,0:T(8,128)(2,1)} %v_hbm.1, f32[128,512]{1,0:T(8,128)} %h_hbm.1), custom_call_target="tpu_custom_call" | custom-call | flops 1 | bytes 1 | tf_op jit(solution)/shard_map/pack_streams/pallas_call | solution.py:579
  3.3 6.9 %all-to-all-start.1 = ((bf16[8,2,128,128]{3,2,1,0:T(8,128)(2,1)}), bf16[8,2,128,128]{3,2,1,0:T(8,128)(2,1)}, u32[]{:S(2)}, u32[]{:S(2)}) async-start(bf16[8,2,128,128]{3,2,1,0:T(8,128)(2,1)} %pack_streams.1), calls=%async_computation.1 | async-start | bytes 1048576 | tf_op jit(solution)/shard_map/all_to_all | solution.py:631
  10.2 1.5 %collective-permute-start.1 = (bf16[128,1024]{1,0:T(8,128)(2,1)}, bf16[128,1024]{1,0:T(8,128)(2,1)S(1)}, u32[]{:S(2)}, u32[]{:S(2)}) collective-permute-start(bf16[128,1024]{1,0:T(8,128)(2,1)} %c0_hbm.1), channel_id=1, source_target_pairs={{0,2},{1,3},{2,0},{3,1},{4,6},{5,7},{6,4},{7,5},{8,10},{9,11},{10,... | collective-permute-start | bytes 786440 | tf_op jit(solution)/shard_map/ppermute | solution.py:203
  11.7 7.1 %collective-permute-done.1.c2_hbm = bf16[128,1024]{1,0:T(8,128)(2,1)S(1)} collective-permute-done((bf16[128,1024]{1,0:T(8,128)(2,1)}, bf16[128,1024]{1,0:T(8,128)(2,1)S(1)}, u32[]{:S(2)}, u32[]{:S(2)}) %collective-permute-start.1) | collective-permute-done | bytes 262176 | tf_op jit(solution)/shard_map/ppermute | solution.py:203
  18.8 1.7 %collective-permute-done.2.c3_hbm = bf16[128,1024]{1,0:T(8,128)(2,1)} collective-permute-done((bf16[128,1024]{1,0:T(8,128)(2,1)S(1)}, bf16[128,1024]{1,0:T(8,128)(2,1)}, u32[]{:S(2)}, u32[]{:S(2)}) %collective-permute-start.2) | collective-permute-done | bytes 262176 | tf_op jit(solution)/shard_map/ppermute | solution.py:203
  20.5 4.9 %grad_gated.1.after_hbm = bf16[8,192,128]{2,1,0:T(8,128)(2,1)} custom-call(bf16[128,1024]{1,0:T(8,128)(2,1)} %c0_hbm.1, bf16[128,1024]{1,0:T(8,128)(2,1)} %collective-permute-done.c1_hbm, bf16[128,1024]{1,0:T(8,128)(2,1)} %copy-done.7, bf16[128,1024]{1,0:T(8,128)(2,1)} %collective-permute-done.2.c3_hbm, bf16[512,4096]{1,0:T(8,128)(2,1)} %refs_16_.1), custom_call_target="tpu_custom_call" | custom-call | flops 1 | bytes 1 | tf_op jit(solution)/shard_map/grad_gated/pallas_call | solution.py:579
  25.3 0.1 all-to-all-done.1.moved_hbm.streams_hbm
  25.4 5.7 %all-to-all-start = ((bf16[8,192,128]{2,1,0:T(8,128)(2,1)}), bf16[8,192,128]{2,1,0:T(8,128)(2,1)S(1)}, u32[]{:S(2)}, u32[]{:S(2)}) async-start(bf16[8,192,128]{2,1,0:T(8,128)(2,1)} %grad_gated.1.after_hbm), calls=%async_computation | async-start | bytes 786432 | tf_op jit(solution)/shard_map/all_to_all | solution.py:643
  31.1 0.1 dynamic-slice_bitcast_fusion.3
  31.2 0.8 dynamic-slice_bitcast_fusion.2
  32.0 0.1 iota.11
  32.0 0.1 concatenate.10
  32.1 0.1 concatenate.9
  32.3 0.7 pad_maximum_fusion.prm_ref
  32.9 5.1 %forward.1 = (bf16[4,128,128]{2,1,0:T(8,128)(2,1)}, f32[1024,128]{1,0:T(8,128)}, f32[1024,128]{1,0:T(8,128)}, f32[1024,128]{1,0:T(8,128)}, f32[4,512,128]{2,1,0:T(8,128)}) custom-call(bf16[8,2,128,128]{3,2,1,0:T(8,128)(2,1)} %all-to-all-done.1.moved_hbm.streams_hbm, bf16[2,1024,512]{2,1,0:T(8,128)(2,1)} %constant.20.clone.fwd_hbm, ...), custom_call_target="tpu_custom_call" | custom-call | flops 1 | bytes 1 | tf_op jit(solution)/shard_map/forward/pallas_call | solution.py:579
  38.1 2.1 %collective-permute-start.4 = (bf16[4,128,128]{2,1,0:T(8,128)(2,1)}, bf16[4,128,128]{2,1,0:T(8,128)(2,1)}, u32[]{:S(2)}, u32[]{:S(2)}) collective-permute-start(bf16[4,128,128]{2,1,0:T(8,128)(2,1)} %get-tuple-element.63.refs_0_.refs_4_), channel_id=1, source_target_pairs={{0,4},{4,0},{8,12},{12,8},{16,20},{20,16},{24,28},{28,24},{1,5},{5... | collective-permute-start | bytes 393224 | tf_op jit(solution)/shard_map/ppermute | solution.py:203
  40.2 1.5 %collective-permute-start.5 = (bf16[4,128,128]{2,1,0:T(8,128)(2,1)}, bf16[4,128,128]{2,1,0:T(8,128)(2,1)}, u32[]{:S(2)}, u32[]{:S(2)}) collective-permute-start(bf16[4,128,128]{2,1,0:T(8,128)(2,1)} %get-tuple-element.63.refs_0_.refs_4_), channel_id=1, source_target_pairs={{0,8},{4,12},{8,0},{12,4},{16,24},{20,28},{24,16},{28,20},{1,9},{5... | collective-permute-start | bytes 393224 | tf_op jit(solution)/shard_map/ppermute | solution.py:203
  41.6 2.4 %collective-permute-start.6 = (bf16[4,128,128]{2,1,0:T(8,128)(2,1)}, bf16[4,128,128]{2,1,0:T(8,128)(2,1)}, u32[]{:S(2)}, u32[]{:S(2)}) collective-permute-start(bf16[4,128,128]{2,1,0:T(8,128)(2,1)} %get-tuple-element.63.refs_0_.refs_4_), channel_id=1, source_target_pairs={{0,16},{4,20},{8,24},{12,28},{16,0},{20,4},{24,8},{28,12},{1,17},{... | collective-permute-start | bytes 393224 | tf_op jit(solution)/shard_map/ppermute | solution.py:203
  44.0 0.8 copy-done.1
  44.8 6.2 %backward.1 = bf16[8,272,128]{2,1,0:T(8,128)(2,1)} custom-call(bf16[8,192,128]{2,1,0:T(8,128)(2,1)} %copy-done.1, f32[1024,128]{1,0:T(8,128)} %get-tuple-element.52.mq_hbm, f32[4,512,128]{2,1,0:T(8,128)} %get-tuple-element.53.spec_hbm, f32[1024,128]{1,0:T(8,128)} %get-tuple-element.54.kqs_hbm, f32[1024,128]{1,0:T(8,128)} %get-tuple-element.55.vhs_hbm, ...), custom_call_target="tpu_custom_call" | custom-call | flops 1 | bytes 1 | tf_op jit(solution)/shard_map/backward/pallas_call | solution.py:579
  51.0 0.6 collective-permute-start.9
  51.6 0.6 collective-permute-start.7
  52.2 1.5 %collective-permute-start.8 = (bf16[4,128,128]{2,1,0:T(8,128)(2,1)}, bf16[4,128,128]{2,1,0:T(8,128)(2,1)S(1)}, u32[]{:S(2)}, u32[]{:S(2)}) collective-permute-start(bf16[4,128,128]{2,1,0:T(8,128)(2,1)} %collective-permute-done.6.refs_4_.refs_8_), channel_id=1, source_target_pairs={{0,4},{4,0},{8,12},{12,8},{16,20},{20,16},{24,28},{28,24},{1,5},{5... | collective-permute-start | bytes 393224 | tf_op jit(solution)/shard_map/ppermute | solution.py:203
  53.7 0.5 collective-permute-start.12
  54.2 2.1 %collective-permute-done.9.refs_6_.refs_10_ = bf16[4,128,128]{2,1,0:T(8,128)(2,1)S(1)} collective-permute-done((bf16[4,128,128]{2,1,0:T(8,128)(2,1)}, bf16[4,128,128]{2,1,0:T(8,128)(2,1)S(1)}, u32[]{:S(2)}, u32[]{:S(2)}) %collective-permute-start.9) | collective-permute-done | bytes 131104 | tf_op jit(solution)/shard_map/ppermute | solution.py:203
  56.3 1.0 %slice.15.refs_0_ = bf16[8,128,128]{2,1,0:T(8,128)(2,1)S(1)} slice(bf16[8,192,128]{2,1,0:T(8,128)(2,1)} %copy-done.1), slice={[0:8], [64:192], [0:128]} | slice | bytes 524288 | tf_op jit(solution)/shard_map/slice | solution.py:679
  57.3 0.0 copy-start.2
  57.3 0.0 copy-start.4
  57.3 0.5 collective-permute-start.15
  57.8 0.7 collective-permute-done.8.refs_5_.refs_9_
  58.5 0.7 collective-permute-start.10
  59.2 0.5 collective-permute-start.16
  59.7 0.1 collective-permute-start.17
  59.8 3.7 %collective-permute-done.10.refs_7_.refs_11_ = bf16[4,128,128]{2,1,0:T(8,128)(2,1)S(1)} collective-permute-done((bf16[4,128,128]{2,1,0:T(8,128)(2,1)S(1)}, bf16[4,128,128]{2,1,0:T(8,128)(2,1)S(1)}, u32[]{:S(2)}, u32[]{:S(2)}) %collective-permute-start.10) | collective-permute-done | bytes 131104 | tf_op jit(solution)/shard_map/ppermute | solution.py:203
  63.6 4.4 %all-to-all-start.2 = ((bf16[8,272,128]{2,1,0:T(8,128)(2,1)}), bf16[8,272,128]{2,1,0:T(8,128)(2,1)}, u32[]{:S(2)}, u32[]{:S(2)}) async-start(bf16[8,272,128]{2,1,0:T(8,128)(2,1)} %backward.1), calls=%async_computation.2 | async-start | bytes 1114112 | tf_op jit(solution)/shard_map/all_to_all | solution.py:686
  68.0 1.6 %collective-permute-start.20 = (bf16[8,128,128]{2,1,0:T(8,128)(2,1)S(1)}, bf16[8,128,128]{2,1,0:T(8,128)(2,1)}, u32[]{:S(2)}, u32[]{:S(2)}) collective-permute-start(bf16[8,128,128]{2,1,0:T(8,128)(2,1)S(1)} %slice.15.refs_0_), channel_id=1, source_target_pairs={{0,2},{1,3},{2,0},{3,1},{4,6},{5,7},{6,4},{7,5},{8,10},{9,11},{10,... | collective-permute-start | bytes 786440 | tf_op jit(solution)/shard_map/ppermute | solution.py:203
  69.5 0.5 collective-permute-start.18
  70.1 0.6 pad_add_fusion.ids_ref
  70.7 0.7 collective-permute-done.18.refs_15_
  71.4 5.1 %project.1 = (f32[128,1024]{1,0:T(8,128)}, bf16[128,1024]{1,0:T(8,128)(2,1)}) custom-call(s32[2]{0:T(128)} %pad_add_fusion.ids_ref, bf16[4,128,128]{2,1,0:T(8,128)(2,1)} %get-tuple-element.63.refs_0_.refs_4_, bf16[4,128,128]{2,1,0:T(8,128)(2,1)} %collective-permute-done.4.refs_1_.refs_5_, bf16[4,128,128]{2,1,0:T(8,128)(2,1)} %collective-permute-done.5.refs_2_.refs_6_, ...), custom_call_target="tpu_custom_call" | custom-call | flops 1 | bytes 1 | tf_op jit(solution)/shard_map/project/pallas_call | solution.py:579
  76.5 0.2 collective-permute-start.22
  76.7 0.5 collective-permute-start.19
  77.3 1.2 %collective-permute-done.22.refs_3_ = bf16[8,128,128]{2,1,0:T(8,128)(2,1)} collective-permute-done((bf16[8,128,128]{2,1,0:T(8,128)(2,1)}, bf16[8,128,128]{2,1,0:T(8,128)(2,1)}, u32[]{:S(2)}, u32[]{:S(2)}) %collective-permute-start.22) | collective-permute-done | bytes 262176 | tf_op jit(solution)/shard_map/ppermute | solution.py:203
  78.5 5.3 %grad_weight.1 = f32[512,512]{1,0:T(8,128)} custom-call(s32[2]{0:T(128)} %pad_add_fusion.ids_ref, bf16[8,128,128]{2,1,0:T(8,128)(2,1)} %copy-done.2, bf16[8,128,128]{2,1,0:T(8,128)(2,1)} %collective-permute-done.21.refs_1_, bf16[8,128,128]{2,1,0:T(8,128)(2,1)} %collective-permute-done.20.refs_2_, bf16[8,128,128]{2,1,0:T(8,128)(2,1)} %collective-permute-done.22.refs_3_, ...), custom_call_target="tpu_custom_call" | custom-call | flops 1 | bytes 1 | tf_op jit(solution)/shard_map/grad_weight/pallas_call | solution.py:579
  83.8 2.8 %unpack.1 = (f32[128,512]{1,0:T(8,128)}, f32[128,512]{1,0:T(8,128)}, f32[128,512]{1,0:T(8,128)}, f32[128,512]{1,0:T(8,128)}, f32[3,3,512]{2,1,0:T(4,128)}, /*index=5*/f32[1,512]{1,0:T(1,128)}) custom-call(bf16[8,272,128]{2,1,0:T(8,128)(2,1)} %all-to-all-done.2.moved_hbm), custom_call_target="tpu_custom_call" | custom-call | flops 1 | bytes 1 | tf_op jit(solution)/shard_map/unpack/pallas_call | solution.py:579
  86.7 1.8 %add_convert_fusion = bf16[128,1024]{1,0:T(8,128)(2,1)} fusion(f32[128,1024]{1,0:T(8,128)} %get-tuple-element.79, bf16[128,1024]{1,0:T(8,128)(2,1)S(1)} %collective-permute-done.19), kind=kLoop, calls=%fused_computation | loop fusion | flops 393216 | bytes 1048576 | tf_op jit(solution)/shard_map/convert_element_type | solution.py:733
  (51 shorter events, 0.1 us)
Async XLA Ops:
  0.6 30.5 %copy-start = (f32[512]{0:T(512)S(1)}, f32[512]{0:T(512)}, u32[]{:S(2)}) copy-start(f32[512]{0:T(512)} %param.15) | copy-start | bytes 6148
  0.6 43.4 %collective-permute-start.3 = (bf16[512,4096]{1,0:T(8,128)(2,1)}, bf16[512,4096]{1,0:T(8,128)(2,1)}, u32[]{:S(2)}, u32[]{:S(2)}) collective-permute-start(bf16[512,4096]{1,0:T(8,128)(2,1)} %refs_16_.1), channel_id=1, source_target_pairs={{0,1},{1,0},{2,3},{3,2},{4,5},{5,4},{6,7},{7,6},{8,9},{9,8},{10,11... | collective-permute-start | bytes 12582920 | tf_op jit(solution)/shard_map/ppermute | solution.py:203
  3.3 22.1 %all-to-all-start.1 = ((bf16[8,2,128,128]{3,2,1,0:T(8,128)(2,1)}), bf16[8,2,128,128]{3,2,1,0:T(8,128)(2,1)}, u32[]{:S(2)}, u32[]{:S(2)}) async-start(bf16[8,2,128,128]{3,2,1,0:T(8,128)(2,1)} %pack_streams.1), calls=%async_computation.1 | async-start | bytes 1048576 | tf_op jit(solution)/shard_map/all_to_all | solution.py:631
  10.2 8.6 %collective-permute-start.1 = (bf16[128,1024]{1,0:T(8,128)(2,1)}, bf16[128,1024]{1,0:T(8,128)(2,1)S(1)}, u32[]{:S(2)}, u32[]{:S(2)}) collective-permute-start(bf16[128,1024]{1,0:T(8,128)(2,1)} %c0_hbm.1), channel_id=1, source_target_pairs={{0,2},{1,3},{2,0},{3,1},{4,6},{5,7},{6,4},{7,5},{8,10},{9,11},{10,... | collective-permute-start | bytes 786440 | tf_op jit(solution)/shard_map/ppermute | solution.py:203
  11.7 7.2 %collective-permute-start = (bf16[128,1024]{1,0:T(8,128)(2,1)}, bf16[128,1024]{1,0:T(8,128)(2,1)}, u32[]{:S(2)}, u32[]{:S(2)}) collective-permute-start(bf16[128,1024]{1,0:T(8,128)(2,1)} %c0_hbm.1), channel_id=1, source_target_pairs={{0,1},{1,0},{2,3},{3,2},{4,5},{5,4},{6,7},{7,6},{8,9},{9,8},{10,11... | collective-permute-start | bytes 786440 | tf_op jit(solution)/shard_map/ppermute | solution.py:203
  18.8 1.7 %copy-start.7 = (bf16[128,1024]{1,0:T(8,128)(2,1)}, bf16[128,1024]{1,0:T(8,128)(2,1)S(1)}, u32[]{:S(2)}) copy-start(bf16[128,1024]{1,0:T(8,128)(2,1)S(1)} %collective-permute-done.1.c2_hbm) | copy-start | bytes 786436
  18.8 1.7 %collective-permute-start.2 = (bf16[128,1024]{1,0:T(8,128)(2,1)S(1)}, bf16[128,1024]{1,0:T(8,128)(2,1)}, u32[]{:S(2)}, u32[]{:S(2)}) collective-permute-start(bf16[128,1024]{1,0:T(8,128)(2,1)S(1)} %collective-permute-done.1.c2_hbm), channel_id=1, source_target_pairs={{0,1},{1,0},{2,3},{3,2},{4,5},{5,4},{6,7},{7,6},{8,9},{9,8},{10,11... | collective-permute-start | bytes 786440 | tf_op jit(solution)/shard_map/ppermute | solution.py:203
  25.4 18.6 %all-to-all-start = ((bf16[8,192,128]{2,1,0:T(8,128)(2,1)}), bf16[8,192,128]{2,1,0:T(8,128)(2,1)S(1)}, u32[]{:S(2)}, u32[]{:S(2)}) async-start(bf16[8,192,128]{2,1,0:T(8,128)(2,1)} %grad_gated.1.after_hbm), calls=%async_computation | async-start | bytes 786432 | tf_op jit(solution)/shard_map/all_to_all | solution.py:643
  38.1 12.9 %collective-permute-start.4 = (bf16[4,128,128]{2,1,0:T(8,128)(2,1)}, bf16[4,128,128]{2,1,0:T(8,128)(2,1)}, u32[]{:S(2)}, u32[]{:S(2)}) collective-permute-start(bf16[4,128,128]{2,1,0:T(8,128)(2,1)} %get-tuple-element.63.refs_0_.refs_4_), channel_id=1, source_target_pairs={{0,4},{4,0},{8,12},{12,8},{16,20},{20,16},{24,28},{28,24},{1,5},{5... | collective-permute-start | bytes 393224 | tf_op jit(solution)/shard_map/ppermute | solution.py:203
  40.2 10.8 %collective-permute-start.5 = (bf16[4,128,128]{2,1,0:T(8,128)(2,1)}, bf16[4,128,128]{2,1,0:T(8,128)(2,1)}, u32[]{:S(2)}, u32[]{:S(2)}) collective-permute-start(bf16[4,128,128]{2,1,0:T(8,128)(2,1)} %get-tuple-element.63.refs_0_.refs_4_), channel_id=1, source_target_pairs={{0,8},{4,12},{8,0},{12,4},{16,24},{20,28},{24,16},{28,20},{1,9},{5... | collective-permute-start | bytes 393224 | tf_op jit(solution)/shard_map/ppermute | solution.py:203
  41.6 9.4 %collective-permute-start.6 = (bf16[4,128,128]{2,1,0:T(8,128)(2,1)}, bf16[4,128,128]{2,1,0:T(8,128)(2,1)}, u32[]{:S(2)}, u32[]{:S(2)}) collective-permute-start(bf16[4,128,128]{2,1,0:T(8,128)(2,1)} %get-tuple-element.63.refs_0_.refs_4_), channel_id=1, source_target_pairs={{0,16},{4,20},{8,24},{12,28},{16,0},{20,4},{24,8},{28,12},{1,17},{... | collective-permute-start | bytes 393224 | tf_op jit(solution)/shard_map/ppermute | solution.py:203
  44.0 0.8 copy-start.1
  51.0 5.2 %collective-permute-start.9 = (bf16[4,128,128]{2,1,0:T(8,128)(2,1)}, bf16[4,128,128]{2,1,0:T(8,128)(2,1)S(1)}, u32[]{:S(2)}, u32[]{:S(2)}) collective-permute-start(bf16[4,128,128]{2,1,0:T(8,128)(2,1)} %collective-permute-done.6.refs_4_.refs_8_), channel_id=1, source_target_pairs={{0,8},{4,12},{8,0},{12,4},{16,24},{20,28},{24,16},{28,20},{1,9},{5... | collective-permute-start | bytes 393224 | tf_op jit(solution)/shard_map/ppermute | solution.py:203
  51.6 5.7 %collective-permute-start.7 = (bf16[4,128,128]{2,1,0:T(8,128)(2,1)}, bf16[4,128,128]{2,1,0:T(8,128)(2,1)S(1)}, u32[]{:S(2)}, u32[]{:S(2)}) collective-permute-start(bf16[4,128,128]{2,1,0:T(8,128)(2,1)} %collective-permute-done.5.refs_2_.refs_6_), channel_id=1, source_target_pairs={{0,4},{4,0},{8,12},{12,8},{16,20},{20,16},{24,28},{28,24},{1,5},{5... | collective-permute-start | bytes 393224 | tf_op jit(solution)/shard_map/ppermute | solution.py:203
  52.2 6.3 %collective-permute-start.8 = (bf16[4,128,128]{2,1,0:T(8,128)(2,1)}, bf16[4,128,128]{2,1,0:T(8,128)(2,1)S(1)}, u32[]{:S(2)}, u32[]{:S(2)}) collective-permute-start(bf16[4,128,128]{2,1,0:T(8,128)(2,1)} %collective-permute-done.6.refs_4_.refs_8_), channel_id=1, source_target_pairs={{0,4},{4,0},{8,12},{12,8},{16,20},{20,16},{24,28},{28,24},{1,5},{5... | collective-permute-start | bytes 393224 | tf_op jit(solution)/shard_map/ppermute | solution.py:203
  53.7 5.5 %collective-permute-start.11 = (bf16[4,128,128]{2,1,0:T(8,128)(2,1)}, bf16[4,128,128]{2,1,0:T(8,128)(2,1)S(1)}, u32[]{:S(2)}, u32[]{:S(2)}) collective-permute-start(bf16[4,128,128]{2,1,0:T(8,128)(2,1)} %get-tuple-element.63.refs_0_.refs_4_), channel_id=1, source_target_pairs={{0,1},{1,0},{2,3},{3,2},{4,5},{5,4},{6,7},{7,6},{8,9},{9,8},{10,11... | collective-permute-start | bytes 393224 | tf_op jit(solution)/shard_map/ppermute | solution.py:203
  53.7 5.6 %collective-permute-start.12 = (bf16[4,128,128]{2,1,0:T(8,128)(2,1)}, bf16[4,128,128]{2,1,0:T(8,128)(2,1)S(1)}, u32[]{:S(2)}, u32[]{:S(2)}) collective-permute-start(bf16[4,128,128]{2,1,0:T(8,128)(2,1)} %collective-permute-done.4.refs_1_.refs_5_), channel_id=1, source_target_pairs={{0,1},{1,0},{2,3},{3,2},{4,5},{5,4},{6,7},{7,6},{8,9},{9,8},{10,11... | collective-permute-start | bytes 393224 | tf_op jit(solution)/shard_map/ppermute | solution.py:203
  56.2 15.1 %copy-start.3 = (bf16[4,128,128]{2,1,0:T(8,128)(2,1)}, bf16[4,128,128]{2,1,0:T(8,128)(2,1)S(1)}, u32[]{:S(2)}) copy-start(bf16[4,128,128]{2,1,0:T(8,128)(2,1)S(1)} %collective-permute-done.9.refs_6_.refs_10_) | copy-start | bytes 393220
  56.2 3.5 %collective-permute-start.13 = (bf16[4,128,128]{2,1,0:T(8,128)(2,1)}, bf16[4,128,128]{2,1,0:T(8,128)(2,1)S(1)}, u32[]{:S(2)}, u32[]{:S(2)}) collective-permute-start(bf16[4,128,128]{2,1,0:T(8,128)(2,1)} %collective-permute-done.5.refs_2_.refs_6_), channel_id=1, source_target_pairs={{0,1},{1,0},{2,3},{3,2},{4,5},{5,4},{6,7},{7,6},{8,9},{9,8},{10,11... | collective-permute-start | bytes 393224 | tf_op jit(solution)/shard_map/ppermute | solution.py:203
  57.3 19.2 %copy-start.2 = (bf16[8,128,128]{2,1,0:T(8,128)(2,1)}, bf16[8,128,128]{2,1,0:T(8,128)(2,1)S(1)}, u32[]{:S(2)}) copy-start(bf16[8,128,128]{2,1,0:T(8,128)(2,1)S(1)} %slice.15.refs_0_) | copy-start | bytes 786436
  57.3 6.2 %copy-start.4 = (bf16[4,128,128]{2,1,0:T(8,128)(2,1)}, bf16[4,128,128]{2,1,0:T(8,128)(2,1)S(1)}, u32[]{:S(2)}) copy-start(bf16[4,128,128]{2,1,0:T(8,128)(2,1)S(1)} %collective-permute-done.7.refs_3_.refs_7_) | copy-start | bytes 393220
  57.3 2.5 %collective-permute-start.15 = (bf16[4,128,128]{2,1,0:T(8,128)(2,1)}, bf16[4,128,128]{2,1,0:T(8,128)(2,1)S(1)}, u32[]{:S(2)}, u32[]{:S(2)}) collective-permute-start(bf16[4,128,128]{2,1,0:T(8,128)(2,1)} %collective-permute-done.6.refs_4_.refs_8_), channel_id=1, source_target_pairs={{0,1},{1,0},{2,3},{3,2},{4,5},{5,4},{6,7},{7,6},{8,9},{9,8},{10,11... | collective-permute-start | bytes 393224 | tf_op jit(solution)/shard_map/ppermute | solution.py:203
  58.5 5.0 %copy-start.5 = (bf16[4,128,128]{2,1,0:T(8,128)(2,1)}, bf16[4,128,128]{2,1,0:T(8,128)(2,1)S(1)}, u32[]{:S(2)}) copy-start(bf16[4,128,128]{2,1,0:T(8,128)(2,1)S(1)} %collective-permute-done.8.refs_5_.refs_9_) | copy-start | bytes 393220
  58.5 5.0 %collective-permute-start.10 = (bf16[4,128,128]{2,1,0:T(8,128)(2,1)S(1)}, bf16[4,128,128]{2,1,0:T(8,128)(2,1)S(1)}, u32[]{:S(2)}, u32[]{:S(2)}) collective-permute-start(bf16[4,128,128]{2,1,0:T(8,128)(2,1)S(1)} %collective-permute-done.9.refs_6_.refs_10_), channel_id=1, source_target_pairs={{0,4},{4,0},{8,12},{12,8},{16,20},{20,16},{24,28},{28,24},{1,5},{5... | collective-permute-start | bytes 393224 | tf_op jit(solution)/shard_map/ppermute | solution.py:203
  59.2 10.8 %copy-start.8 = (bf16[4,128,128]{2,1,0:T(8,128)(2,1)}, bf16[4,128,128]{2,1,0:T(8,128)(2,1)S(1)}, u32[]{:S(2)}) copy-start(bf16[4,128,128]{2,1,0:T(8,128)(2,1)S(1)} %collective-permute-done.11.refs_8_) | copy-start | bytes 393220
  59.2 4.3 %collective-permute-start.14 = (bf16[4,128,128]{2,1,0:T(8,128)(2,1)S(1)}, bf16[4,128,128]{2,1,0:T(8,128)(2,1)S(1)}, u32[]{:S(2)}, u32[]{:S(2)}) collective-permute-start(bf16[4,128,128]{2,1,0:T(8,128)(2,1)S(1)} %collective-permute-done.7.refs_3_.refs_7_), channel_id=1, source_target_pairs={{0,1},{1,0},{2,3},{3,2},{4,5},{5,4},{6,7},{7,6},{8,9},{9,8},{10,11... | collective-permute-start | bytes 393224 | tf_op jit(solution)/shard_map/ppermute | solution.py:203
  59.2 10.8 %copy-start.9 = (bf16[4,128,128]{2,1,0:T(8,128)(2,1)}, bf16[4,128,128]{2,1,0:T(8,128)(2,1)S(1)}, u32[]{:S(2)}) copy-start(bf16[4,128,128]{2,1,0:T(8,128)(2,1)S(1)} %collective-permute-done.12.refs_9_) | copy-start | bytes 393220
  59.2 4.3 %collective-permute-start.16 = (bf16[4,128,128]{2,1,0:T(8,128)(2,1)S(1)}, bf16[4,128,128]{2,1,0:T(8,128)(2,1)S(1)}, u32[]{:S(2)}, u32[]{:S(2)}) collective-permute-start(bf16[4,128,128]{2,1,0:T(8,128)(2,1)S(1)} %collective-permute-done.8.refs_5_.refs_9_), channel_id=1, source_target_pairs={{0,1},{1,0},{2,3},{3,2},{4,5},{5,4},{6,7},{7,6},{8,9},{9,8},{10,11... | collective-permute-start | bytes 393224 | tf_op jit(solution)/shard_map/ppermute | solution.py:203
  59.7 10.3 %copy-start.10 = (bf16[4,128,128]{2,1,0:T(8,128)(2,1)}, bf16[4,128,128]{2,1,0:T(8,128)(2,1)S(1)}, u32[]{:S(2)}) copy-start(bf16[4,128,128]{2,1,0:T(8,128)(2,1)S(1)} %collective-permute-done.13.refs_10_) | copy-start | bytes 393220
  59.7 3.8 %collective-permute-start.17 = (bf16[4,128,128]{2,1,0:T(8,128)(2,1)S(1)}, bf16[4,128,128]{2,1,0:T(8,128)(2,1)S(1)}, u32[]{:S(2)}, u32[]{:S(2)}) collective-permute-start(bf16[4,128,128]{2,1,0:T(8,128)(2,1)S(1)} %collective-permute-done.9.refs_6_.refs_10_), channel_id=1, source_target_pairs={{0,1},{1,0},{2,3},{3,2},{4,5},{5,4},{6,7},{7,6},{8,9},{9,8},{10,11... | collective-permute-start | bytes 393224 | tf_op jit(solution)/shard_map/ppermute | solution.py:203
  59.8 10.2 %copy-start.11 = (bf16[4,128,128]{2,1,0:T(8,128)(2,1)}, bf16[4,128,128]{2,1,0:T(8,128)(2,1)S(1)}, u32[]{:S(2)}) copy-start(bf16[4,128,128]{2,1,0:T(8,128)(2,1)S(1)} %collective-permute-done.15.refs_12_) | copy-start | bytes 393220
  63.5 6.0 %copy-start.6 = (bf16[4,128,128]{2,1,0:T(8,128)(2,1)}, bf16[4,128,128]{2,1,0:T(8,128)(2,1)S(1)}, u32[]{:S(2)}) copy-start(bf16[4,128,128]{2,1,0:T(8,128)(2,1)S(1)} %collective-permute-done.10.refs_7_.refs_11_) | copy-start | bytes 393220
  63.5 6.5 %copy-start.12 = (bf16[4,128,128]{2,1,0:T(8,128)(2,1)}, bf16[4,128,128]{2,1,0:T(8,128)(2,1)S(1)}, u32[]{:S(2)}) copy-start(bf16[4,128,128]{2,1,0:T(8,128)(2,1)S(1)} %collective-permute-done.14.refs_11_) | copy-start | bytes 393220
  63.5 7.1 %copy-start.13 = (bf16[4,128,128]{2,1,0:T(8,128)(2,1)}, bf16[4,128,128]{2,1,0:T(8,128)(2,1)S(1)}, u32[]{:S(2)}) copy-start(bf16[4,128,128]{2,1,0:T(8,128)(2,1)S(1)} %collective-permute-done.16.refs_13_) | copy-start | bytes 393220
  63.5 7.1 %copy-start.14 = (bf16[4,128,128]{2,1,0:T(8,128)(2,1)}, bf16[4,128,128]{2,1,0:T(8,128)(2,1)S(1)}, u32[]{:S(2)}) copy-start(bf16[4,128,128]{2,1,0:T(8,128)(2,1)S(1)} %collective-permute-done.17.refs_14_) | copy-start | bytes 393220
  63.6 20.3 %all-to-all-start.2 = ((bf16[8,272,128]{2,1,0:T(8,128)(2,1)}), bf16[8,272,128]{2,1,0:T(8,128)(2,1)}, u32[]{:S(2)}, u32[]{:S(2)}) async-start(bf16[8,272,128]{2,1,0:T(8,128)(2,1)} %backward.1), calls=%async_computation.2 | async-start | bytes 1114112 | tf_op jit(solution)/shard_map/all_to_all | solution.py:686
  68.0 8.5 %collective-permute-start.20 = (bf16[8,128,128]{2,1,0:T(8,128)(2,1)S(1)}, bf16[8,128,128]{2,1,0:T(8,128)(2,1)}, u32[]{:S(2)}, u32[]{:S(2)}) collective-permute-start(bf16[8,128,128]{2,1,0:T(8,128)(2,1)S(1)} %slice.15.refs_0_), channel_id=1, source_target_pairs={{0,2},{1,3},{2,0},{3,1},{4,6},{5,7},{6,4},{7,5},{8,10},{9,11},{10,... | collective-permute-start | bytes 786440 | tf_op jit(solution)/shard_map/ppermute | solution.py:203
  69.5 7.0 %collective-permute-start.21 = (bf16[8,128,128]{2,1,0:T(8,128)(2,1)S(1)}, bf16[8,128,128]{2,1,0:T(8,128)(2,1)}, u32[]{:S(2)}, u32[]{:S(2)}) collective-permute-start(bf16[8,128,128]{2,1,0:T(8,128)(2,1)S(1)} %slice.15.refs_0_), channel_id=1, source_target_pairs={{0,1},{1,0},{2,3},{3,2},{4,5},{5,4},{6,7},{7,6},{8,9},{9,8},{10,11... | collective-permute-start | bytes 786440 | tf_op jit(solution)/shard_map/ppermute | solution.py:203
  69.5 1.8 %collective-permute-start.18 = (bf16[4,128,128]{2,1,0:T(8,128)(2,1)S(1)}, bf16[4,128,128]{2,1,0:T(8,128)(2,1)}, u32[]{:S(2)}, u32[]{:S(2)}) collective-permute-start(bf16[4,128,128]{2,1,0:T(8,128)(2,1)S(1)} %collective-permute-done.10.refs_7_.refs_11_), channel_id=1, source_target_pairs={{0,1},{1,0},{2,3},{3,2},{4,5},{5,4},{6,7},{7,6},{8,9},{9,8},{10,11... | collective-permute-start | bytes 393224 | tf_op jit(solution)/shard_map/ppermute | solution.py:203
  76.5 1.9 %collective-permute-start.22 = (bf16[8,128,128]{2,1,0:T(8,128)(2,1)}, bf16[8,128,128]{2,1,0:T(8,128)(2,1)}, u32[]{:S(2)}, u32[]{:S(2)}) collective-permute-start(bf16[8,128,128]{2,1,0:T(8,128)(2,1)} %collective-permute-done.20.refs_2_), channel_id=1, source_target_pairs={{0,1},{1,0},{2,3},{3,2},{4,5},{5,4},{6,7},{7,6},{8,9},{9,8},{10,11... | collective-permute-start | bytes 786440 | tf_op jit(solution)/shard_map/ppermute | solution.py:203
  76.7 10.0 %collective-permute-start.19 = (bf16[128,1024]{1,0:T(8,128)(2,1)}, bf16[128,1024]{1,0:T(8,128)(2,1)S(1)}, u32[]{:S(2)}, u32[]{:S(2)}) collective-permute-start(bf16[128,1024]{1,0:T(8,128)(2,1)} %get-tuple-element.80), channel_id=1, source_target_pairs={{0,2},{1,3},{2,0},{3,1},{4,6},{5,7},{6,4},{7,5},{8,10},{9,11},{10,... | collective-permute-start | bytes 786440 | tf_op jit(solution)/shard_map/ppermute | solution.py:203
